TPU v7x, 512 devices: a whole 4x8x8 slice. The times are simulated.
512 devices in a mesh: seq: 128 (over y, z, core), mp: 4 (over x).
Axes of the slice: x: 4, y: 8, z: 8, core: 2. Of those that a mesh axis runs over, the one named last changes fastest.
Arguments:
- owned_rows: bfloat16 [16384, 2304], P('seq'), may hold values from -6 to 6
- arrival: int32 [128, 128], P('seq'), may hold values from 0 to 127, each once within a row
- image_lengths: int32 [256], replicated, may hold values from 1 to 384, 16384 in all
- probe_seeds: int32 [256], replicated, may hold values from 0 to 999999
- in_gain: float32 [2304], replicated, may hold values from 0.1 to 1.9
- w_q: bfloat16 [2304, 2304], P('seq', 'mp')
- w_kv: bfloat16 [2304, 2, 768], P('seq', None, 'mp')
- w_out: bfloat16 [2304, 2304], P('mp', 'seq'), may hold values from -0.125 to 0.125
Outputs:
- velocity: bfloat16 [16384, 2304], P('seq', 'mp')
- divergence: float32 [256], replicated
Inputs may be any that keep to these rules, and one draw needn't show every extreme that they name: Each row of arrival holds every number of 0 to 127 once. `image_lengths`: the lengths sum to 16384; the longest is exactly 384.
All inputs are finite; a program needn't handle non-finite values.
Results may differ from a plain program's by a relative error of at most 0.015.
Values may be sent and summed in bfloat16 or wider, within the bound.
No kernel may reach another device: no remote copies, remote signals or barrier semaphores. Data moves between devices by JAX's collectives and lax.ppermute only.
A program may use at most 64 MiB of HBM per device.

v0:
```python
import jax
import jax.numpy as jnp
from jax import lax
from jax.sharding import PartitionSpec as P

HEADS = 24
KV_HEADS = 8
HEAD_DIM = 96
SPAN = 3


def passed_along(array, axis, by):
    length = lax.axis_size(axis)
    pairs = [(i, i + by) for i in range(length) if 0 <= i + by < length]
    return lax.ppermute(array, axis, pairs)


def segment_of(pos, ends):
    return jnp.sum((ends[None, :] <= pos[:, None]).astype(jnp.int32), axis=1, dtype=jnp.int32)


def probe_signs(seed_row, local_row, width):
    columns = jnp.arange(width, dtype=jnp.int32)
    mixed = seed_row[:, None] * 40503 + local_row[:, None] * 69069 + columns[None, :] * 2654435
    mixed = mixed ^ jnp.right_shift(mixed, 15)
    mixed = mixed * 1597334677
    mixed = mixed ^ jnp.right_shift(mixed, 13)
    mixed = mixed * 668265263
    bit = jnp.right_shift(mixed, 11) & 1
    return (1 - 2 * bit).astype(jnp.float32)


def normalize(packed, signs, in_gain):
    xf = packed.astype(jnp.float32)
    inv = lax.rsqrt(jnp.mean(xf * xf, axis=1, keepdims=True) + 1e-06)
    along = jnp.mean(xf * signs, axis=1, keepdims=True)
    h = (xf * inv * in_gain).astype(jnp.bfloat16)
    h_t = ((signs * inv - xf * inv * inv * inv * along) * in_gain).astype(jnp.bfloat16)
    return (h, h_t)


def attend(qh, kh, vh, qth, kth, vth, mask, head_dim):
    scale = 1.0 / head_dim**0.5
    scores = jnp.dot(qh, kh.T, preferred_element_type=jnp.float32) * scale
    scores = jnp.where(mask, scores, -1e30)
    top = jnp.max(scores, axis=1, keepdims=True)
    expo = jnp.exp(scores - top)
    probs = expo / jnp.sum(expo, axis=1, keepdims=True)
    tangent = (
        jnp.dot(qth, kh.T, preferred_element_type=jnp.float32)
        + jnp.dot(qh, kth.T, preferred_element_type=jnp.float32)
    ) * scale
    tangent = jnp.where(mask, tangent, 0.0)
    probs_t = probs * (tangent - jnp.sum(probs * tangent, axis=1, keepdims=True))
    pb = probs.astype(jnp.bfloat16)
    ptb = probs_t.astype(jnp.bfloat16)
    out = jnp.dot(pb, vh, preferred_element_type=jnp.float32).astype(jnp.bfloat16)
    out_t = (
        jnp.dot(ptb, vh, preferred_element_type=jnp.float32)
        + jnp.dot(pb, vth, preferred_element_type=jnp.float32)
    ).astype(jnp.bfloat16)
    return (out, out_t)


def body(owned_rows, arrival, image_lengths, probe_seeds, in_gain, w_q, w_kv, w_out):
    rows = owned_rows.shape[0]
    width = owned_rows.shape[1]
    n_seq = lax.axis_size("seq")
    n_mp = lax.axis_size("mp")
    shard = lax.axis_index("seq")
    member = lax.axis_index("mp")
    quarter = width // n_mp
    arrived = lax.all_to_all(owned_rows, "seq", split_axis=0, concat_axis=0, tiled=True)
    packed = jnp.take(arrived, arrival[0], axis=0)
    images = image_lengths.shape[0]
    ends = jnp.cumsum(image_lengths, dtype=jnp.int32)
    starts = ends - image_lengths
    positions = shard * rows + jnp.arange(rows, dtype=jnp.int32)
    seg = segment_of(positions, ends)
    onehot = seg[:, None] == jnp.arange(images, dtype=jnp.int32)[None, :]
    start_row = jnp.sum(jnp.where(onehot, starts[None, :], 0), axis=1, dtype=jnp.int32)
    seed_row = jnp.sum(jnp.where(onehot, probe_seeds[None, :], 0), axis=1, dtype=jnp.int32)
    signs = probe_signs(seed_row, positions - start_row, width)
    h, h_t = normalize(packed, signs, in_gain)
    both = jnp.concatenate([h, h_t], axis=0)
    q_width = w_q.shape[1]
    new_q = jnp.dot(
        both, lax.all_gather(w_q, "seq", axis=0, tiled=True), preferred_element_type=jnp.float32
    )
    new_kv = jnp.einsum(
        "rc,cgw->rgw",
        both,
        lax.all_gather(w_kv, "seq", axis=0, tiled=True),
        preferred_element_type=jnp.float32,
    )
    proj_q = new_q
    proj_kv = new_kv
    proj_q = proj_q.astype(jnp.bfloat16)
    proj_kv = proj_kv.astype(jnp.bfloat16)
    query, query_t = (proj_q[:rows], proj_q[rows:])
    own = jnp.stack([proj_kv[:rows, 0], proj_kv[:rows, 1], proj_kv[rows:, 0], proj_kv[rows:, 1]])
    blocks = []
    for offset in range(-SPAN, SPAN + 1):
        if offset == 0:
            blocks.append(own)
        else:
            blocks.append(passed_along(own, "seq", -offset))
    window = jnp.concatenate(blocks, axis=1)
    reach = (2 * SPAN + 1) * rows
    kpos = shard * rows - SPAN * rows + jnp.arange(reach, dtype=jnp.int32)
    valid = (kpos >= 0) & (kpos < rows * n_seq)
    mask = (seg[:, None] == segment_of(kpos, ends)[None, :]) & valid[None, :]
    group_size = HEADS // KV_HEADS
    outs, outs_t = ([], [])
    for head in range(q_width // HEAD_DIM):
        lo = head * HEAD_DIM
        hi = lo + HEAD_DIM
        klo = head // group_size * HEAD_DIM
        khi = klo + HEAD_DIM
        out, out_t = attend(
            query[:, lo:hi],
            window[0, :, klo:khi],
            window[1, :, klo:khi],
            query_t[:, lo:hi],
            window[2, :, klo:khi],
            window[3, :, klo:khi],
            mask,
            HEAD_DIM,
        )
        outs.append(out)
        outs_t.append(out_t)
    attended = jnp.concatenate(outs + outs_t, axis=1).reshape(rows, 2, q_width)
    attended = jnp.concatenate([attended[:, 0], attended[:, 1]], axis=0)
    terms = jnp.dot(
        attended,
        lax.all_gather(w_out, "seq", axis=1, tiled=True),
        preferred_element_type=jnp.float32,
    )
    sums = lax.psum_scatter(
        terms.astype(jnp.bfloat16), "mp", scatter_dimension=1, tiled=True
    ).astype(jnp.float32)
    velocity = sums[:rows].astype(jnp.bfloat16)
    total_t = sums[rows:]
    mine_signs = lax.dynamic_slice_in_dim(signs, member * quarter, quarter, 1)
    row_terms = jnp.sum(total_t * mine_signs, axis=1)
    shares = jnp.sum(jnp.where(onehot, row_terms[:, None], 0.0), axis=0) / width
    divergence = lax.psum(shares, ("seq", "mp"))
    return (velocity, divergence)


def solution(mesh):
    in_specs = (
        P("seq", None),
        P("seq", None),
        P(),
        P(),
        P(),
        P("seq", "mp"),
        P("seq", None, "mp"),
        P("mp", "seq"),
    )
    out_specs = (P("seq", "mp"), P())
    return jax.shard_map(body, mesh=mesh, in_specs=in_specs, out_specs=out_specs, check_vma=False)
```

profile of v0, /device:TPU:1, one launch (start us, length us, event | category | flops | bytes accessed | tf_op | source)
XLA Modules:
  0.0 418.4 jit_solution(903929687972432540)
XLA Ops:
  9.2 2.1 reduce.2
  11.3 1.0 reshape.157
  12.3 18.4 %all-to-all-start = ((bf16[128,2,1152]{2,1,0:T(2,128)(2,1)}), bf16[128,2,1152]{2,1,0:T(2,128)(2,1)S(1)}, u32[]{:S(2)}, u32[]{:S(2)}) async-start(bf16[128,2,1152]{2,1,0:T(2,128)(2,1)} %reshape.157), calls=%async_computation | async-start | bytes 1179648 | tf_op jit(solution)/shard_map/all_to_all | solution.py:73
  32.6 19.4 %all-to-all-done = bf16[128,2,1152]{2,1,0:T(2,128)(2,1)S(1)} async-done(((bf16[128,2,1152]{2,1,0:T(2,128)(2,1)}), bf16[128,2,1152]{2,1,0:T(2,128)(2,1)S(1)}, u32[]{:S(2)}, u32[]{:S(2)}) %all-to-all-start) | async-done | bytes 589856 | tf_op jit(solution)/shard_map/all_to_all | solution.py:73
  52.6 1.0 gather_fusion
  53.6 0.8 fusion.29
  54.4 1.1 fusion.23
  55.5 50.0 %all-gather.6.cloned.1.call-done = bf16[2304,2,192]{2,1,0:T(2,128)(2,1)} async-done(((bf16[18,2,192]{2,1,0:T(2,128)(2,1)}), bf16[2304,2,192]{2,1,0:T(2,128)(2,1)}) %all-gather.6.cloned.1.call-update) | async-done | bytes 1769488 | tf_op jit(solution)/shard_map/all_gather | solution.py:93
  105.5 2.6 fusion.39
  108.2 3.5 collective-permute-start
  111.7 0.9 convert_reduce_fusion
  112.6 3.1 collective-permute-start.1
  116.3 2.6 collective-permute-start.2
  119.0 1.9 collective-permute-start.3
  120.9 1.3 collective-permute-start.4
  122.2 1.5 collective-permute-start.5
  123.7 0.8 constant_dynamic-update-slice_fusion.6
  127.8 2.2 collective-permute-done.4
  130.7 7.8 %collective-permute-done.5 = bf16[4,128,192]{1,2,0:T(8,128)(2,1)S(1)} collective-permute-done((bf16[4,128,192]{1,2,0:T(8,128)(2,1)S(1)}, bf16[4,128,192]{1,2,0:T(8,128)(2,1)S(1)}, u32[]{:S(2)}, u32[]{:S(2)}) %collective-permute-start.5) | collective-permute-done | bytes 196640 | tf_op jit(solution)/shard_map/ppermute | solution.py:15
  139.2 55.8 %all-gather.8.cloned.1.call-done = bf16[128,18,576]{2,1,0:T(8,128)(2,1)} async-done(((bf16[1,18,576]{2,1,0:T(8,128)(2,1)}), bf16[128,18,576]{2,1,0:T(8,128)(2,1)}) %all-gather.8.cloned.1.call-update) | async-done | bytes 2654224 | tf_op jit(solution)/shard_map/all_gather | solution.py:88
  195.0 5.1 %reshape.150 = bf16[2304,576]{1,0:T(8,128)(2,1)S(1)} reshape(bf16[128,18,576]{2,1,0:T(8,128)(2,1)} %all-gather.8.cloned.1.call-done) | data formatting | bytes 5308416
  200.2 2.3 convolution_convert_fusion.1
  202.5 1.2 fusion.89
  203.6 1.2 fusion.90
  204.8 1.3 fusion.154
  206.1 1.3 fusion.153
  207.4 1.2 fusion.91
  208.5 1.3 fusion.152
  209.8 1.2 fusion.83
  211.0 1.3 fusion.151
  212.2 1.2 fusion.84
  213.4 1.3 fusion.150
  214.7 1.3 fusion.149
  216.2 1.3 fusion.61
  218.6 1.3 fusion.60
  219.9 1.3 fusion.59
  221.2 1.3 fusion.58
  222.4 1.3 fusion.57
  223.7 1.2 fusion.85
  224.9 1.3 fusion.56
  226.1 1.2 fusion.92
  227.4 1.2 fusion.93
  228.6 1.2 fusion.94
  229.9 1.2 fusion.86
  231.1 1.3 fusion.87
  232.4 1.2 fusion.88
  233.7 1.3 multiply_reduce_fusion.5
  235.0 1.3 fusion.45
  236.3 1.3 multiply_reduce_fusion.4
  237.6 1.3 fusion.47
  238.9 1.3 multiply_reduce_fusion.3
  240.2 1.3 fusion.49
  241.5 1.3 multiply_reduce_fusion.2
  242.8 1.3 fusion.51
  244.1 1.3 multiply_reduce_fusion.1
  245.4 1.3 fusion.53
  246.7 1.3 multiply_reduce_fusion
  248.0 1.4 fusion.55
  249.4 30.1 %all-gather.10.cloned.1.call-done = bf16[128,18,576]{2,1,0:T(8,128)(2,1)} async-done(((bf16[1,18,576]{2,1,0:T(8,128)(2,1)}), bf16[128,18,576]{2,1,0:T(8,128)(2,1)}) %all-gather.10.cloned.1.call-update) | async-done | bytes 2654224 | tf_op jit(solution)/shard_map/all_gather | solution.py:136
  279.6 5.1 %reshape.152 = bf16[2304,576]{1,0:T(8,128)(2,1)S(1)} reshape(bf16[128,18,576]{2,1,0:T(8,128)(2,1)} %all-gather.10.cloned.1.call-done) | data formatting | bytes 5308416
  284.7 2.1 fusion
  287.4 24.2 %reduce-scatter.4.cloned.1.call-done = bf16[576,256]{1,0:T(8,128)(2,1)} async-done(((bf16[2304,256]{1,0:T(8,128)(2,1)}), bf16[576,256]{1,0:T(8,128)(2,1)}) %reduce-scatter.4.cloned.1.call-update) | async-done | bytes 294928
  311.6 1.7 fusion.148
  313.8 98.1 %psum.7 = f32[256]{0:T(256)} all-reduce(f32[256]{0:T(256)S(1)} %broadcast_multiply_fusion), channel_id=1, replica_groups=mesh['seq'=128,'mp'=4] {'seq','mp'}, use_global_device_ids=true, to_apply=%region_29.30 | all-reduce | flops 256 | bytes 2048 | tf_op jit(solution)/shard_map/psum | solution.py:147
  (71 shorter events, 12.2 us)
Async XLA Ops:
  7.2 98.3 %all-gather.6.cloned.1.call-start = ((), (), s32[]{:S(2)}) async-start(), calls=%async_computation.2 | async-start | bytes 2377728 | tf_op jit(solution)/shard_map/all_gather | solution.py:93
  7.9 187.1 %all-gather.8.cloned.1.call-start = ((), (), s32[]{:S(2)}) async-start(), calls=%async_computation.3 | async-start | bytes 3962880 | tf_op jit(solution)/shard_map/all_gather | solution.py:88
  11.3 20.2 %copy-start.6 = (s32[256]{0:T(256)S(1)}, s32[256]{0:T(256)}, u32[]{:S(2)}) copy-start(s32[256]{0:T(256)} %param.10) | copy-start | bytes 3076
  11.3 20.8 %copy-start.8 = (s32[1,128]{1,0:T(1,128)S(1)}, s32[1,128]{1,0:T(1,128)}, u32[]{:S(2)}) copy-start(s32[1,128]{1,0:T(1,128)} %param.9) | copy-start | bytes 1540
  11.3 21.1 %copy-start.7 = (s32[256]{0:T(256)S(1)}, s32[256]{0:T(256)}, u32[]{:S(2)}) copy-start(s32[256]{0:T(256)} %param.11) | copy-start | bytes 3076
  12.3 39.7 %all-to-all-start = ((bf16[128,2,1152]{2,1,0:T(2,128)(2,1)}), bf16[128,2,1152]{2,1,0:T(2,128)(2,1)S(1)}, u32[]{:S(2)}, u32[]{:S(2)}) async-start(bf16[128,2,1152]{2,1,0:T(2,128)(2,1)} %reshape.157), calls=%async_computation | async-start | bytes 1179648 | tf_op jit(solution)/shard_map/all_to_all | solution.py:73
  30.7 248.9 %all-gather.10.cloned.1.call-start = ((), (), s32[]{:S(2)}) async-start(), calls=%async_computation.4 | async-start | bytes 3962880 | tf_op jit(solution)/shard_map/all_gather | solution.py:136
  31.4 280.1 %reduce-scatter.4.cloned.1.call-start = ((), (), s32[]{:S(2)}) async-start(), calls=%async_computation.5 | async-start | bytes 1474560
  32.4 20.2 %copy-start.2 = (s32[128]{0:T(128)}, s32[128]{0:T(128)S(1)}, u32[]{:S(2)}) copy-start(s32[128]{0:T(128)S(1)} %convert_reduce_fusion.1) | copy-start | bytes 1540
  52.6 1.8 copy-start.1
  55.5 52.6 %copy-start = (bf16[128,2304]{1,0:T(8,128)(2,1)}, bf16[128,2304]{1,0:T(8,128)(2,1)S(1)}, u32[]{:S(2)}) copy-start(bf16[128,2304]{1,0:T(8,128)(2,1)S(1)} %get-tuple-element.19) | copy-start | bytes 1769476
  108.2 14.0 %collective-permute-start = (bf16[4,128,192]{1,2,0:T(8,128)(2,1)S(1)}, bf16[4,128,192]{1,2,0:T(8,128)(2,1)S(1)}, u32[]{:S(2)}, u32[]{:S(2)}) collective-permute-start(bf16[4,128,192]{1,2,0:T(8,128)(2,1)S(1)} %pad_maximum_fusion.3), channel_id=1, source_target_pairs={{0,12},{4,16},{8,20},{12,24},{16,28},{20,32},{24,36},{28,40},{32,4... | collective-permute-start | bytes 589832 | tf_op jit(solution)/shard_map/ppermute | solution.py:15
  112.6 11.8 %collective-permute-start.1 = (bf16[4,128,192]{1,2,0:T(8,128)(2,1)S(1)}, bf16[4,128,192]{1,2,0:T(8,128)(2,1)S(1)}, u32[]{:S(2)}, u32[]{:S(2)}) collective-permute-start(bf16[4,128,192]{1,2,0:T(8,128)(2,1)S(1)} %pad_maximum_fusion.3), channel_id=1, source_target_pairs={{0,8},{4,12},{8,16},{12,20},{16,24},{20,28},{24,32},{28,36},{32,40... | collective-permute-start | bytes 589832 | tf_op jit(solution)/shard_map/ppermute | solution.py:15
  116.3 8.9 %collective-permute-start.2 = (bf16[4,128,192]{1,2,0:T(8,128)(2,1)S(1)}, bf16[4,128,192]{1,2,0:T(8,128)(2,1)S(1)}, u32[]{:S(2)}, u32[]{:S(2)}) collective-permute-start(bf16[4,128,192]{1,2,0:T(8,128)(2,1)S(1)} %pad_maximum_fusion.3), channel_id=1, source_target_pairs={{0,4},{4,8},{8,12},{12,16},{16,20},{20,24},{24,28},{28,32},{32,36}... | collective-permute-start | bytes 589832 | tf_op jit(solution)/shard_map/ppermute | solution.py:15
  119.0 8.1 %collective-permute-start.3 = (bf16[4,128,192]{1,2,0:T(8,128)(2,1)S(1)}, bf16[4,128,192]{1,2,0:T(8,128)(2,1)S(1)}, u32[]{:S(2)}, u32[]{:S(2)}) collective-permute-start(bf16[4,128,192]{1,2,0:T(8,128)(2,1)S(1)} %pad_maximum_fusion.3), channel_id=1, source_target_pairs={{4,0},{8,4},{12,8},{16,12},{20,16},{24,20},{28,24},{32,28},{36,32}... | collective-permute-start | bytes 589832 | tf_op jit(solution)/shard_map/ppermute | solution.py:15
  120.9 9.1 %collective-permute-start.4 = (bf16[4,128,192]{1,2,0:T(8,128)(2,1)S(1)}, bf16[4,128,192]{1,2,0:T(8,128)(2,1)S(1)}, u32[]{:S(2)}, u32[]{:S(2)}) collective-permute-start(bf16[4,128,192]{1,2,0:T(8,128)(2,1)S(1)} %pad_maximum_fusion.3), channel_id=1, source_target_pairs={{8,0},{12,4},{16,8},{20,12},{24,16},{28,20},{32,24},{36,28},{40,32... | collective-permute-start | bytes 589832 | tf_op jit(solution)/shard_map/ppermute | solution.py:15
  122.2 16.3 %collective-permute-start.5 = (bf16[4,128,192]{1,2,0:T(8,128)(2,1)S(1)}, bf16[4,128,192]{1,2,0:T(8,128)(2,1)S(1)}, u32[]{:S(2)}, u32[]{:S(2)}) collective-permute-start(bf16[4,128,192]{1,2,0:T(8,128)(2,1)S(1)} %pad_maximum_fusion.3), channel_id=1, source_target_pairs={{12,0},{16,4},{20,8},{24,12},{28,16},{32,20},{36,24},{40,28},{44,3... | collective-permute-start | bytes 589832 | tf_op jit(solution)/shard_map/ppermute | solution.py:15
  200.1 4.7 %copy-start.3 = (s32[128]{0:T(128)S(1)}, s32[128]{0:T(128)}, u32[]{:S(2)}) copy-start(s32[128]{0:T(128)} %copy-done.2) | copy-start | bytes 1540
  200.1 4.7 %copy-start.5 = (s32[896]{0:T(1024)S(1)}, s32[896]{0:T(1024)}, u32[]{:S(2)}) copy-start(s32[896]{0:T(1024)} %convert_reduce_fusion) | copy-start | bytes 10756
  200.2 4.7 %copy-start.9 = (pred[896]{0:T(1024)(128)(4,1)S(1)}, pred[896]{0:T(1024)(128)(4,1)}, u32[]{:S(2)}) copy-start(pred[896]{0:T(1024)(128)(4,1)} %compare_and_fusion.1) | copy-start | bytes 2692
  286.8 26.8 %copy-start.4 = (s32[128]{0:T(128)S(1)}, s32[128]{0:T(128)}, u32[]{:S(2)}) copy-start(s32[128]{0:T(128)} %copy-done.2) | copy-start | bytes 1540
Sparse Core Ops, SparseCore 0:
  11.2 94.2 all-gather.5
  108.6 86.3 all-gather.7
  198.2 81.3 all-gather.9
  287.0 24.5 reduce-scatter.3
where the time goes:
time: 420 us; the launch traced here: 418 us
  waiting for transfers between devices  192 us (46%)
  blocking collectives  98.1 us (23%)
  matrix products  52.4 us (12%)
  starting transfers between devices  32.5 us (8%)
  local copies, waits for them, and re-layouts  19.8 us (5%)
  between operations  14.3 us (3%)
  other arithmetic  9.34 us (2%)
    psum x1, blocking collectives, body(): divergence = lax.psum(shares, ('seq', 'mp'))  98.1 us
    all_gather x1, waiting for transfers between devices, body(): lax.all_gather(w_q, 'seq', axis=0, tiled=True)  55.8 us
    all_gather x1, waiting for transfers between devices, body(): lax.all_gather(w_kv, 'seq', axis=0, tiled=True)  50 us
    all_gather x1, waiting for transfers between devices, body(): lax.all_gather(w_out, 'seq', axis=1, tiled=True)  30.1 us
    unnamed x5, waiting for transfers between devices  26.3 us
    all_to_all x1, waiting for transfers between devices, body(): lax.all_to_all(owned_rows, 'seq', split_axis=0, concat_axis=0, tiled=True)  19.4 us
    all_to_all x1, starting transfers between devices, body(): lax.all_to_all(owned_rows, 'seq', split_axis=0, concat_axis=0, tiled=True)  18.4 us
    unnamed x31, local copies, waits for them, and re-layouts  15.7 us
  transfers between devices with their start and end apart: 11, of which 8 were waited for; matrix products, arithmetic and copies ran while one was open for 17% of the time, Pallas kernels for 0%

commit v1 on v0

v1 whole, which is shorter than its diff:
```python
import functools

import jax
import jax.numpy as jnp
from jax import lax
from jax.experimental import pallas as pl
from jax.experimental.pallas import tpu as pltpu
from jax.sharding import Mesh
from jax.sharding import PartitionSpec as P

HEADS = 24
KV_HEADS = 8
HEAD_DIM = 96
GROUP = HEADS // KV_HEADS
SPAN = 3
SEQ = ("y", "z", "c")
COLUMN = ("y", "z")
TILE = ("c", "x")


def segment_of(pos, ends):
    return jnp.sum((ends[None, :] <= pos[:, None]).astype(jnp.int32), axis=1, dtype=jnp.int32)


def probe_signs(seed_row, local_row, width):
    columns = jnp.arange(width, dtype=jnp.int32)
    mixed = seed_row[:, None] * 40503 + local_row[:, None] * 69069 + columns[None, :] * 2654435
    mixed = mixed ^ jnp.right_shift(mixed, 15)
    mixed = mixed * 1597334677
    mixed = mixed ^ jnp.right_shift(mixed, 13)
    mixed = mixed * 668265263
    bit = jnp.right_shift(mixed, 11) & 1
    return (1 - 2 * bit).astype(jnp.float32)


def normalize(packed, signs, in_gain):
    xf = packed.astype(jnp.float32)
    inv = lax.rsqrt(jnp.mean(xf * xf, axis=1, keepdims=True) + 1e-06)
    along = jnp.mean(xf * signs, axis=1, keepdims=True)
    h = (xf * inv * in_gain).astype(jnp.bfloat16)
    h_t = ((signs * inv - xf * inv * inv * inv * along) * in_gain).astype(jnp.bfloat16)
    return (h, h_t)


def spread(array, axes):
    count = lax.axis_size(axes)
    copies = jnp.broadcast_to(array[None], (count,) + array.shape)
    return lax.all_to_all(copies, axes, split_axis=0, concat_axis=0, tiled=True)


def moved(array, by):
    count = lax.axis_size(COLUMN)
    pairs = [(i, i + by) for i in range(count) if 0 <= i + by < count]
    return lax.ppermute(array, COLUMN, pairs)


NT = (((1,), (1,)), ((), ()))


def attend_kernel(
    rows, q_ref, far_before, before, here, after, far_after, segq_ref, segk_ref, u_ref, w_any,
    part_ref, share_ref, window, weight, o_ext, w_sem,
):
    block = 2 * rows
    reach = (2 * SPAN + 1) * rows
    q_width = GROUP * HEAD_DIM
    o_width = weight.shape[1]
    fetch = pltpu.make_async_copy(w_any.at[:, pl.ds(w_any.shape[1] - o_width, o_width)], weight, w_sem)
    fetch.start()
    window[0:rows] = far_before[...]
    window[rows : rows + block] = before[...]
    window[rows + block : rows + 2 * block] = here[...]
    window[rows + 2 * block : rows + 3 * block] = after[...]
    window[rows + 3 * block : 2 * rows + 3 * block] = far_after[...]
    scale = 1.0 / HEAD_DIM**0.5
    to_exp2 = scale * 1.4426950408889634
    row_terms = []
    o_ext[:, : o_width - q_width] = jnp.zeros((block, o_width - q_width), jnp.bfloat16)
    for tile in range(2):
        lo = tile * rows
        keys = window[lo : lo + reach, 0:HEAD_DIM]
        values = window[lo : lo + reach, HEAD_DIM : 2 * HEAD_DIM]
        keys_t = window[lo : lo + reach, 2 * HEAD_DIM : 3 * HEAD_DIM]
        values_t = window[lo : lo + reach, 3 * HEAD_DIM : 4 * HEAD_DIM]
        mask = segq_ref[lo : lo + rows, :] == segk_ref[:, lo : lo + reach]
        terms = jnp.zeros((rows, 1), jnp.float32)
        for head in range(GROUP):
            a, b = head * HEAD_DIM, (head + 1) * HEAD_DIM
            q = q_ref[lo : lo + rows, a:b]
            q_t = q_ref[block + lo : block + lo + rows, a:b]
            s = lax.dot_general(q, keys, NT, preferred_element_type=jnp.float32)
            s_t = lax.dot_general(q_t, keys, NT, preferred_element_type=jnp.float32)
            s_t += lax.dot_general(q, keys_t, NT, preferred_element_type=jnp.float32)
            s = jnp.where(mask, s, -1e30)
            e = jnp.exp2((s - jnp.max(s, axis=1, keepdims=True)) * to_exp2)
            inv = 1.0 / jnp.sum(e, axis=1, keepdims=True)
            mean = jnp.sum(e * s_t, axis=1, keepdims=True) * inv
            e_t = (e * ((s_t - mean) * scale)).astype(jnp.bfloat16)
            e = e.astype(jnp.bfloat16)
            out = jnp.dot(e, values, preferred_element_type=jnp.float32) * inv
            out_t = jnp.dot(e_t, values, preferred_element_type=jnp.float32)
            out_t += jnp.dot(e, values_t, preferred_element_type=jnp.float32)
            out_t = (out_t * inv).astype(jnp.bfloat16).astype(jnp.float32)
            shift = o_width - q_width
            o_ext[lo : lo + rows, shift + a : shift + b] = out.astype(jnp.bfloat16)
            terms += jnp.sum(out_t * u_ref[lo : lo + rows, a:b], axis=1, keepdims=True)
        row_terms.append(terms)
    images = share_ref.shape[1]
    share = jnp.zeros((1, images), jnp.float32)
    for tile in range(2):
        lo = tile * rows
        numbers = lax.broadcasted_iota(jnp.int32, (rows, images), 1)
        hit = segq_ref[lo : lo + rows, :] == numbers
        share += jnp.sum(jnp.where(hit, row_terms[tile], 0.0), axis=0, keepdims=True)
    share_ref[...] = share
    fetch.wait()
    width = weight.shape[0]
    step = width // 6
    for part in range(6):
        a, b = part * step, (part + 1) * step
        part_ref[:, a:b] = lax.dot_general(
            o_ext[...], weight[a:b, :], NT, preferred_element_type=jnp.float32
        ).astype(jnp.bfloat16)


def attend(q, neighbours, segq, segk, u, weights, images):
    block = q.shape[0] // 2
    rows = block // 2
    width, columns = weights.shape
    o_width = 3 * 128
    vmem = pl.BlockSpec(memory_space=pltpu.VMEM)
    return pl.pallas_call(
        functools.partial(attend_kernel, rows),
        out_shape=(
            jax.ShapeDtypeStruct((block, width), jnp.bfloat16),
            jax.ShapeDtypeStruct((1, images), jnp.float32),
        ),
        in_specs=[vmem] * 9 + [pl.BlockSpec(memory_space=pl.ANY)],
        out_specs=(vmem, vmem),
        scratch_shapes=[
            pltpu.VMEM((8 * rows, 4 * HEAD_DIM), jnp.bfloat16),
            pltpu.VMEM((width, o_width), jnp.bfloat16),
            pltpu.VMEM((block, o_width), jnp.bfloat16),
            pltpu.SemaphoreType.DMA,
        ],
        compiler_params=pltpu.CompilerParams(vmem_limit_bytes=40 * 1024 * 1024),
        cost_estimate=pl.CostEstimate(flops=2_000_000_000, bytes_accessed=5_000_000, transcendentals=700_000),
    )(q, *neighbours, segq, segk, u, weights)


def body(owned_rows, arrival, image_lengths, probe_seeds, in_gain, w_q, w_kv, w_out):
    rows, width = owned_rows.shape
    n_x = lax.axis_size("x")
    core, member = lax.axis_index("c"), lax.axis_index("x")
    n_block = lax.axis_size(COLUMN)
    block_index = lax.axis_index(COLUMN)
    quarter = width // n_x
    depth = w_q.shape[0]
    block = 2 * rows
    images = image_lengths.shape[0]

    halves = jnp.concatenate(
        [
            w_q.reshape(depth, 2, -1),
            w_kv[:, 0].reshape(depth, 2, -1),
            w_kv[:, 1].reshape(depth, 2, -1),
            w_out.T.reshape(depth, 2, -1),
        ],
        axis=2,
    )
    halves = jnp.transpose(halves, (1, 0, 2))
    columns = halves.shape[2]
    n_z = lax.axis_size("z")
    pieces = jnp.broadcast_to(halves[None], (n_z,) + halves.shape).reshape(2 * n_z, depth, columns)
    strip = lax.all_to_all(pieces, ("z", "c"), split_axis=0, concat_axis=0, tiled=True)
    strip = strip.reshape(2 * n_z * depth, columns)
    weights = lax.all_gather(strip, "y", axis=0, tiled=True)

    part = lax.dynamic_slice_in_dim(owned_rows, member * quarter, quarter, 1)
    part, strip = lax.optimization_barrier((part, strip))
    arrived = lax.all_to_all(part, SEQ, split_axis=0, concat_axis=0, tiled=True)
    arrived = jnp.take(arrived, arrival[0], axis=0)
    own = lax.all_gather(arrived, "x", axis=1, tiled=True)
    other = lax.ppermute(own, "c", [(0, 1), (1, 0)])
    packed = jnp.concatenate([jnp.where(core == 0, own, other), jnp.where(core == 0, other, own)], axis=0)

    ends = jnp.cumsum(image_lengths, dtype=jnp.int32)
    starts = ends - image_lengths
    first = block_index * block
    positions = first + jnp.arange(block, dtype=jnp.int32)
    seg = segment_of(positions, ends)
    onehot = seg[:, None] == jnp.arange(images, dtype=jnp.int32)[None, :]
    start_row = jnp.sum(jnp.where(onehot, starts[None, :], 0), axis=1, dtype=jnp.int32)
    seed_row = jnp.sum(jnp.where(onehot, probe_seeds[None, :], 0), axis=1, dtype=jnp.int32)
    signs = probe_signs(seed_row, positions - start_row, width)
    kpos = first - SPAN * rows + jnp.arange(block + 2 * SPAN * rows, dtype=jnp.int32)
    valid = (kpos >= 0) & (kpos < block * n_block)
    segk = jnp.where(valid, segment_of(kpos, ends), -1)

    h, h_t = normalize(packed, signs, in_gain)
    stacked = jnp.concatenate([h, h_t, signs.astype(jnp.bfloat16)], axis=0)
    products = jnp.dot(stacked, weights, preferred_element_type=jnp.float32)
    q_width = GROUP * HEAD_DIM
    kv_end = q_width + 2 * HEAD_DIM
    q = products[: 2 * block, :q_width].astype(jnp.bfloat16)
    kv = jnp.concatenate(
        [products[:block, q_width:kv_end], products[block : 2 * block, q_width:kv_end]], axis=1
    ).astype(jnp.bfloat16)
    u = products[2 * block :, kv_end:]

    neighbours = (moved(kv[rows:], 2), moved(kv, 1), kv, moved(kv, -1), moved(kv[:rows], -2))
    partial, share = attend(q, neighbours, seg[:, None], segk[None, :], u, weights, images)

    halves_out = partial.reshape(2, rows, width)
    mine = lax.dynamic_index_in_dim(halves_out, core, 0, keepdims=False)
    theirs = lax.dynamic_index_in_dim(halves_out, 1 - core, 0, keepdims=False)
    theirs = lax.ppermute(theirs, "c", [(0, 1), (1, 0)])
    group = (mine.astype(jnp.float32) + theirs.astype(jnp.float32)).astype(jnp.bfloat16)
    group = jnp.transpose(group.reshape(rows, n_x, quarter), (1, 0, 2))
    groups = lax.all_to_all(group, "x", split_axis=0, concat_axis=0, tiled=True)
    velocity = jnp.sum(groups.astype(jnp.float32), axis=0).astype(jnp.bfloat16)

    share = jnp.sum(spread(share[0], TILE), axis=0)
    share = jnp.sum(spread(share, COLUMN), axis=0)
    divergence = share / width
    return (velocity, divergence)


def solution(mesh):
    n_seq, n_x = mesh.devices.shape
    n_y = 1
    while n_y * n_y * 2 < n_seq:
        n_y *= 2
    devices = mesh.devices.reshape(n_y, n_seq // 2 // n_y, 2, n_x)
    split = Mesh(devices, ("y", "z", "c", "x"))
    in_specs = (
        P(SEQ, None),
        P(SEQ, None),
        P(),
        P(),
        P(),
        P(SEQ, "x"),
        P(SEQ, None, "x"),
        P("x", SEQ),
    )
    out_specs = (P(SEQ, "x"), P())
    return jax.shard_map(body, mesh=split, in_specs=in_specs, out_specs=out_specs, check_vma=False)
```

time: 420 us -> 185 us (0.44)
  waiting for transfers between devices: 192 us -> 45 us
  blocking collectives: 98.1 us -> 43 us
  matrix products: 52.4 us -> 6.8 us
  starting transfers between devices: 32.5 us -> 43.9 us
  local copies, waits for them, and re-layouts: 19.8 us -> 13.6 us
  Pallas kernels: 0 us -> 5.37 us
    all_gather x3 -> x1, waiting for transfers between devices: 136 us -> 0.02 us  [body(): weights = lax.all_gather(strip, 'y', axis=0, tiled=True)]
    psum x1 -> x0, blocking collectives: 98.1 us -> none  [body(): divergence = lax.psum(shares, ('seq', 'mp'))]
    dot_general x39 -> x1, matrix products: 52.4 us -> 6.8 us  [body(): products = jnp.dot(stacked, weights, preferred_element_type=jnp.float32)]
    all_to_all x0 -> x1, blocking collectives: none -> 30.6 us  [body(): lax.all_to_all(pieces, ('z', 'c'), split_axis=0, concat_axis=0, tiled=True)]
    unnamed x5 -> x1, waiting for transfers between devices: 26.3 us -> 0.02 us
    all_to_all x1 -> x4, waiting for transfers between devices: 19.4 us -> 37.7 us  [the longest x1 15.5 us: body(): arrived = lax.all_to_all(part, SEQ, split_axis=0, concat_axis=0, tiled=True)]
    all_gather x0 -> x1, blocking collectives: none -> 12.5 us  [body(): own = lax.all_gather(arrived, 'x', axis=1, tiled=True)]
    unnamed x31 -> x18, local copies, waits for them, and re-layouts: 15.7 us -> 3.68 us
  transfers between devices with their start and end apart: 11 -> 11, of which waited for: 8 -> 5; matrix products, arithmetic and copies ran while one was open for 17% -> 9% of each run, Pallas kernels for 0% -> 0%
where the time goes in v1:
time: 185 us; the launch traced here: 183 us
  waiting for transfers between devices  45 us (24%)
  starting transfers between devices  43.9 us (24%)
  blocking collectives  43 us (23%)
  between operations  14.4 us (8%)
  local copies, waits for them, and re-layouts  13.6 us (7%)
  other arithmetic  11 us (6%)
  matrix products  6.8 us (4%)
  Pallas kernels  5.37 us (3%)
    all_to_all x1, blocking collectives, body(): lax.all_to_all(pieces, ('z', 'c'), split_axis=0, concat_axis=0, tiled=True)  30.6 us
    all_to_all x1, waiting for transfers between devices, body(): arrived = lax.all_to_all(part, SEQ, split_axis=0, concat_axis=0, tiled=True)  15.5 us
    all_to_all x2, waiting for transfers between devices, spread(): return lax.all_to_all(copies, axes, split_axis=0, concat_axis=0, tiled=True)  14.7 us
    all_to_all x2, starting transfers between devices, spread(): return lax.all_to_all(copies, axes, split_axis=0, concat_axis=0, tiled=True)  14.4 us
    all_gather x1, blocking collectives, body(): own = lax.all_gather(arrived, 'x', axis=1, tiled=True)  12.5 us
    ppermute x4, starting transfers between devices, moved(): return lax.ppermute(array, COLUMN, pairs)  9.55 us
    all_to_all x1, starting transfers between devices, body(): arrived = lax.all_to_all(part, SEQ, split_axis=0, concat_axis=0, tiled=True)  9.26 us
    all_to_all x1, waiting for transfers between devices, body(): groups = lax.all_to_all(group, 'x', split_axis=0, concat_axis=0, tiled=True)  7.39 us
  transfers between devices with their start and end apart: 11, of which 5 were waited for; matrix products, arithmetic and copies ran while one was open for 9% of the time, Pallas kernels for 0%

profile of v1, /device:TPU:1, one launch (start us, length us, event | category | flops | bytes accessed | tf_op | source)
XLA Modules:
  0.0 183.1 jit_solution(786830404548046216)
XLA Ops:
  7.2 0.0 all-gather.2.cloned.1.call-start
  7.3 0.9 slice_reduce_fusion.1
  8.1 0.1 reshape_squeeze.6
  8.2 0.1 reshape_squeeze.7
  8.3 0.9 reshape.164
  9.2 0.9 reshape.165
  10.1 0.1 maximum_bitcast_fusion
  10.3 30.6 %all_to_all.34 = bf16[16,18,768]{2,1,0:T(8,128)(2,1)S(1)} all-to-all(bf16[16,18,768]{2,1,0:T(8,128)(2,1)S(1)} %bitcast.34), channel_id=1, replica_groups=mesh['y'=8,'z'=8,'c'=2,'x'=4] {'z','c'}, dimensions={0} | all-to-all | bytes 884736 | tf_op jit(solution)/shard_map/all_to_all | solution.py:175
  40.8 0.9 reshape.167
  41.8 0.1 constant_dynamic-slice_fusion.2
  41.9 0.1 copy.65
  42.1 0.3 reduce-window.9
  42.4 0.1 slice.36
  42.5 0.1 slice_reduce_fusion.2
  42.6 0.1 fusion.29
  42.7 0.2 convert_reduce_fusion.1
  42.9 0.2 select_reduce_fusion.1
  43.1 0.4 convert_reduce_fusion
  43.5 0.5 broadcast.138
  44.0 0.7 reduce.9
  44.7 0.2 copy.69
  44.9 0.9 reshape.184
  45.8 9.3 %all-to-all-start.1 = ((bf16[128,2,288]{2,1,0:T(2,128)(2,1)}), bf16[128,2,288]{2,1,0:T(2,128)(2,1)S(1)}, u32[]{:S(2)}, u32[]{:S(2)}) async-start(bf16[128,2,288]{2,1,0:T(2,128)(2,1)} %reshape.184), calls=%async_computation.1 | async-start | bytes 393216 | tf_op jit(solution)/shard_map/all_to_all | solution.py:181
  55.1 15.5 %all-to-all-done.1 = bf16[128,2,288]{2,1,0:T(2,128)(2,1)S(1)} async-done(((bf16[128,2,288]{2,1,0:T(2,128)(2,1)}), bf16[128,2,288]{2,1,0:T(2,128)(2,1)S(1)}, u32[]{:S(2)}, u32[]{:S(2)}) %all-to-all-start.1) | async-done | bytes 147488 | tf_op jit(solution)/shard_map/all_to_all | solution.py:181
  70.6 0.3 reshape.185
  71.0 0.9 gather_fusion
  71.8 0.1 broadcast_select_fusion.2
  71.9 0.1 copy.53
  72.1 12.5 %all_gather.6 = bf16[128,2304]{0,1:T(8,128)(2,1)S(1)} all-gather(bf16[128,576]{0,1:T(8,128)(2,1)S(1)} %copy.53), channel_id=1, replica_groups=mesh['y'=8,'z'=8,'c'=2,'x'=4] {'x'}, dimensions={1}, use_global_device_ids=true | all-gather | bytes 737280 | tf_op jit(solution)/shard_map/all_gather | solution.py:183
  84.6 4.1 %collective-permute-start = (bf16[128,2304]{0,1:T(8,128)(2,1)S(1)}, bf16[128,2304]{0,1:T(8,128)(2,1)S(1)}, u32[]{:S(2)}, u32[]{:S(2)}) collective-permute-start(bf16[128,2304]{0,1:T(8,128)(2,1)S(1)} %all_gather.6), channel_id=1, source_target_pairs={{0,4},{4,0},{1,5},{5,1},{2,6},{6,2},{3,7},{7,3},{8,12},{12,8},{9,1... | collective-permute-start | bytes 1769480 | tf_op jit(solution)/shard_map/ppermute | solution.py:184
  88.7 2.1 %fusion.23 = bf16[256,2304]{0,1:T(8,128)(2,1)} fusion(s32[2304]{0:T(1024)S(1)} %iota_multiply_fusion, s32[256]{0:T(256)S(1)} %multiply_add_fusion), kind=kLoop, calls=%fused_computation.29 | loop fusion | flops 7667712 | bytes 1189888 | tf_op jit(solution)/shard_map/convert_element_type | solution.py:201
  90.8 0.1 broadcast_select_fusion.1
  90.9 1.8 fusion.14
  92.7 2.3 %fusion.8 = (bf16[256,2304]{0,1:T(8,128)(2,1)S(1)}, bf16[256,2304]{0,1:T(8,128)(2,1)S(1)}) fusion(f32[2304]{0:T(1024)S(1)} %copy-done.3, f32[256]{0:T(256)S(1)} %get-tuple-element.28, bf16[128,2304]{0,1:T(8,128)(2,1)S(1)} %get-tuple-element.23, bf16[128,2304]{0,1:T(8,128)(2,1)S(1)} %get-tuple-element.22, f32[256]{0:T(256)S(1)} %get-tuple-element.29, ...), kind=kLoop, calls=%fused_computation.14 | loop fusion | flops 15335424 | bytes 3560448 | tf_op jit(solution)/shard_map/convert_element_type | solution.py:40
  95.0 6.8 %fusion.31 = (bf16[768,768]{1,0:T(8,128)(2,1)S(1)}, f32[768,768]{1,0:T(8,128)}) fusion(bf16[2304,768]{1,0:T(8,128)(2,1)} %all-gather.2.cloned.1.call-done.w_any, bf16[256,2304]{0,1:T(8,128)(2,1)} %fusion.23, bf16[256,2304]{0,1:T(8,128)(2,1)S(1)} %get-tuple-element.17, bf16[256,2304]{0,1:T(8,128)(2,1)S(1)} %get-tuple-element.16), kind=kOutput, calls=%fused_computation.73 | convolution fusion | flops 2729115648 | bytes 10616832 | tf_op jit(solution)/shard_map/dot_general | solution.py:202
  101.8 0.1 fusion.30
  102.0 0.1 pad_maximum_fusion.1.here
  102.1 2.1 %collective-permute-start.2 = (bf16[256,384]{1,0:T(8,128)(2,1)S(1)}, bf16[256,384]{1,0:T(8,128)(2,1)S(1)}, u32[]{:S(2)}, u32[]{:S(2)}) collective-permute-start(bf16[256,384]{1,0:T(8,128)(2,1)S(1)} %pad_maximum_fusion.1.here), channel_id=1, source_target_pairs={{0,8},{8,16},{16,24},{24,32},{32,40},{40,48},{48,56},{56,64},{64,7... | collective-permute-start | bytes 589832 | tf_op jit(solution)/shard_map/ppermute | solution.py:54
  104.2 1.3 collective-permute-start.3
  105.5 0.1 fusion.26
  105.6 4.6 %collective-permute-start.1 = (bf16[128,384]{1,0:T(8,128)(2,1)S(1)}, bf16[128,384]{1,0:T(8,128)(2,1)S(1)}, u32[]{:S(2)}, u32[]{:S(2)}) collective-permute-start(bf16[128,384]{1,0:T(8,128)(2,1)S(1)} %get-tuple-element.25), channel_id=1, source_target_pairs={{0,16},{8,24},{16,32},{24,40},{32,48},{40,56},{48,64},{56,72},{64,... | collective-permute-start | bytes 294920 | tf_op jit(solution)/shard_map/ppermute | solution.py:54
  110.3 1.5 collective-permute-start.4
  111.8 0.1 copy.56.segq_ref
  111.9 1.0 slice.46.q_ref
  113.0 1.2 slice.53.u_ref
  114.2 7.2 %collective-permute-done.4.far_after = bf16[128,384]{1,0:T(8,128)(2,1)S(1)} collective-permute-done((bf16[128,384]{1,0:T(8,128)(2,1)S(1)}, bf16[128,384]{1,0:T(8,128)(2,1)S(1)}, u32[]{:S(2)}, u32[]{:S(2)}) %collective-permute-start.4) | collective-permute-done | bytes 98336 | tf_op jit(solution)/shard_map/ppermute | solution.py:54
  121.4 2.0 %copy-done.1 = bf16[2304,768]{1,0:T(8,128)(2,1)S(1)} copy-done((bf16[2304,768]{1,0:T(8,128)(2,1)S(1)}, bf16[2304,768]{1,0:T(8,128)(2,1)}, u32[]{:S(2)}) %copy-start.1) | copy-done | bytes 3538968
  123.4 5.4 %shard_map.95 = (bf16[256,2304]{1,0:T(8,128)(2,1)S(1)}, f32[1,256]{1,0:T(1,128)S(1)}) custom-call(bf16[512,288]{1,0:T(8,128)(2,1)S(1)} %slice.46.q_ref, bf16[128,384]{1,0:T(8,128)(2,1)S(1)} %collective-permute-done.1.far_before, bf16[256,384]{1,0:T(8,128)(2,1)S(1)} %collective-permute-done.2.before, bf16[256,384]{1,0:T(8,128)(2,1)S(1)} %pad_maximum_fusion.1.here, ...), custom_call_target="tpu_custom_call" | custom-call | flops 2000000000 | bytes 5000000 | tf_op jit(solution)/shard_map/pallas_call | solution.py:132
  128.8 0.1 constant_dynamic-slice_fusion.1
  128.9 0.3 copy.58
  129.2 3.1 %collective-permute-start.5 = (bf16[128,2304]{0,1:T(8,128)(2,1)S(1)}, bf16[128,2304]{0,1:T(8,128)(2,1)S(1)}, u32[]{:S(2)}, u32[]{:S(2)}) collective-permute-start(bf16[128,2304]{0,1:T(8,128)(2,1)S(1)} %bitcast.35), channel_id=1, source_target_pairs={{0,4},{4,0},{1,5},{5,1},{2,6},{6,2},{3,7},{7,3},{8,12},{12,8},{9,1... | collective-permute-start | bytes 1769480 | tf_op jit(solution)/shard_map/ppermute | solution.py:217
  132.3 0.6 broadcast_in_dim.76
  132.9 4.4 %all-to-all-start.3 = ((f32[8,1,256]{2,1,0:T(1,128)}), f32[8,1,256]{2,1,0:T(1,128)S(1)}, u32[]{:S(2)}, u32[]{:S(2)}) async-start(f32[8,1,256]{2,1,0:T(1,128)} %broadcast_in_dim.76), calls=%async_computation.3 | async-start | bytes 16384 | tf_op jit(solution)/shard_map/all_to_all | solution.py:48
  137.3 0.3 copy.66
  137.6 4.6 %all-to-all-done.3 = f32[8,1,256]{2,1,0:T(1,128)S(1)} async-done(((f32[8,1,256]{2,1,0:T(1,128)}), f32[8,1,256]{2,1,0:T(1,128)S(1)}, u32[]{:S(2)}, u32[]{:S(2)}) %all-to-all-start.3) | async-done | bytes 8224 | tf_op jit(solution)/shard_map/all_to_all | solution.py:48
  142.2 0.7 broadcast_in_dim.77
  142.8 10.0 %all-to-all-start.4 = ((f32[64,1,256]{2,1,0:T(1,128)}), f32[64,1,256]{2,1,0:T(1,128)S(1)}, u32[]{:S(2)}, u32[]{:S(2)}) async-start(f32[64,1,256]{2,1,0:T(1,128)} %broadcast_in_dim.77), calls=%async_computation.4 | async-start | bytes 131072 | tf_op jit(solution)/shard_map/all_to_all | solution.py:48
  152.8 1.0 fusion.24
  153.8 10.1 %all-to-all-done.4 = f32[64,1,256]{2,1,0:T(1,128)S(1)} async-done(((f32[64,1,256]{2,1,0:T(1,128)}), f32[64,1,256]{2,1,0:T(1,128)S(1)}, u32[]{:S(2)}, u32[]{:S(2)}) %all-to-all-start.4) | async-done | bytes 65568 | tf_op jit(solution)/shard_map/all_to_all | solution.py:48
  164.0 3.5 %all-to-all-start.2 = ((bf16[4,128,576]{1,2,0:T(8,128)(2,1)}), bf16[4,128,576]{1,2,0:T(8,128)(2,1)S(1)}, u32[]{:S(2)}, u32[]{:S(2)}) async-start(bf16[4,128,576]{1,2,0:T(8,128)(2,1)} %bitcast.17), calls=%async_computation.2 | async-start | bytes 1179648 | tf_op jit(solution)/shard_map/all_to_all | solution.py:220
  167.4 0.1 reduce_sum.95
  167.5 0.6 broadcast_multiply_fusion
  168.1 7.4 %all-to-all-done.2 = bf16[4,128,576]{1,2,0:T(8,128)(2,1)S(1)} async-done(((bf16[4,128,576]{1,2,0:T(8,128)(2,1)}), bf16[4,128,576]{1,2,0:T(8,128)(2,1)S(1)}, u32[]{:S(2)}, u32[]{:S(2)}) %all-to-all-start.2) | async-done | bytes 589856 | tf_op jit(solution)/shard_map/all_to_all | solution.py:220
  175.5 0.8 reduce_sum.93
  (34 shorter events, 0.3 us)
Async XLA Ops:
  7.2 34.6 %copy-start = (bf16[128,2304]{1,0:T(8,128)(2,1)S(1)}, bf16[128,2304]{1,0:T(8,128)(2,1)}, u32[]{:S(2)}) copy-start(bf16[128,2304]{1,0:T(8,128)(2,1)} %param.8) | copy-start | bytes 1769476
  7.2 34.9 %copy-start.4 = (s32[256]{0:T(256)S(1)}, s32[256]{0:T(256)}, u32[]{:S(2)}) copy-start(s32[256]{0:T(256)} %param.10) | copy-start | bytes 3076
  7.2 35.7 %copy-start.5 = (s32[256]{0:T(256)S(1)}, s32[256]{0:T(256)}, u32[]{:S(2)}) copy-start(s32[256]{0:T(256)} %param.11) | copy-start | bytes 3076
  7.2 36.3 %copy-start.6 = (s32[1,128]{1,0:T(1,128)S(1)}, s32[1,128]{1,0:T(1,128)}, u32[]{:S(2)}) copy-start(s32[1,128]{1,0:T(1,128)} %param.9) | copy-start | bytes 1540
  7.2 87.8 %all-gather.2.cloned.1.call-start = ((), (), s32[]{:S(2)}) async-start(), calls=%async_computation.5 | async-start | bytes 3981312 | tf_op jit(solution)/shard_map/all_gather | solution.py:177
  45.8 24.8 %all-to-all-start.1 = ((bf16[128,2,288]{2,1,0:T(2,128)(2,1)}), bf16[128,2,288]{2,1,0:T(2,128)(2,1)S(1)}, u32[]{:S(2)}, u32[]{:S(2)}) async-start(bf16[128,2,288]{2,1,0:T(2,128)(2,1)} %reshape.184), calls=%async_computation.1 | async-start | bytes 393216 | tf_op jit(solution)/shard_map/all_to_all | solution.py:181
  84.6 8.1 %copy-start.3 = (f32[2304]{0:T(1024)S(1)}, f32[2304]{0:T(1024)}, u32[]{:S(2)}) copy-start(f32[2304]{0:T(1024)} %param.12) | copy-start | bytes 27652
  84.6 6.2 %collective-permute-start = (bf16[128,2304]{0,1:T(8,128)(2,1)S(1)}, bf16[128,2304]{0,1:T(8,128)(2,1)S(1)}, u32[]{:S(2)}, u32[]{:S(2)}) collective-permute-start(bf16[128,2304]{0,1:T(8,128)(2,1)S(1)} %all_gather.6), channel_id=1, source_target_pairs={{0,4},{4,0},{1,5},{5,1},{2,6},{6,2},{3,7},{7,3},{8,12},{12,8},{9,1... | collective-permute-start | bytes 1769480 | tf_op jit(solution)/shard_map/ppermute | solution.py:184
  101.8 10.0 %copy-start.2 = (bf16[768,768]{1,0:T(8,128)(2,1)}, bf16[768,768]{1,0:T(8,128)(2,1)S(1)}, u32[]{:S(2)}) copy-start(bf16[768,768]{1,0:T(8,128)(2,1)S(1)} %get-tuple-element.26) | copy-start | bytes 3538948
  102.1 19.3 %collective-permute-start.2 = (bf16[256,384]{1,0:T(8,128)(2,1)S(1)}, bf16[256,384]{1,0:T(8,128)(2,1)S(1)}, u32[]{:S(2)}, u32[]{:S(2)}) collective-permute-start(bf16[256,384]{1,0:T(8,128)(2,1)S(1)} %pad_maximum_fusion.1.here), channel_id=1, source_target_pairs={{0,8},{8,16},{16,24},{24,32},{32,40},{40,48},{48,56},{56,64},{64,7... | collective-permute-start | bytes 589832 | tf_op jit(solution)/shard_map/ppermute | solution.py:54
  104.2 17.2 %collective-permute-start.3 = (bf16[256,384]{1,0:T(8,128)(2,1)S(1)}, bf16[256,384]{1,0:T(8,128)(2,1)S(1)}, u32[]{:S(2)}, u32[]{:S(2)}) collective-permute-start(bf16[256,384]{1,0:T(8,128)(2,1)S(1)} %pad_maximum_fusion.1.here), channel_id=1, source_target_pairs={{8,0},{16,8},{24,16},{32,24},{40,32},{48,40},{56,48},{64,56},{72,6... | collective-permute-start | bytes 589832 | tf_op jit(solution)/shard_map/ppermute | solution.py:54
  105.6 8.5 %collective-permute-start.1 = (bf16[128,384]{1,0:T(8,128)(2,1)S(1)}, bf16[128,384]{1,0:T(8,128)(2,1)S(1)}, u32[]{:S(2)}, u32[]{:S(2)}) collective-permute-start(bf16[128,384]{1,0:T(8,128)(2,1)S(1)} %get-tuple-element.25), channel_id=1, source_target_pairs={{0,16},{8,24},{16,32},{24,40},{32,48},{40,56},{48,64},{56,72},{64,... | collective-permute-start | bytes 294920 | tf_op jit(solution)/shard_map/ppermute | solution.py:54
  110.3 11.1 %collective-permute-start.4 = (bf16[128,384]{1,0:T(8,128)(2,1)S(1)}, bf16[128,384]{1,0:T(8,128)(2,1)S(1)}, u32[]{:S(2)}, u32[]{:S(2)}) collective-permute-start(bf16[128,384]{1,0:T(8,128)(2,1)S(1)} %get-tuple-element.24), channel_id=1, source_target_pairs={{16,0},{24,8},{32,16},{40,24},{48,32},{56,40},{64,48},{72,56},{80,... | collective-permute-start | bytes 294920 | tf_op jit(solution)/shard_map/ppermute | solution.py:54
  121.4 2.0 %copy-start.1 = (bf16[2304,768]{1,0:T(8,128)(2,1)S(1)}, bf16[2304,768]{1,0:T(8,128)(2,1)}, u32[]{:S(2)}) copy-start(bf16[2304,768]{1,0:T(8,128)(2,1)} %all-gather.2.cloned.1.call-done.w_any) | copy-start | bytes 10616836
  129.2 23.7 %collective-permute-start.5 = (bf16[128,2304]{0,1:T(8,128)(2,1)S(1)}, bf16[128,2304]{0,1:T(8,128)(2,1)S(1)}, u32[]{:S(2)}, u32[]{:S(2)}) collective-permute-start(bf16[128,2304]{0,1:T(8,128)(2,1)S(1)} %bitcast.35), channel_id=1, source_target_pairs={{0,4},{4,0},{1,5},{5,1},{2,6},{6,2},{3,7},{7,3},{8,12},{12,8},{9,1... | collective-permute-start | bytes 1769480 | tf_op jit(solution)/shard_map/ppermute | solution.py:217
  132.9 9.3 %all-to-all-start.3 = ((f32[8,1,256]{2,1,0:T(1,128)}), f32[8,1,256]{2,1,0:T(1,128)S(1)}, u32[]{:S(2)}, u32[]{:S(2)}) async-start(f32[8,1,256]{2,1,0:T(1,128)} %broadcast_in_dim.76), calls=%async_computation.3 | async-start | bytes 16384 | tf_op jit(solution)/shard_map/all_to_all | solution.py:48
  142.8 21.1 %all-to-all-start.4 = ((f32[64,1,256]{2,1,0:T(1,128)}), f32[64,1,256]{2,1,0:T(1,128)S(1)}, u32[]{:S(2)}, u32[]{:S(2)}) async-start(f32[64,1,256]{2,1,0:T(1,128)} %broadcast_in_dim.77), calls=%async_computation.4 | async-start | bytes 131072 | tf_op jit(solution)/shard_map/all_to_all | solution.py:48
  164.0 11.5 %all-to-all-start.2 = ((bf16[4,128,576]{1,2,0:T(8,128)(2,1)}), bf16[4,128,576]{1,2,0:T(8,128)(2,1)S(1)}, u32[]{:S(2)}, u32[]{:S(2)}) async-start(bf16[4,128,576]{1,2,0:T(8,128)(2,1)} %bitcast.17), calls=%async_computation.2 | async-start | bytes 1179648 | tf_op jit(solution)/shard_map/all_to_all | solution.py:220
Sparse Core Ops, SparseCore 0:
  41.9 51.5 all-gather.1

commit v2 on v1

v2 whole, which is shorter than its diff:
```python
import functools

import jax
import jax.numpy as jnp
from jax import lax
from jax.experimental import pallas as pl
from jax.experimental.pallas import tpu as pltpu
from jax.sharding import Mesh
from jax.sharding import PartitionSpec as P

HEADS = 24
KV_HEADS = 8
HEAD_DIM = 96
GROUP = HEADS // KV_HEADS
SPAN = 3
SEQ = ("y", "z", "c")
COLUMN = ("y", "z")


def segment_of(pos, ends):
    return jnp.sum((ends[None, :] <= pos[:, None]).astype(jnp.int32), axis=1, dtype=jnp.int32)


def probe_signs(seed_row, local_row, width):
    columns = jnp.arange(width, dtype=jnp.int32)
    mixed = seed_row[:, None] * 40503 + local_row[:, None] * 69069 + columns[None, :] * 2654435
    mixed = mixed ^ jnp.right_shift(mixed, 15)
    mixed = mixed * 1597334677
    mixed = mixed ^ jnp.right_shift(mixed, 13)
    mixed = mixed * 668265263
    bit = jnp.right_shift(mixed, 11) & 1
    return (1 - 2 * bit).astype(jnp.float32)


def spread(array, axes):
    count = lax.axis_size(axes)
    copies = jnp.broadcast_to(array[None], (count,) + array.shape)
    return lax.all_to_all(copies, axes, split_axis=0, concat_axis=0, tiled=True)


def moved(array, by):
    count = lax.axis_size(COLUMN)
    pairs = [(i, i + by) for i in range(count) if 0 <= i + by < count]
    return lax.ppermute(array, COLUMN, pairs)


NT = (((1,), (1,)), ((), ()))
VMEM = pl.BlockSpec(memory_space=pltpu.VMEM)
SMEM = pl.BlockSpec(memory_space=pltpu.SMEM)
ANY = pl.BlockSpec(memory_space=pl.ANY)
LANES = 128


def params(mib):
    return pltpu.CompilerParams(vmem_limit_bytes=mib * 1024 * 1024)


def pack_kernel(depth, wq_ref, wkv_ref, wo_ref, out_ref, wide, tall):
    q_width = GROUP * HEAD_DIM
    kv_width = wkv_ref.shape[1] // 2
    tiles = wide.shape[1] // LANES
    wq = wq_ref[...].astype(jnp.float32)
    wkv = wkv_ref[...].astype(jnp.float32)
    wo = wo_ref[...].astype(jnp.float32)
    tall[...] = jnp.zeros_like(tall)
    for core in range(2):
        k, q = core * HEAD_DIM, core * q_width
        wide[:, :HEAD_DIM] = wkv[:, k : k + HEAD_DIM]
        wide[:, HEAD_DIM : 2 * HEAD_DIM] = wkv[:, kv_width + k : kv_width + k + HEAD_DIM]
        wide[:, 2 * HEAD_DIM : 2 * HEAD_DIM + q_width] = wq[:, q : q + q_width]
        wide[:, 2 * HEAD_DIM + q_width :] = wo[:, q : q + q_width]
        for tile in range(tiles):
            tall[tile * depth : (tile + 1) * depth, :] = wide[:, tile * LANES : (tile + 1) * LANES]
        piece = tall[...].astype(jnp.bfloat16)
        for z in range(out_ref.shape[0] // 2):
            out_ref[2 * z + core] = piece


def unpack_kernel(depth, in_ref, out_ref, tall, wide):
    for source in range(in_ref.shape[0]):
        tall[...] = in_ref[source].astype(jnp.float32)
        for tile in range(out_ref.shape[1] // LANES):
            wide[source * depth : (source + 1) * depth, tile * LANES : (tile + 1) * LANES] = tall[
                tile * depth : (tile + 1) * depth, :
            ]
    out_ref[...] = wide[...].astype(jnp.bfloat16)


def norm_kernel(core_ref, own_ref, other_ref, signs_ref, gain_ref, out_ref, wide):
    rows, width = wide.shape
    quarter = own_ref.shape[1]
    gain = gain_ref[...]
    for half in range(2):
        mine = core_ref[0] == half
        for x in range(width // quarter):
            a, b = x * rows, (x + 1) * rows
            both = jnp.where(mine, own_ref[a:b, :].astype(jnp.float32), other_ref[a:b, :].astype(jnp.float32))
            wide[:, x * quarter : (x + 1) * quarter] = both
        x = wide[...]
        signs = signs_ref[half * rows : (half + 1) * rows, :].astype(jnp.float32)
        inv = lax.rsqrt(jnp.sum(x * x, axis=1, keepdims=True) / width + 1e-06)
        along = jnp.sum(x * signs, axis=1, keepdims=True) / width
        out_ref[half * rows : (half + 1) * rows, :] = (x * inv * gain).astype(jnp.bfloat16)
        out_ref[(2 + half) * rows : (3 + half) * rows, :] = (
            (signs * inv - x * (inv * inv * inv * along)) * gain
        ).astype(jnp.bfloat16)


def kv_kernel(hh_ref, w_any, kv_ref, qa_ref, weight, sem):
    block = kv_ref.shape[0]
    fetch = pltpu.make_async_copy(w_any.at[:, pl.ds(0, 2 * LANES)], weight, sem)
    fetch.start()
    fetch.wait()
    both = 2 * HEAD_DIM
    for part in range(2):
        r = jnp.dot(
            hh_ref[part * block : (part + 1) * block, :], weight[...], preferred_element_type=jnp.float32
        )
        kv_ref[:, part * both : (part + 1) * both] = r[:, :both].astype(jnp.bfloat16)
        qa_ref[part * block : (part + 1) * block, :] = r[:, LANES:].astype(jnp.bfloat16)


def q_kernel(hh_ref, signs_ref, qa_ref, w_any, q_ref, u_ref, weight, sem):
    fetch = pltpu.make_async_copy(w_any.at[:, pl.ds(2 * LANES, 4 * LANES)], weight, sem)
    fetch.start()
    fetch.wait()
    early = 2 * LANES - 2 * HEAD_DIM
    late = q_ref.shape[1] - early
    q_ref[:, :early] = qa_ref[:, LANES - early :]
    r = jnp.dot(hh_ref[...], weight[:, : 2 * LANES], preferred_element_type=jnp.float32)
    q_ref[:, early:] = r[:, :late].astype(jnp.bfloat16)
    u_ref[...] = jnp.dot(signs_ref[...], weight[:, LANES:], preferred_element_type=jnp.float32)


def thirds(total):
    high = total.astype(jnp.bfloat16).astype(jnp.float32)
    middle = (total - high).astype(jnp.bfloat16).astype(jnp.float32)
    low = total - high - middle
    at = lax.broadcasted_iota(jnp.int32, (16, total.shape[1]), 0)
    rest = jnp.where(at == 1, middle, jnp.where(at == 2, low, 0.0))
    return jnp.where(at == 0, high, rest).astype(jnp.bfloat16)


def attend_kernel(
    rows, core_ref, q_ref, far_before, before, here, after, far_after, segq_ref, segk_ref, u_ref, w_any,
    mine_ref, theirs_ref, share_ref, window, weight, o_ext, w_sem,
):
    block = 2 * rows
    reach = (2 * SPAN + 1) * rows
    q_width = GROUP * HEAD_DIM
    o_width = weight.shape[1]
    shift = o_width - q_width
    fetch = pltpu.make_async_copy(w_any.at[:, pl.ds(w_any.shape[1] - o_width, o_width)], weight, w_sem)
    fetch.start()
    window[0:rows] = far_before[...]
    window[rows : rows + block] = before[...]
    window[rows + block : rows + 2 * block] = here[...]
    window[rows + 2 * block : rows + 3 * block] = after[...]
    window[rows + 3 * block : 2 * rows + 3 * block] = far_after[...]
    scale = 1.0 / HEAD_DIM**0.5
    to_exp2 = scale * 1.4426950408889634
    o_ext[:, :shift] = jnp.zeros((block, shift), jnp.bfloat16)
    images = share_ref.shape[1]
    share = jnp.zeros((1, images), jnp.float32)
    for tile in range(2):
        lo = tile * rows
        keys = window[lo : lo + reach, 0:HEAD_DIM]
        values = window[lo : lo + reach, HEAD_DIM : 2 * HEAD_DIM]
        keys_t = window[lo : lo + reach, 2 * HEAD_DIM : 3 * HEAD_DIM]
        values_t = window[lo : lo + reach, 3 * HEAD_DIM : 4 * HEAD_DIM]
        mask = segq_ref[lo : lo + rows, :] == segk_ref[:, lo : lo + reach]
        terms = jnp.zeros((rows, 1), jnp.float32)
        for head in range(GROUP):
            a, b = head * HEAD_DIM, (head + 1) * HEAD_DIM
            q = q_ref[lo : lo + rows, a:b]
            q_t = q_ref[block + lo : block + lo + rows, a:b]
            s = lax.dot_general(q, keys, NT, preferred_element_type=jnp.float32)
            s_t = lax.dot_general(q_t, keys, NT, preferred_element_type=jnp.float32)
            s_t += lax.dot_general(q, keys_t, NT, preferred_element_type=jnp.float32)
            s = jnp.where(mask, s, -1e30)
            e = jnp.exp2((s - jnp.max(s, axis=1, keepdims=True)) * to_exp2)
            inv = 1.0 / jnp.sum(e, axis=1, keepdims=True)
            mean = jnp.sum(e * s_t, axis=1, keepdims=True) * inv
            e_t = (e * ((s_t - mean) * scale)).astype(jnp.bfloat16)
            e = e.astype(jnp.bfloat16)
            out = jnp.dot(e, values, preferred_element_type=jnp.float32) * inv
            out_t = jnp.dot(e_t, values, preferred_element_type=jnp.float32)
            out_t += jnp.dot(e, values_t, preferred_element_type=jnp.float32)
            out_t = (out_t * inv).astype(jnp.bfloat16).astype(jnp.float32)
            o_ext[lo : lo + rows, shift + a : shift + b] = out.astype(jnp.bfloat16)
            terms += jnp.sum(out_t * u_ref[lo : lo + rows, shift + a : shift + b], axis=1, keepdims=True)
        numbers = lax.broadcasted_iota(jnp.int32, (rows, images), 1)
        hit = segq_ref[lo : lo + rows, :] == numbers
        share += jnp.sum(jnp.where(hit, terms, 0.0), axis=0, keepdims=True)
    share_ref[...] = share
    width = weight.shape[0]
    theirs_ref[rows:, :images] = thirds(share)
    theirs_ref[rows:, images:] = jnp.zeros((theirs_ref.shape[0] - rows, width - images), jnp.bfloat16)
    fetch.wait()
    step = width // 6
    core = core_ref[0]
    own = o_ext[pl.ds(pl.multiple_of(core * rows, rows), rows), :]
    other = o_ext[pl.ds(pl.multiple_of((1 - core) * rows, rows), rows), :]
    for part in range(6):
        a, b = part * step, (part + 1) * step
        theirs_ref[:rows, a:b] = lax.dot_general(
            other, weight[a:b, :], NT, preferred_element_type=jnp.float32
        ).astype(jnp.bfloat16)
        mine_ref[:, a:b] = lax.dot_general(own, weight[a:b, :], NT, preferred_element_type=jnp.float32)


def join_kernel(mine_ref, share_ref, theirs_ref, out_ref):
    rows = mine_ref.shape[0]
    images = share_ref.shape[1]
    extra, quarter = out_ref.shape[1] - rows, out_ref.shape[2]
    got = theirs_ref[rows:, :images].astype(jnp.float32)
    share = thirds(share_ref[...] + jnp.sum(got, axis=0, keepdims=True))
    for x in range(out_ref.shape[0]):
        a, b = x * quarter, (x + 1) * quarter
        out_ref[x, :rows, :] = (mine_ref[:, a:b] + theirs_ref[:rows, a:b].astype(jnp.float32)).astype(jnp.bfloat16)
        out_ref[x, rows:, :images] = share
        out_ref[x, rows:, images:] = jnp.zeros((extra, quarter - images), jnp.bfloat16)


def body(owned_rows, arrival, image_lengths, probe_seeds, in_gain, w_q, w_kv, w_out):
    bf16, f32 = jnp.bfloat16, jnp.float32
    rows, width = owned_rows.shape
    n_x, n_z, n_seq = lax.axis_size("x"), lax.axis_size("z"), lax.axis_size(SEQ)
    core, member = lax.axis_index("c"), lax.axis_index("x")
    core_word = jnp.reshape(core, (1,)).astype(jnp.int32)
    n_block = lax.axis_size(COLUMN)
    block_index = lax.axis_index(COLUMN)
    quarter = width // n_x
    depth = w_q.shape[0]
    block = 2 * rows
    images = image_lengths.shape[0]
    q_width = GROUP * HEAD_DIM
    columns = 2 * HEAD_DIM + 2 * q_width

    tall_rows = -(-depth * (columns // LANES) // 16) * 16
    pieces = pl.pallas_call(
        functools.partial(pack_kernel, depth),
        out_shape=jax.ShapeDtypeStruct((2 * n_z, tall_rows, LANES), bf16),
        in_specs=[VMEM] * 3,
        out_specs=VMEM,
        scratch_shapes=[pltpu.VMEM((depth, columns), f32), pltpu.VMEM((tall_rows, LANES), f32)],
        compiler_params=params(16),
    )(w_q, w_kv.reshape(depth, -1), w_out.T)
    strip = lax.all_to_all(pieces, ("z", "c"), split_axis=0, concat_axis=0, tiled=True)
    strip = pl.pallas_call(
        functools.partial(unpack_kernel, depth),
        out_shape=jax.ShapeDtypeStruct((2 * n_z * depth, columns), bf16),
        in_specs=[VMEM],
        out_specs=VMEM,
        scratch_shapes=[pltpu.VMEM((tall_rows, LANES), f32), pltpu.VMEM((2 * n_z * depth, columns), f32)],
        compiler_params=params(16),
    )(strip)
    weights = lax.all_gather(strip, "y", axis=0, tiled=True)

    part = lax.dynamic_slice_in_dim(owned_rows, member * quarter, quarter, 1)
    padded = -(-quarter // LANES) * LANES
    part = jnp.pad(part, ((0, 0), (0, padded - quarter))).reshape(rows, 1, padded)
    part, strip = lax.optimization_barrier((part, strip))
    arrived = lax.all_to_all(part, SEQ, split_axis=0, concat_axis=0, tiled=True)
    arrived = jnp.take(arrived.reshape(rows, padded)[:, :quarter], arrival[0], axis=0)
    own = lax.all_gather(arrived, "x", axis=0, tiled=True)
    other = lax.ppermute(own, "c", [(0, 1), (1, 0)])

    ends = jnp.cumsum(image_lengths, dtype=jnp.int32)
    starts = ends - image_lengths
    first = block_index * block
    positions = first + jnp.arange(block, dtype=jnp.int32)
    seg = segment_of(positions, ends)
    onehot = seg[:, None] == jnp.arange(images, dtype=jnp.int32)[None, :]
    start_row = jnp.sum(jnp.where(onehot, starts[None, :], 0), axis=1, dtype=jnp.int32)
    seed_row = jnp.sum(jnp.where(onehot, probe_seeds[None, :], 0), axis=1, dtype=jnp.int32)
    signs = probe_signs(seed_row, positions - start_row, width).astype(bf16)
    kpos = first - SPAN * rows + jnp.arange(block + 2 * SPAN * rows, dtype=jnp.int32)
    valid = (kpos >= 0) & (kpos < block * n_block)
    segk = jnp.where(valid, segment_of(kpos, ends), -1)

    hh = pl.pallas_call(
        norm_kernel,
        out_shape=jax.ShapeDtypeStruct((2 * block, width), bf16),
        in_specs=[SMEM] + [VMEM] * 4,
        out_specs=VMEM,
        scratch_shapes=[pltpu.VMEM((rows, width), f32)],
        compiler_params=params(24),
    )(core_word, own, other, signs, in_gain[None, :])

    kv, q_early = pl.pallas_call(
        kv_kernel,
        out_shape=(
            jax.ShapeDtypeStruct((block, 4 * HEAD_DIM), bf16),
            jax.ShapeDtypeStruct((2 * block, LANES), bf16),
        ),
        in_specs=[VMEM, ANY],
        out_specs=(VMEM, VMEM),
        scratch_shapes=[pltpu.VMEM((width, 2 * LANES), bf16), pltpu.SemaphoreType.DMA],
        compiler_params=params(24),
        cost_estimate=pl.CostEstimate(flops=4 * block * width * 2 * LANES, bytes_accessed=4_000_000, transcendentals=0),
    )(hh, weights)
    neighbours = (moved(kv[rows:], 2), moved(kv, 1), kv, moved(kv, -1), moved(kv[:rows], -2))
    q, u = pl.pallas_call(
        q_kernel,
        out_shape=(
            jax.ShapeDtypeStruct((2 * block, q_width), bf16),
            jax.ShapeDtypeStruct((block, 3 * LANES), f32),
        ),
        in_specs=[VMEM, VMEM, VMEM, ANY],
        out_specs=(VMEM, VMEM),
        scratch_shapes=[pltpu.VMEM((width, 4 * LANES), bf16), pltpu.SemaphoreType.DMA],
        compiler_params=params(24),
        cost_estimate=pl.CostEstimate(flops=6 * block * width * 3 * LANES, bytes_accessed=6_000_000, transcendentals=0),
    )(hh, signs, q_early, weights)

    mine, theirs, share = pl.pallas_call(
        functools.partial(attend_kernel, rows),
        out_shape=(
            jax.ShapeDtypeStruct((rows, width), f32),
            jax.ShapeDtypeStruct((rows + 16, width), bf16),
            jax.ShapeDtypeStruct((1, images), f32),
        ),
        in_specs=[SMEM] + [VMEM] * 9 + [ANY],
        out_specs=(VMEM, VMEM, VMEM),
        scratch_shapes=[
            pltpu.VMEM((8 * rows, 4 * HEAD_DIM), bf16),
            pltpu.VMEM((width, 3 * LANES), bf16),
            pltpu.VMEM((block, 3 * LANES), bf16),
            pltpu.SemaphoreType.DMA,
        ],
        compiler_params=params(40),
        cost_estimate=pl.CostEstimate(flops=2_000_000_000, bytes_accessed=5_000_000, transcendentals=700_000),
    )(core_word, q, *neighbours, seg[:, None], segk[None, :], u, weights)

    theirs = lax.ppermute(theirs, "c", [(0, 1), (1, 0)])
    group = pl.pallas_call(
        join_kernel,
        out_shape=jax.ShapeDtypeStruct((n_x, rows + 16, quarter), bf16),
        in_specs=[VMEM] * 3,
        out_specs=VMEM,
        compiler_params=params(16),
    )(mine, share, theirs)
    groups = lax.all_to_all(group, "x", split_axis=0, concat_axis=0, tiled=True)
    velocity = jnp.sum(groups[:, :rows].astype(f32), axis=0).astype(bf16)
    share = jnp.sum(groups[:, rows:, :images].astype(f32), axis=(0, 1))
    divergence = jnp.sum(spread(share, COLUMN), axis=0) / width
    return (velocity, divergence)


def solution(mesh):
    n_seq, n_x = mesh.devices.shape
    n_y = 1
    while n_y * n_y * 2 < n_seq:
        n_y *= 2
    devices = mesh.devices.reshape(n_y, n_seq // 2 // n_y, 2, n_x)
    split = Mesh(devices, ("y", "z", "c", "x"))
    in_specs = (
        P(SEQ, None),
        P(SEQ, None),
        P(),
        P(),
        P(),
        P(SEQ, "x"),
        P(SEQ, None, "x"),
        P("x", SEQ),
    )
    out_specs = (P(SEQ, "x"), P())
    return jax.shard_map(body, mesh=split, in_specs=in_specs, out_specs=out_specs, check_vma=False)
```

time: 185 us -> 170 us (0.919)
  blocking collectives: 43 us -> 55 us
  waiting for transfers between devices: 45 us -> 34.6 us
  starting transfers between devices: 43.9 us -> 35.5 us
  matrix products: 6.8 us -> 0 us
  other arithmetic: 11 us -> 4.86 us
  Pallas kernels: 5.37 us -> 11 us
    all_to_all x0 -> x1, blocking collectives: none -> 14.7 us  [body(): groups = lax.all_to_all(group, 'x', split_axis=0, concat_axis=0, tiled=True)]
    all_to_all x1 -> x0, waiting for transfers between devices: 7.39 us -> none  [body(): groups = lax.all_to_all(group, 'x', split_axis=0, concat_axis=0, tiled=True)]
    dot_general x1 -> x0, matrix products: 6.8 us -> none  [body(): products = jnp.dot(stacked, weights, preferred_element_type=jnp.float32)]
    pallas_call x1 -> x7, Pallas kernels: 5.37 us -> 11 us  [the longest x1 5.63 us: body(): pl.pallas_call(functools.partial(attend_kernel, rows), out_shape=(jax.Sha...]
    unnamed x18 -> x32, local copies, waits for them, and re-layouts: 3.68 us -> 8.94 us
    all_to_all x2 -> x1, starting transfers between devices: 14.4 us -> 9.21 us  [spread(): return lax.all_to_all(copies, axes, split_axis=0, concat_axis=0, tiled=True)]
    all_to_all x2 -> x1, waiting for transfers between devices: 14.7 us -> 10.2 us  [spread(): return lax.all_to_all(copies, axes, split_axis=0, concat_axis=0, tiled=True)]
    all_to_all x1 -> x0, starting transfers between devices: 3.48 us -> none  [body(): groups = lax.all_to_all(group, 'x', split_axis=0, concat_axis=0, tiled=True)]
  transfers between devices with their start and end apart: 11 -> 9, of which waited for: 5 -> 4; matrix products, arithmetic and copies ran while one was open for 9% -> 6% of each run, Pallas kernels for 0% -> 2%
where the time goes in v2:
time: 170 us; the launch traced here: 169 us
  blocking collectives  55 us (32%)
  starting transfers between devices  35.5 us (21%)
  waiting for transfers between devices  34.6 us (20%)
  between operations  14.4 us (8%)
  local copies, waits for them, and re-layouts  13.7 us (8%)
  Pallas kernels  11 us (6%)
  other arithmetic  4.86 us (3%)
    all_to_all x1, blocking collectives, body(): lax.all_to_all(pieces, ('z', 'c'), split_axis=0, concat_axis=0, tiled=True)  27.6 us
    all_to_all x1, waiting for transfers between devices, body(): arrived = lax.all_to_all(part, SEQ, split_axis=0, concat_axis=0, tiled=True)  15.5 us
    all_to_all x1, blocking collectives, body(): groups = lax.all_to_all(group, 'x', split_axis=0, concat_axis=0, tiled=True)  14.7 us
    all_gather x1, blocking collectives, body(): own = lax.all_gather(arrived, 'x', axis=0, tiled=True)  12.7 us
    all_to_all x1, waiting for transfers between devices, spread(): return lax.all_to_all(copies, axes, split_axis=0, concat_axis=0, tiled=True)  10.2 us
    all_to_all x1, starting transfers between devices, body(): arrived = lax.all_to_all(part, SEQ, split_axis=0, concat_axis=0, tiled=True)  9.43 us
    all_to_all x1, starting transfers between devices, spread(): return lax.all_to_all(copies, axes, split_axis=0, concat_axis=0, tiled=True)  9.21 us
    ppermute x4, starting transfers between devices, moved(): return lax.ppermute(array, COLUMN, pairs)  9.02 us
  transfers between devices with their start and end apart: 9, of which 4 were waited for; matrix products, arithmetic and copies ran while one was open for 6% of the time, Pallas kernels for 2%

profile of v2, /device:TPU:1, one launch (start us, length us, event | category | flops | bytes accessed | tf_op | source)
XLA Modules:
  0.0 169.1 jit_solution(11284338707171661674)
XLA Ops:
  7.2 0.0 copy-start
  7.2 0.0 copy-start.11
  7.2 0.0 copy-start.10
  7.2 0.0 copy-start.12
  7.2 0.0 copy-start.13
  7.2 0.0 all-gather.2.cloned.1.call-start
  7.3 0.9 reshape.136.wkv_ref
  8.2 0.8 copy-done.8
  8.9 0.8 copy-done.9
  9.7 0.1 shard_map.95
  9.8 27.6 %all_to_all.21.in_ref = bf16[16,112,128]{2,1,0:T(8,128)(2,1)S(1)} all-to-all(bf16[16,112,128]{2,1,0:T(8,128)(2,1)S(1)} %shard_map.95), channel_id=1, replica_groups=mesh['y'=8,'z'=8,'c'=2,'x'=4] {'z','c'}, dimensions={0} | all-to-all | bytes 917504 | tf_op jit(solution)/shard_map/all_to_all | solution.py:249
  37.4 1.0 shard_map.96
  38.4 0.0 all-gather.2.cloned.1.call-update
  38.4 0.3 reduce-window.9
  38.7 0.1 slice.23
  38.8 0.1 slice_reduce_fusion.1
  39.0 0.1 fusion.9
  39.0 0.2 convert_reduce_fusion.1
  39.2 0.1 copy.28.segq_ref
  39.4 0.1 constant_dynamic-slice_fusion
  39.6 0.2 select_reduce_fusion.1
  39.8 0.4 convert_reduce_fusion
  40.2 0.5 broadcast.106
  40.7 0.7 reduce.4
  41.4 0.9 reshape.149
  42.3 9.4 %all-to-all-start.1 = ((bf16[128,2,320]{2,1,0:T(2,128)(2,1)}), bf16[128,2,320]{2,1,0:T(2,128)(2,1)S(1)}, u32[]{:S(2)}, u32[]{:S(2)}) async-start(bf16[128,2,320]{2,1,0:T(2,128)(2,1)} %reshape.149), calls=%async_computation.1 | async-start | bytes 393216 | tf_op jit(solution)/shard_map/all_to_all | solution.py:264
  51.8 15.5 %all-to-all-done.1 = bf16[128,2,320]{2,1,0:T(2,128)(2,1)S(1)} async-done(((bf16[128,2,320]{2,1,0:T(2,128)(2,1)}), bf16[128,2,320]{2,1,0:T(2,128)(2,1)S(1)}, u32[]{:S(2)}, u32[]{:S(2)}) %all-to-all-start.1) | async-done | bytes 163872 | tf_op jit(solution)/shard_map/all_to_all | solution.py:264
  67.3 0.3 reshape.150
  67.6 0.9 gather_fusion
  68.5 0.1 broadcast_select_fusion
  68.6 12.7 %all_gather.6.own_ref = bf16[512,576]{1,0:T(8,128)(2,1)S(1)} all-gather(bf16[128,576]{1,0:T(8,128)(2,1)S(1)} %broadcast_select_fusion), channel_id=1, replica_groups=mesh['y'=8,'z'=8,'c'=2,'x'=4] {'x'}, dimensions={0}, use_global_device_ids=true | all-gather | bytes 737280 | tf_op jit(solution)/shard_map/all_gather | solution.py:266
  81.3 0.2 copy.26
  81.5 3.9 %collective-permute-start = (bf16[512,576]{0,1:T(8,128)(2,1)S(1)}, bf16[512,576]{0,1:T(8,128)(2,1)S(1)}, u32[]{:S(2)}, u32[]{:S(2)}) collective-permute-start(bf16[512,576]{0,1:T(8,128)(2,1)S(1)} %copy.26), channel_id=1, source_target_pairs={{0,4},{4,0},{1,5},{5,1},{2,6},{6,2},{3,7},{7,3},{8,12},{12,8},{9,1... | collective-permute-start | bytes 1769480 | tf_op jit(solution)/shard_map/ppermute | solution.py:267
  85.4 2.0 %fusion.7.signs_ref = bf16[256,2304]{1,0:T(8,128)(2,1)} fusion(s32[2304]{0:T(1024)S(1)} %iota_multiply_fusion, s32[256]{0:T(256)S(1)} %multiply_add_fusion), kind=kLoop, calls=%fused_computation.10 | loop fusion | flops 7667712 | bytes 1189888 | tf_op jit(solution)/shard_map/convert_element_type | solution.py:277
  87.5 0.0 collective-permute-done
  87.5 1.1 copy.27.other_ref
  88.6 1.3 copy-done.3
  89.9 1.1 copy-done.6
  91.0 1.1 copy-done.7
  92.1 1.5 shard_map.97.hh_ref
  93.5 0.0 all-gather.2.cloned.1.call-done.w_any
  93.6 2.0 %copy-done.1 = bf16[2304,768]{1,0:T(8,128)(2,1)S(1)} copy-done((bf16[2304,768]{1,0:T(8,128)(2,1)S(1)}, bf16[2304,768]{1,0:T(8,128)(2,1)}, u32[]{:S(2)}) %copy-start.1) | copy-done | bytes 3538968
  95.6 0.9 shard_map.98
  96.5 2.3 %collective-permute-start.2 = (bf16[256,384]{1,0:T(8,128)(2,1)S(1)}, bf16[256,384]{1,0:T(8,128)(2,1)S(1)}, u32[]{:S(2)}, u32[]{:S(2)}) collective-permute-start(bf16[256,384]{1,0:T(8,128)(2,1)S(1)} %get-tuple-element.13.here), channel_id=1, source_target_pairs={{0,8},{8,16},{16,24},{24,32},{32,40},{40,48},{48,56},{56,64},{64,7... | collective-permute-start | bytes 589832 | tf_op jit(solution)/shard_map/ppermute | solution.py:44
  98.8 1.3 collective-permute-start.3
  100.1 4.0 %collective-permute-start.1 = (bf16[128,384]{1,0:T(8,128)(2,1)S(1)}, bf16[128,384]{1,0:T(8,128)(2,1)S(1)}, u32[]{:S(2)}, u32[]{:S(2)}) collective-permute-start(bf16[128,384]{1,0:T(8,128)(2,1)S(1)} %get-tuple-element.31), channel_id=1, source_target_pairs={{0,16},{8,24},{16,32},{24,40},{32,48},{40,56},{48,64},{56,72},{64,... | collective-permute-start | bytes 294920 | tf_op jit(solution)/shard_map/ppermute | solution.py:44
  104.1 1.5 collective-permute-start.4
  105.6 1.7 shard_map.99
  107.3 0.0 collective-permute-done.1.far_before
  107.3 7.2 %collective-permute-done.4.far_after = bf16[128,384]{1,0:T(8,128)(2,1)S(1)} collective-permute-done((bf16[128,384]{1,0:T(8,128)(2,1)S(1)}, bf16[128,384]{1,0:T(8,128)(2,1)S(1)}, u32[]{:S(2)}, u32[]{:S(2)}) %collective-permute-start.4) | collective-permute-done | bytes 98336 | tf_op jit(solution)/shard_map/ppermute | solution.py:44
  114.4 0.0 collective-permute-done.2.before
  114.4 0.0 collective-permute-done.3.after
  114.4 5.6 %shard_map.100 = (f32[128,2304]{1,0:T(8,128)S(1)}, bf16[144,2304]{1,0:T(8,128)(2,1)S(1)}, f32[1,256]{1,0:T(1,128)S(1)}) custom-call(s32[1]{0:T(128)} %bitcast.core_ref, bf16[512,288]{1,0:T(8,128)(2,1)S(1)} %get-tuple-element.12.q_ref, bf16[128,384]{1,0:T(8,128)(2,1)S(1)} %collective-permute-done.1.far_before, ...), custom_call_target="tpu_custom_call" | custom-call | flops 2000000000 | bytes 5000000 | tf_op jit(solution)/shard_map/pallas_call | solution.py:317
  120.1 3.9 %collective-permute-start.5 = (bf16[144,2304]{1,0:T(8,128)(2,1)S(1)}, bf16[144,2304]{1,0:T(8,128)(2,1)S(1)}, u32[]{:S(2)}, u32[]{:S(2)}) collective-permute-start(bf16[144,2304]{1,0:T(8,128)(2,1)S(1)} %get-tuple-element.17), channel_id=1, source_target_pairs={{0,4},{4,0},{1,5},{5,1},{2,6},{6,2},{3,7},{7,3},{8,12},{12,8},{9,1... | collective-permute-start | bytes 1990664 | tf_op jit(solution)/shard_map/ppermute | solution.py:336
  123.9 1.7 %collective-permute-done.5.theirs_ref = bf16[144,2304]{1,0:T(8,128)(2,1)S(1)} collective-permute-done((bf16[144,2304]{1,0:T(8,128)(2,1)S(1)}, bf16[144,2304]{1,0:T(8,128)(2,1)S(1)}, u32[]{:S(2)}, u32[]{:S(2)}) %collective-permute-start.5) | collective-permute-done | bytes 663584 | tf_op jit(solution)/shard_map/ppermute | solution.py:336
  125.7 0.2 shard_map.101
  125.9 14.7 %all_to_all.22 = bf16[4,144,576]{2,1,0:T(8,128)(2,1)S(1)} all-to-all(bf16[4,144,576]{2,1,0:T(8,128)(2,1)S(1)} %shard_map.101), channel_id=1, replica_groups=mesh['y'=8,'z'=8,'c'=2,'x'=4] {'x'}, dimensions={0} | all-to-all | bytes 1327104 | tf_op jit(solution)/shard_map/all_to_all | solution.py:344
  140.6 0.7 broadcast_in_dim.64
  141.2 9.2 %all-to-all-start.3 = ((f32[64,1,256]{2,1,0:T(1,128)}), f32[64,1,256]{2,1,0:T(1,128)S(1)}, u32[]{:S(2)}, u32[]{:S(2)}) async-start(f32[64,1,256]{2,1,0:T(1,128)} %broadcast_in_dim.64), calls=%async_computation.3 | async-start | bytes 131072 | tf_op jit(solution)/shard_map/all_to_all | solution.py:38
  150.5 0.1 slice_reduce_fusion
  150.6 0.8 copy.30
  151.4 10.2 %all-to-all-done.3 = f32[64,1,256]{2,1,0:T(1,128)S(1)} async-done(((f32[64,1,256]{2,1,0:T(1,128)}), f32[64,1,256]{2,1,0:T(1,128)S(1)}, u32[]{:S(2)}, u32[]{:S(2)}) %all-to-all-start.3) | async-done | bytes 65568 | tf_op jit(solution)/shard_map/all_to_all | solution.py:38
  161.6 0.1 reduce_sum.75
  161.7 0.6 broadcast_multiply_fusion
  (30 shorter events, 0.2 us)
Async XLA Ops:
  7.2 32.2 %copy-start = (bf16[128,2304]{1,0:T(8,128)(2,1)S(1)}, bf16[128,2304]{1,0:T(8,128)(2,1)}, u32[]{:S(2)}) copy-start(bf16[128,2304]{1,0:T(8,128)(2,1)} %param.8) | copy-start | bytes 1769476
  7.2 31.2 %copy-start.11 = (s32[256]{0:T(256)S(1)}, s32[256]{0:T(256)}, u32[]{:S(2)}) copy-start(s32[256]{0:T(256)} %param.10) | copy-start | bytes 3076
  7.2 31.6 %copy-start.10 = (f32[2304]{0:T(1024)S(1)}, f32[2304]{0:T(1024)}, u32[]{:S(2)}) copy-start(f32[2304]{0:T(1024)} %param.12) | copy-start | bytes 27652
  7.2 32.4 %copy-start.12 = (s32[256]{0:T(256)S(1)}, s32[256]{0:T(256)}, u32[]{:S(2)}) copy-start(s32[256]{0:T(256)} %param.11) | copy-start | bytes 3076
  7.2 33.0 %copy-start.13 = (s32[1,128]{1,0:T(1,128)S(1)}, s32[1,128]{1,0:T(1,128)}, u32[]{:S(2)}) copy-start(s32[1,128]{1,0:T(1,128)} %param.9) | copy-start | bytes 1540
  7.2 86.3 %all-gather.2.cloned.1.call-start = ((), (), s32[]{:S(2)}) async-start(), calls=%async_computation.4 | async-start | bytes 3981312 | tf_op jit(solution)/shard_map/all_gather | solution.py:258
  8.2 0.8 copy-start.8
  8.9 0.8 copy-start.9
  42.3 25.0 %all-to-all-start.1 = ((bf16[128,2,320]{2,1,0:T(2,128)(2,1)}), bf16[128,2,320]{2,1,0:T(2,128)(2,1)S(1)}, u32[]{:S(2)}, u32[]{:S(2)}) async-start(bf16[128,2,320]{2,1,0:T(2,128)(2,1)} %reshape.149), calls=%async_computation.1 | async-start | bytes 393216 | tf_op jit(solution)/shard_map/all_to_all | solution.py:264
  81.3 7.3 %copy-start.5 = (bf16[512,576]{1,0:T(8,128)(2,1)}, bf16[512,576]{1,0:T(8,128)(2,1)S(1)}, u32[]{:S(2)}) copy-start(bf16[512,576]{1,0:T(8,128)(2,1)S(1)} %all_gather.6.own_ref) | copy-start | bytes 1769476
  81.5 6.0 %collective-permute-start = (bf16[512,576]{0,1:T(8,128)(2,1)S(1)}, bf16[512,576]{0,1:T(8,128)(2,1)S(1)}, u32[]{:S(2)}, u32[]{:S(2)}) collective-permute-start(bf16[512,576]{0,1:T(8,128)(2,1)S(1)} %copy.26), channel_id=1, source_target_pairs={{0,4},{4,0},{1,5},{5,1},{2,6},{6,2},{3,7},{7,3},{8,12},{12,8},{9,1... | collective-permute-start | bytes 1769480 | tf_op jit(solution)/shard_map/ppermute | solution.py:267
  88.6 1.3 copy-start.3
  89.9 1.1 copy-start.6
  91.0 1.1 copy-start.7
  93.6 2.0 %copy-start.1 = (bf16[2304,768]{1,0:T(8,128)(2,1)S(1)}, bf16[2304,768]{1,0:T(8,128)(2,1)}, u32[]{:S(2)}) copy-start(bf16[2304,768]{1,0:T(8,128)(2,1)} %all-gather.2.cloned.1.call-done.w_any) | copy-start | bytes 10616836
  95.6 10.0 %copy-start.2 = (bf16[2304,768]{1,0:T(8,128)(2,1)S(1)}, bf16[2304,768]{1,0:T(8,128)(2,1)}, u32[]{:S(2)}) copy-start(bf16[2304,768]{1,0:T(8,128)(2,1)} %all-gather.2.cloned.1.call-done.w_any) | copy-start | bytes 10616836
  95.6 10.0 %copy-start.4 = (bf16[256,2304]{1,0:T(8,128)(2,1)S(1)}, bf16[256,2304]{1,0:T(8,128)(2,1)}, u32[]{:S(2)}) copy-start(bf16[256,2304]{1,0:T(8,128)(2,1)} %fusion.7.signs_ref) | copy-start | bytes 3538948
  96.5 17.9 %collective-permute-start.2 = (bf16[256,384]{1,0:T(8,128)(2,1)S(1)}, bf16[256,384]{1,0:T(8,128)(2,1)S(1)}, u32[]{:S(2)}, u32[]{:S(2)}) collective-permute-start(bf16[256,384]{1,0:T(8,128)(2,1)S(1)} %get-tuple-element.13.here), channel_id=1, source_target_pairs={{0,8},{8,16},{16,24},{24,32},{32,40},{40,48},{48,56},{56,64},{64,7... | collective-permute-start | bytes 589832 | tf_op jit(solution)/shard_map/ppermute | solution.py:44
  98.8 15.7 %collective-permute-start.3 = (bf16[256,384]{1,0:T(8,128)(2,1)S(1)}, bf16[256,384]{1,0:T(8,128)(2,1)S(1)}, u32[]{:S(2)}, u32[]{:S(2)}) collective-permute-start(bf16[256,384]{1,0:T(8,128)(2,1)S(1)} %get-tuple-element.13.here), channel_id=1, source_target_pairs={{8,0},{16,8},{24,16},{32,24},{40,32},{48,40},{56,48},{64,56},{72,6... | collective-permute-start | bytes 589832 | tf_op jit(solution)/shard_map/ppermute | solution.py:44
  100.1 7.2 %collective-permute-start.1 = (bf16[128,384]{1,0:T(8,128)(2,1)S(1)}, bf16[128,384]{1,0:T(8,128)(2,1)S(1)}, u32[]{:S(2)}, u32[]{:S(2)}) collective-permute-start(bf16[128,384]{1,0:T(8,128)(2,1)S(1)} %get-tuple-element.31), channel_id=1, source_target_pairs={{0,16},{8,24},{16,32},{24,40},{32,48},{40,56},{48,64},{56,72},{64,... | collective-permute-start | bytes 294920 | tf_op jit(solution)/shard_map/ppermute | solution.py:44
  104.1 10.3 %collective-permute-start.4 = (bf16[128,384]{1,0:T(8,128)(2,1)S(1)}, bf16[128,384]{1,0:T(8,128)(2,1)S(1)}, u32[]{:S(2)}, u32[]{:S(2)}) collective-permute-start(bf16[128,384]{1,0:T(8,128)(2,1)S(1)} %get-tuple-element.30), channel_id=1, source_target_pairs={{16,0},{24,8},{32,16},{40,24},{48,32},{56,40},{64,48},{72,56},{80,... | collective-permute-start | bytes 294920 | tf_op jit(solution)/shard_map/ppermute | solution.py:44
  120.1 5.6 %collective-permute-start.5 = (bf16[144,2304]{1,0:T(8,128)(2,1)S(1)}, bf16[144,2304]{1,0:T(8,128)(2,1)S(1)}, u32[]{:S(2)}, u32[]{:S(2)}) collective-permute-start(bf16[144,2304]{1,0:T(8,128)(2,1)S(1)} %get-tuple-element.17), channel_id=1, source_target_pairs={{0,4},{4,0},{1,5},{5,1},{2,6},{6,2},{3,7},{7,3},{8,12},{12,8},{9,1... | collective-permute-start | bytes 1990664 | tf_op jit(solution)/shard_map/ppermute | solution.py:336
  141.2 20.3 %all-to-all-start.3 = ((f32[64,1,256]{2,1,0:T(1,128)}), f32[64,1,256]{2,1,0:T(1,128)S(1)}, u32[]{:S(2)}, u32[]{:S(2)}) async-start(f32[64,1,256]{2,1,0:T(1,128)} %broadcast_in_dim.64), calls=%async_computation.3 | async-start | bytes 131072 | tf_op jit(solution)/shard_map/all_to_all | solution.py:38
Sparse Core Ops, SparseCore 0:
  38.5 51.6 all-gather.1

commit v3 on v2

--- a/solution.py
+++ b/solution.py
@@ -55,20 +55,20 @@
     return pltpu.CompilerParams(vmem_limit_bytes=mib * 1024 * 1024)
 
 
-def pack_kernel(depth, wq_ref, wkv_ref, wo_ref, out_ref, wide, tall):
+def pack_kernel(depth, in_ref, out_ref, wide, tall):
     q_width = GROUP * HEAD_DIM
-    kv_width = wkv_ref.shape[1] // 2
     tiles = wide.shape[1] // LANES
-    wq = wq_ref[...].astype(jnp.float32)
-    wkv = wkv_ref[...].astype(jnp.float32)
-    wo = wo_ref[...].astype(jnp.float32)
+    k_first = 2 * q_width
+    v_first = k_first + 2 * HEAD_DIM
+    o_first = v_first + 2 * HEAD_DIM
+    held = in_ref[...].astype(jnp.float32)
     tall[...] = jnp.zeros_like(tall)
     for core in range(2):
         k, q = core * HEAD_DIM, core * q_width
-        wide[:, :HEAD_DIM] = wkv[:, k : k + HEAD_DIM]
-        wide[:, HEAD_DIM : 2 * HEAD_DIM] = wkv[:, kv_width + k : kv_width + k + HEAD_DIM]
-        wide[:, 2 * HEAD_DIM : 2 * HEAD_DIM + q_width] = wq[:, q : q + q_width]
-        wide[:, 2 * HEAD_DIM + q_width :] = wo[:, q : q + q_width]
+        wide[:, :HEAD_DIM] = held[:, k_first + k : k_first + k + HEAD_DIM]
+        wide[:, HEAD_DIM : 2 * HEAD_DIM] = held[:, v_first + k : v_first + k + HEAD_DIM]
+        wide[:, 2 * HEAD_DIM : 2 * HEAD_DIM + q_width] = held[:, q : q + q_width]
+        wide[:, 2 * HEAD_DIM + q_width :] = held[:, o_first + q : o_first + q + q_width]
         for tile in range(tiles):
             tall[tile * depth : (tile + 1) * depth, :] = wide[:, tile * LANES : (tile + 1) * LANES]
         piece = tall[...].astype(jnp.bfloat16)
@@ -88,14 +88,15 @@
 
 def norm_kernel(core_ref, own_ref, other_ref, signs_ref, gain_ref, out_ref, wide):
     rows, width = wide.shape
-    quarter = own_ref.shape[1]
+    members = own_ref.shape[0] // rows
+    quarter = width // members
     gain = gain_ref[...]
     for half in range(2):
         mine = core_ref[0] == half
-        for x in range(width // quarter):
+        for x in range(members):
             a, b = x * rows, (x + 1) * rows
             both = jnp.where(mine, own_ref[a:b, :].astype(jnp.float32), other_ref[a:b, :].astype(jnp.float32))
-            wide[:, x * quarter : (x + 1) * quarter] = both
+            wide[:, x * quarter : (x + 1) * quarter] = both[:, :quarter]
         x = wide[...]
         signs = signs_ref[half * rows : (half + 1) * rows, :].astype(jnp.float32)
         inv = lax.rsqrt(jnp.sum(x * x, axis=1, keepdims=True) / width + 1e-06)
@@ -106,52 +107,52 @@
         ).astype(jnp.bfloat16)
 
 
-def kv_kernel(hh_ref, w_any, kv_ref, qa_ref, weight, sem):
+def project_kernel(hh_any, signs_any, w_any, kv_ref, head_ref, tail_ref, q_ref, u_ref, hh, signs, weight, sems):
     block = kv_ref.shape[0]
-    fetch = pltpu.make_async_copy(w_any.at[:, pl.ds(0, 2 * LANES)], weight, sem)
-    fetch.start()
-    fetch.wait()
+    rows = block // 2
     both = 2 * HEAD_DIM
+    q_width = q_ref.shape[1]
+    depth = weight.shape[1]
+    thirds = weight.shape[0]
+    fetches = []
+    for k in range(thirds):
+        at = pl.ds(k * depth, depth)
+        fetches.append(
+            (
+                pltpu.make_async_copy(w_any.at[at, :], weight.at[k], sems.at[k, 0]),
+                pltpu.make_async_copy(hh_any.at[:, at], hh.at[k], sems.at[k, 1]),
+                pltpu.make_async_copy(signs_any.at[:, at], signs.at[k], sems.at[k, 2]),
+            )
+        )
+        for fetch in fetches[k]:
+            fetch.start()
+    for k in range(thirds):
+        for fetch in fetches[k]:
+            fetch.wait()
+        r_k = jnp.dot(hh[k], weight[k, :, : 4 * LANES], preferred_element_type=jnp.float32)
+        u_k = jnp.dot(signs[k], weight[k, :, 3 * LANES :], preferred_element_type=jnp.float32)
+        r, u = (r_k, u_k) if k == 0 else (r + r_k, u + u_k)
     for part in range(2):
-        r = jnp.dot(
-            hh_ref[part * block : (part + 1) * block, :], weight[...], preferred_element_type=jnp.float32
-        )
-        kv_ref[:, part * both : (part + 1) * both] = r[:, :both].astype(jnp.bfloat16)
-        qa_ref[part * block : (part + 1) * block, :] = r[:, LANES:].astype(jnp.bfloat16)
-
-
-def q_kernel(hh_ref, signs_ref, qa_ref, w_any, q_ref, u_ref, weight, sem):
-    fetch = pltpu.make_async_copy(w_any.at[:, pl.ds(2 * LANES, 4 * LANES)], weight, sem)
-    fetch.start()
-    fetch.wait()
-    early = 2 * LANES - 2 * HEAD_DIM
-    late = q_ref.shape[1] - early
-    q_ref[:, :early] = qa_ref[:, LANES - early :]
-    r = jnp.dot(hh_ref[...], weight[:, : 2 * LANES], preferred_element_type=jnp.float32)
-    q_ref[:, early:] = r[:, :late].astype(jnp.bfloat16)
-    u_ref[...] = jnp.dot(signs_ref[...], weight[:, LANES:], preferred_element_type=jnp.float32)
-
-
-def thirds(total):
-    high = total.astype(jnp.bfloat16).astype(jnp.float32)
-    middle = (total - high).astype(jnp.bfloat16).astype(jnp.float32)
-    low = total - high - middle
-    at = lax.broadcasted_iota(jnp.int32, (16, total.shape[1]), 0)
-    rest = jnp.where(at == 1, middle, jnp.where(at == 2, low, 0.0))
-    return jnp.where(at == 0, high, rest).astype(jnp.bfloat16)
+        a, b = part * block, (part + 1) * block
+        made = r[a:b, :both].astype(jnp.bfloat16)
+        kv_ref[:, part * both : (part + 1) * both] = made
+        head_ref[:, part * both : (part + 1) * both] = made[:rows]
+        tail_ref[:, part * both : (part + 1) * both] = made[rows:]
+        q_ref[a:b, :] = r[a:b, both : both + q_width].astype(jnp.bfloat16)
+    u_ref[...] = u
 
 
 def attend_kernel(
     rows, core_ref, q_ref, far_before, before, here, after, far_after, segq_ref, segk_ref, u_ref, w_any,
-    mine_ref, theirs_ref, share_ref, window, weight, o_ext, w_sem,
+    mine_ref, theirs_ref, share_ref, window, o_ext, weight, w_sem,
 ):
     block = 2 * rows
     reach = (2 * SPAN + 1) * rows
     q_width = GROUP * HEAD_DIM
     o_width = weight.shape[1]
-    shift = o_width - q_width
     fetch = pltpu.make_async_copy(w_any.at[:, pl.ds(w_any.shape[1] - o_width, o_width)], weight, w_sem)
     fetch.start()
+    shift = o_width - q_width
     window[0:rows] = far_before[...]
     window[rows : rows + block] = before[...]
     window[rows + block : rows + 2 * block] = here[...]
@@ -193,33 +194,17 @@
         hit = segq_ref[lo : lo + rows, :] == numbers
         share += jnp.sum(jnp.where(hit, terms, 0.0), axis=0, keepdims=True)
     share_ref[...] = share
-    width = weight.shape[0]
-    theirs_ref[rows:, :images] = thirds(share)
-    theirs_ref[rows:, images:] = jnp.zeros((theirs_ref.shape[0] - rows, width - images), jnp.bfloat16)
-    fetch.wait()
-    step = width // 6
     core = core_ref[0]
     own = o_ext[pl.ds(pl.multiple_of(core * rows, rows), rows), :]
     other = o_ext[pl.ds(pl.multiple_of((1 - core) * rows, rows), rows), :]
-    for part in range(6):
+    both = jnp.concatenate([other, own], axis=0)
+    fetch.wait()
+    step = weight.shape[0] // 4
+    for part in range(4):
         a, b = part * step, (part + 1) * step
-        theirs_ref[:rows, a:b] = lax.dot_general(
-            other, weight[a:b, :], NT, preferred_element_type=jnp.float32
-        ).astype(jnp.bfloat16)
-        mine_ref[:, a:b] = lax.dot_general(own, weight[a:b, :], NT, preferred_element_type=jnp.float32)
-
-
-def join_kernel(mine_ref, share_ref, theirs_ref, out_ref):
-    rows = mine_ref.shape[0]
-    images = share_ref.shape[1]
-    extra, quarter = out_ref.shape[1] - rows, out_ref.shape[2]
-    got = theirs_ref[rows:, :images].astype(jnp.float32)
-    share = thirds(share_ref[...] + jnp.sum(got, axis=0, keepdims=True))
-    for x in range(out_ref.shape[0]):
-        a, b = x * quarter, (x + 1) * quarter
-        out_ref[x, :rows, :] = (mine_ref[:, a:b] + theirs_ref[:rows, a:b].astype(jnp.float32)).astype(jnp.bfloat16)
-        out_ref[x, rows:, :images] = share
-        out_ref[x, rows:, images:] = jnp.zeros((extra, quarter - images), jnp.bfloat16)
+        r = lax.dot_general(weight[a:b, :], both, NT, preferred_element_type=jnp.float32)
+        theirs_ref[a:b, :] = r[:, :rows].astype(jnp.bfloat16)
+        mine_ref[a:b, :] = r[:, rows:]
 
 
 def body(owned_rows, arrival, image_lengths, probe_seeds, in_gain, w_q, w_kv, w_out):
@@ -241,11 +226,11 @@
     pieces = pl.pallas_call(
         functools.partial(pack_kernel, depth),
         out_shape=jax.ShapeDtypeStruct((2 * n_z, tall_rows, LANES), bf16),
-        in_specs=[VMEM] * 3,
+        in_specs=[VMEM],
         out_specs=VMEM,
         scratch_shapes=[pltpu.VMEM((depth, columns), f32), pltpu.VMEM((tall_rows, LANES), f32)],
-        compiler_params=params(16),
-    )(w_q, w_kv.reshape(depth, -1), w_out.T)
+        compiler_params=params(50),
+    )(jnp.concatenate([w_q, w_kv[:, 0], w_kv[:, 1], w_out.T], axis=1))
     strip = lax.all_to_all(pieces, ("z", "c"), split_axis=0, concat_axis=0, tiled=True)
     strip = pl.pallas_call(
         functools.partial(unpack_kernel, depth),
@@ -253,7 +238,7 @@
         in_specs=[VMEM],
         out_specs=VMEM,
         scratch_shapes=[pltpu.VMEM((tall_rows, LANES), f32), pltpu.VMEM((2 * n_z * depth, columns), f32)],
-        compiler_params=params(16),
+        compiler_params=params(50),
     )(strip)
     weights = lax.all_gather(strip, "y", axis=0, tiled=True)
 
@@ -262,7 +247,7 @@
     part = jnp.pad(part, ((0, 0), (0, padded - quarter))).reshape(rows, 1, padded)
     part, strip = lax.optimization_barrier((part, strip))
     arrived = lax.all_to_all(part, SEQ, split_axis=0, concat_axis=0, tiled=True)
-    arrived = jnp.take(arrived.reshape(rows, padded)[:, :quarter], arrival[0], axis=0)
+    arrived = jnp.take(arrived.reshape(rows, padded), arrival[0], axis=0, mode="clip")
     own = lax.all_gather(arrived, "x", axis=0, tiled=True)
     other = lax.ppermute(own, "c", [(0, 1), (1, 0)])
 
@@ -285,66 +270,56 @@
         in_specs=[SMEM] + [VMEM] * 4,
         out_specs=VMEM,
         scratch_shapes=[pltpu.VMEM((rows, width), f32)],
-        compiler_params=params(24),
+        compiler_params=params(50),
     )(core_word, own, other, signs, in_gain[None, :])
 
-    kv, q_early = pl.pallas_call(
-        kv_kernel,
+    kv, head, tail, q, u = pl.pallas_call(
+        project_kernel,
         out_shape=(
             jax.ShapeDtypeStruct((block, 4 * HEAD_DIM), bf16),
-            jax.ShapeDtypeStruct((2 * block, LANES), bf16),
-        ),
-        in_specs=[VMEM, ANY],
-        out_specs=(VMEM, VMEM),
-        scratch_shapes=[pltpu.VMEM((width, 2 * LANES), bf16), pltpu.SemaphoreType.DMA],
-        compiler_params=params(24),
-        cost_estimate=pl.CostEstimate(flops=4 * block * width * 2 * LANES, bytes_accessed=4_000_000, transcendentals=0),
-    )(hh, weights)
-    neighbours = (moved(kv[rows:], 2), moved(kv, 1), kv, moved(kv, -1), moved(kv[:rows], -2))
-    q, u = pl.pallas_call(
-        q_kernel,
-        out_shape=(
+            jax.ShapeDtypeStruct((rows, 4 * HEAD_DIM), bf16),
+            jax.ShapeDtypeStruct((rows, 4 * HEAD_DIM), bf16),
             jax.ShapeDtypeStruct((2 * block, q_width), bf16),
             jax.ShapeDtypeStruct((block, 3 * LANES), f32),
         ),
-        in_specs=[VMEM, VMEM, VMEM, ANY],
-        out_specs=(VMEM, VMEM),
-        scratch_shapes=[pltpu.VMEM((width, 4 * LANES), bf16), pltpu.SemaphoreType.DMA],
-        compiler_params=params(24),
-        cost_estimate=pl.CostEstimate(flops=6 * block * width * 3 * LANES, bytes_accessed=6_000_000, transcendentals=0),
-    )(hh, signs, q_early, weights)
+        in_specs=[ANY] * 3,
+        out_specs=(VMEM,) * 5,
+        scratch_shapes=[
+            pltpu.VMEM((3, 2 * block, width // 3), bf16),
+            pltpu.VMEM((3, block, width // 3), bf16),
+            pltpu.VMEM((3, width // 3, columns), bf16),
+            pltpu.SemaphoreType.DMA((3, 3)),
+        ],
+        compiler_params=params(50),
+        cost_estimate=pl.CostEstimate(flops=6 * block * width * columns, bytes_accessed=8_000_000, transcendentals=0),
+    )(hh, signs, weights)
+    neighbours = (moved(tail, 2), moved(kv, 1), kv, moved(kv, -1), moved(head, -2))
 
     mine, theirs, share = pl.pallas_call(
         functools.partial(attend_kernel, rows),
         out_shape=(
-            jax.ShapeDtypeStruct((rows, width), f32),
-            jax.ShapeDtypeStruct((rows + 16, width), bf16),
+            jax.ShapeDtypeStruct((width, rows), f32),
+            jax.ShapeDtypeStruct((width, rows), bf16),
             jax.ShapeDtypeStruct((1, images), f32),
         ),
         in_specs=[SMEM] + [VMEM] * 9 + [ANY],
         out_specs=(VMEM, VMEM, VMEM),
         scratch_shapes=[
             pltpu.VMEM((8 * rows, 4 * HEAD_DIM), bf16),
+            pltpu.VMEM((block, 3 * LANES), bf16),
             pltpu.VMEM((width, 3 * LANES), bf16),
-            pltpu.VMEM((block, 3 * LANES), bf16),
             pltpu.SemaphoreType.DMA,
         ],
-        compiler_params=params(40),
+        compiler_params=params(50),
         cost_estimate=pl.CostEstimate(flops=2_000_000_000, bytes_accessed=5_000_000, transcendentals=700_000),
     )(core_word, q, *neighbours, seg[:, None], segk[None, :], u, weights)
 
     theirs = lax.ppermute(theirs, "c", [(0, 1), (1, 0)])
-    group = pl.pallas_call(
-        join_kernel,
-        out_shape=jax.ShapeDtypeStruct((n_x, rows + 16, quarter), bf16),
-        in_specs=[VMEM] * 3,
-        out_specs=VMEM,
-        compiler_params=params(16),
-    )(mine, share, theirs)
-    groups = lax.all_to_all(group, "x", split_axis=0, concat_axis=0, tiled=True)
-    velocity = jnp.sum(groups[:, :rows].astype(f32), axis=0).astype(bf16)
-    share = jnp.sum(groups[:, rows:, :images].astype(f32), axis=(0, 1))
-    divergence = jnp.sum(spread(share, COLUMN), axis=0) / width
+    group = (mine + theirs.astype(f32)).astype(bf16)
+    velocity = lax.psum_scatter(group, "x", scatter_dimension=0, tiled=True).T
+    share, group = lax.optimization_barrier((share, group))
+    share = jnp.sum(spread(share[0], ("y", "c")), axis=0)
+    divergence = jnp.sum(spread(share, ("z", "x")), axis=0) / width
     return (velocity, divergence)
 
 

time: 170 us -> 164 us (0.965)
  blocking collectives: 55 us -> 70 us
  local copies, waits for them, and re-layouts: 13.7 us -> 4.8 us
  starting transfers between devices: 35.5 us -> 27.7 us
  waiting for transfers between devices: 34.6 us -> 27.9 us
  Pallas kernels: 11 us -> 14.8 us
    all_to_all x1 -> x2, blocking collectives: 14.7 us -> 29.6 us  [spread(): return lax.all_to_all(copies, axes, split_axis=0, concat_axis=0, tiled=True)]
    all_to_all x1 -> x0, waiting for transfers between devices: 10.2 us -> none  [spread(): return lax.all_to_all(copies, axes, split_axis=0, concat_axis=0, tiled=True)]
    all_to_all x1 -> x0, starting transfers between devices: 9.21 us -> none  [spread(): return lax.all_to_all(copies, axes, split_axis=0, concat_axis=0, tiled=True)]
    unnamed x32 -> x13, local copies, waits for them, and re-layouts: 8.94 us -> 1.19 us
    ppermute x4, waiting for transfers between devices: 7.16 us -> 9.47 us  [moved(): return lax.ppermute(array, COLUMN, pairs)]
    ppermute x4, starting transfers between devices: 9.02 us -> 11.1 us  [moved(): return lax.ppermute(array, COLUMN, pairs)]
    pallas_call x3 -> x1, Pallas kernels: 2.84 us -> 4.32 us  [body(): pl.pallas_call(project_kernel, out_shape=(jax.ShapeDtypeStruct((block, 4...]
  transfers between devices with their start and end apart: 9 -> 9, of which waited for: 4 -> 5; matrix products, arithmetic and copies ran while one was open for 6% -> 4% of each run, Pallas kernels for 2% -> 2%
where the time goes in v3:
time: 164 us
  blocking collectives  70 us (43%)
  waiting for transfers between devices  27.9 us (17%)
  starting transfers between devices  27.7 us (17%)
  Pallas kernels  14.8 us (9%)
  between operations  14.3 us (9%)
  local copies, waits for them, and re-layouts  4.8 us (3%)
  other arithmetic  4.52 us (3%)
    all_to_all x2, blocking collectives, spread(): return lax.all_to_all(copies, axes, split_axis=0, concat_axis=0, tiled=True)  29.6 us
    all_to_all x1, blocking collectives, body(): lax.all_to_all(pieces, ('z', 'c'), split_axis=0, concat_axis=0, tiled=True)  27.6 us
    all_to_all x1, waiting for transfers between devices, body(): arrived = lax.all_to_all(part, SEQ, split_axis=0, concat_axis=0, tiled=True)  15.4 us
    all_gather x1, blocking collectives, body(): own = lax.all_gather(arrived, 'x', axis=0, tiled=True)  12.8 us
    ppermute x4, starting transfers between devices, moved(): return lax.ppermute(array, COLUMN, pairs)  11.1 us
    ppermute x4, waiting for transfers between devices, moved(): return lax.ppermute(array, COLUMN, pairs)  9.47 us
    all_to_all x1, starting transfers between devices, body(): arrived = lax.all_to_all(part, SEQ, split_axis=0, concat_axis=0, tiled=True)  9.43 us
    pallas_call x1, Pallas kernels, body(): pl.pallas_call(functools.partial(attend_kernel, rows), out_shape=(jax.Sha...  6.39 us
  transfers between devices with their start and end apart: 9, of which 5 were waited for; matrix products, arithmetic and copies ran while one was open for 4% of the time, Pallas kernels for 2%

profile of v3, /device:TPU:1, one launch (start us, length us, event | category | flops | bytes accessed | tf_op | source)
XLA Modules:
  0.0 164.0 jit_solution(4128020681694747359)
XLA Ops:
  7.2 0.0 copy-start
  7.2 0.0 copy-start.2
  7.2 0.0 copy-start.1
  7.2 0.0 copy-start.3
  7.2 0.0 all-gather.3.cloned.1.call-start
  7.3 0.8 fusion.9
  8.1 0.9 concatenate.3.in_ref
  9.0 0.0 copy-start.4
  9.0 0.1 shard_map.95
  9.1 27.6 %all_to_all.22.in_ref = bf16[16,112,128]{2,1,0:T(8,128)(2,1)S(1)} all-to-all(bf16[16,112,128]{2,1,0:T(8,128)(2,1)S(1)} %shard_map.95), channel_id=1, replica_groups=mesh['y'=8,'z'=8,'c'=2,'x'=4] {'z','c'}, dimensions={0} | all-to-all | bytes 917504 | tf_op jit(solution)/shard_map/all_to_all | solution.py:234
  36.7 1.0 shard_map.96
  37.7 0.0 all-gather.3.cloned.1.call-update
  37.7 0.0 copy-done.2
  37.7 0.3 reduce-window.9
  38.1 0.1 slice.15
  38.2 0.0 copy-done.1
  38.2 0.1 slice_reduce_fusion
  38.3 0.1 fusion.8
  38.4 0.2 convert_reduce_fusion.1
  38.6 0.0 copy-done
  38.6 0.1 constant_dynamic-slice_fusion
  38.7 0.0 copy-done.3
  38.7 0.2 select_reduce_fusion.1
  39.0 0.4 convert_reduce_fusion
  39.3 0.5 broadcast.86
  39.9 0.7 reduce.4
  40.5 0.9 reshape.120
  41.4 9.4 %all-to-all-start.1 = ((bf16[128,2,320]{2,1,0:T(2,128)(2,1)}), bf16[128,2,320]{2,1,0:T(2,128)(2,1)S(1)}, u32[]{:S(2)}, u32[]{:S(2)}) async-start(bf16[128,2,320]{2,1,0:T(2,128)(2,1)} %reshape.120), calls=%async_computation.1 | async-start | bytes 393216 | tf_op jit(solution)/shard_map/all_to_all | solution.py:249
  50.9 0.0 reduce-scatter.2.cloned.1.call-start
  50.9 0.0 copy-done.4
  50.9 15.4 %all-to-all-done.1 = bf16[128,2,320]{2,1,0:T(2,128)(2,1)S(1)} async-done(((bf16[128,2,320]{2,1,0:T(2,128)(2,1)}), bf16[128,2,320]{2,1,0:T(2,128)(2,1)S(1)}, u32[]{:S(2)}, u32[]{:S(2)}) %all-to-all-start.1) | async-done | bytes 163872 | tf_op jit(solution)/shard_map/all_to_all | solution.py:249
  66.3 0.3 reshape.121
  66.6 0.9 gather_fusion
  67.5 12.8 %all-gather.own_ref = bf16[512,640]{1,0:T(8,128)(2,1)S(1)} all-gather(bf16[128,640]{1,0:T(8,128)(2,1)S(1)} %gather_fusion), channel_id=2, replica_groups=mesh['y'=8,'z'=8,'c'=2,'x'=4] {'x'}, dimensions={0}, use_global_device_ids=true | all-gather | bytes 819200 | tf_op jit(solution)/shard_map/all_gather | solution.py:251
  80.3 3.9 %collective-permute-start = (bf16[512,640]{1,0:T(8,128)(2,1)S(1)}, bf16[512,640]{1,0:T(8,128)(2,1)S(1)}, u32[]{:S(2)}, u32[]{:S(2)}) collective-permute-start(bf16[512,640]{1,0:T(8,128)(2,1)S(1)} %all-gather.own_ref), channel_id=1, source_target_pairs={{0,4},{4,0},{1,5},{5,1},{2,6},{6,2},{3,7},{7,3},{8,12},{12,8},{9,1... | collective-permute-start | bytes 1966088 | tf_op jit(solution)/shard_map/ppermute | solution.py:252
  84.2 1.0 fusion.7.signs_ref.signs_any
  85.2 0.7 collective-permute-done.other_ref
  85.9 2.9 %shard_map.97.hh_any = bf16[512,2304]{1,0:T(8,128)(2,1)} custom-call(s32[1]{0:T(128)} %bitcast.core_ref, bf16[512,640]{1,0:T(8,128)(2,1)S(1)} %all-gather.own_ref, bf16[512,640]{1,0:T(8,128)(2,1)S(1)} %collective-permute-done.other_ref, bf16[256,2304]{1,0:T(8,128)(2,1)S(1)} %fusion.7.signs_ref.signs_any, f32[1,2304]{1,0:T(1,128)S(1)} %broadcast_in_dim.59.gain_ref), custom_call_target="tpu_custom_call" | custom-call | tf_op jit(solution)/shard_map/pallas_call | solution.py:267
  88.8 0.8 all-gather.3.cloned.1.call-done.w_any
  89.6 4.3 %shard_map.98 = (bf16[256,384]{1,0:T(8,128)(2,1)S(1)}, bf16[128,384]{1,0:T(8,128)(2,1)S(1)}, bf16[128,384]{1,0:T(8,128)(2,1)S(1)}, bf16[512,288]{1,0:T(8,128)(2,1)S(1)}, f32[256,384]{1,0:T(8,128)S(1)}) custom-call(bf16[512,2304]{1,0:T(8,128)(2,1)} %shard_map.97.hh_any, bf16[256,2304]{1,0:T(8,128)(2,1)S(1)} %fusion.7.signs_ref.signs_any, ...), custom_call_target="tpu_custom_call" | custom-call | flops 2717908992 | bytes 8000000 | tf_op jit(solution)/shard_map/pallas_call | solution.py:276
  93.9 3.3 %collective-permute-start.2 = (bf16[256,384]{1,0:T(8,128)(2,1)S(1)}, bf16[256,384]{1,0:T(8,128)(2,1)S(1)}, u32[]{:S(2)}, u32[]{:S(2)}) collective-permute-start(bf16[256,384]{1,0:T(8,128)(2,1)S(1)} %get-tuple-element.15.here), channel_id=1, source_target_pairs={{0,8},{8,16},{16,24},{24,32},{32,40},{40,48},{48,56},{56,64},{64,7... | collective-permute-start | bytes 589832 | tf_op jit(solution)/shard_map/ppermute | solution.py:44
  97.2 1.3 collective-permute-start.3
  98.5 5.1 %collective-permute-start.1 = (bf16[128,384]{1,0:T(8,128)(2,1)S(1)}, bf16[128,384]{1,0:T(8,128)(2,1)S(1)}, u32[]{:S(2)}, u32[]{:S(2)}) collective-permute-start(bf16[128,384]{1,0:T(8,128)(2,1)S(1)} %get-tuple-element.14), channel_id=1, source_target_pairs={{0,16},{8,24},{16,32},{24,40},{32,48},{40,56},{48,64},{56,72},{64,... | collective-permute-start | bytes 294920 | tf_op jit(solution)/shard_map/ppermute | solution.py:44
  103.6 1.5 collective-permute-start.4
  105.1 0.1 copy.29.segq_ref
  105.2 0.0 collective-permute-done.1.far_before
  105.2 9.5 %collective-permute-done.4.far_after = bf16[128,384]{1,0:T(8,128)(2,1)S(1)} collective-permute-done((bf16[128,384]{1,0:T(8,128)(2,1)S(1)}, bf16[128,384]{1,0:T(8,128)(2,1)S(1)}, u32[]{:S(2)}, u32[]{:S(2)}) %collective-permute-start.4) | collective-permute-done | bytes 98336 | tf_op jit(solution)/shard_map/ppermute | solution.py:44
  114.7 0.0 collective-permute-done.2.before
  114.7 0.0 collective-permute-done.3.after
  114.7 6.4 %shard_map.99 = (f32[2304,128]{1,0:T(8,128)S(1)}, bf16[2304,128]{1,0:T(8,128)(2,1)S(1)}, f32[1,256]{1,0:T(1,128)S(1)}) custom-call(s32[1]{0:T(128)} %bitcast.core_ref, bf16[512,288]{1,0:T(8,128)(2,1)S(1)} %get-tuple-element.13.q_ref, bf16[128,384]{1,0:T(8,128)(2,1)S(1)} %collective-permute-done.1.far_before, ...), custom_call_target="tpu_custom_call" | custom-call | flops 2000000000 | bytes 5000000 | tf_op jit(solution)/shard_map/pallas_call | solution.py:298
  121.1 3.1 %collective-permute-start.5 = (bf16[2304,128]{1,0:T(8,128)(2,1)S(1)}, bf16[2304,128]{1,0:T(8,128)(2,1)S(1)}, u32[]{:S(2)}, u32[]{:S(2)}) collective-permute-start(bf16[2304,128]{1,0:T(8,128)(2,1)S(1)} %get-tuple-element.19), channel_id=1, source_target_pairs={{0,4},{4,0},{1,5},{5,1},{2,6},{6,2},{3,7},{7,3},{8,12},{12,8},{9,1... | collective-permute-start | bytes 1769480 | tf_op jit(solution)/shard_map/ppermute | solution.py:317
  124.2 1.6 collective-permute-done.5
  125.8 0.9 add_convert_fusion
  126.8 0.0 reduce-scatter.2.cloned.1.call-update
  126.8 12.8 %all_to_all.23 = f32[16,1,256]{2,1,0:T(1,128)S(1)} all-to-all(f32[16,1,256]{2,1,0:T(1,128)S(1)} %broadcast_in_dim.62), channel_id=1, replica_groups=mesh['y'=8,'z'=8,'c'=2,'x'=4] {'y','c'}, dimensions={0} | all-to-all | bytes 32768 | tf_op jit(solution)/shard_map/all_to_all | solution.py:38
  139.7 16.8 %all_to_all.24 = f32[32,1,256]{2,1,0:T(1,128)S(1)} all-to-all(f32[32,1,256]{2,1,0:T(1,128)S(1)} %broadcast_in_dim.63), channel_id=1, replica_groups=mesh['y'=8,'z'=8,'c'=2,'x'=4] {'z','x'}, dimensions={0} | all-to-all | bytes 65536 | tf_op jit(solution)/shard_map/all_to_all | solution.py:38
  156.5 0.1 reduce_sum.62
  156.6 0.6 broadcast_multiply_fusion
  157.1 0.0 reduce-scatter.2.cloned.1.call-done
  (13 shorter events, 0.2 us)
Async XLA Ops:
  7.2 31.4 %copy-start = (bf16[128,2304]{1,0:T(8,128)(2,1)S(1)}, bf16[128,2304]{1,0:T(8,128)(2,1)}, u32[]{:S(2)}) copy-start(bf16[128,2304]{1,0:T(8,128)(2,1)} %param.8) | copy-start | bytes 1769476
  7.2 30.6 %copy-start.2 = (s32[256]{0:T(256)S(1)}, s32[256]{0:T(256)}, u32[]{:S(2)}) copy-start(s32[256]{0:T(256)} %param.10) | copy-start | bytes 3076
  7.2 31.0 %copy-start.1 = (f32[2304]{0:T(1024)S(1)}, f32[2304]{0:T(1024)}, u32[]{:S(2)}) copy-start(f32[2304]{0:T(1024)} %param.12) | copy-start | bytes 27652
  7.2 31.5 %copy-start.3 = (s32[256]{0:T(256)S(1)}, s32[256]{0:T(256)}, u32[]{:S(2)}) copy-start(s32[256]{0:T(256)} %param.11) | copy-start | bytes 3076
  7.2 82.4 %all-gather.3.cloned.1.call-start = ((), (), s32[]{:S(2)}) async-start(), calls=%async_computation.5 | async-start | bytes 3981312 | tf_op jit(solution)/shard_map/all_gather | solution.py:243
  9.0 41.9 %copy-start.4 = (s32[1,128]{1,0:T(1,128)S(1)}, s32[1,128]{1,0:T(1,128)}, u32[]{:S(2)}) copy-start(s32[1,128]{1,0:T(1,128)} %param.9) | copy-start | bytes 1540
  41.4 24.9 %all-to-all-start.1 = ((bf16[128,2,320]{2,1,0:T(2,128)(2,1)}), bf16[128,2,320]{2,1,0:T(2,128)(2,1)S(1)}, u32[]{:S(2)}, u32[]{:S(2)}) async-start(bf16[128,2,320]{2,1,0:T(2,128)(2,1)} %reshape.120), calls=%async_computation.1 | async-start | bytes 393216 | tf_op jit(solution)/shard_map/all_to_all | solution.py:249
  50.9 106.3 %reduce-scatter.2.cloned.1.call-start = ((), (), s32[]{:S(2)}) async-start(), calls=%async_computation.6 | async-start | bytes 737280 | tf_op jit(solution)/shard_map/reduce_scatter | solution.py:319
  80.3 5.6 %collective-permute-start = (bf16[512,640]{1,0:T(8,128)(2,1)S(1)}, bf16[512,640]{1,0:T(8,128)(2,1)S(1)}, u32[]{:S(2)}, u32[]{:S(2)}) collective-permute-start(bf16[512,640]{1,0:T(8,128)(2,1)S(1)} %all-gather.own_ref), channel_id=1, source_target_pairs={{0,4},{4,0},{1,5},{5,1},{2,6},{6,2},{3,7},{7,3},{8,12},{12,8},{9,1... | collective-permute-start | bytes 1966088 | tf_op jit(solution)/shard_map/ppermute | solution.py:252
  93.9 20.8 %collective-permute-start.2 = (bf16[256,384]{1,0:T(8,128)(2,1)S(1)}, bf16[256,384]{1,0:T(8,128)(2,1)S(1)}, u32[]{:S(2)}, u32[]{:S(2)}) collective-permute-start(bf16[256,384]{1,0:T(8,128)(2,1)S(1)} %get-tuple-element.15.here), channel_id=1, source_target_pairs={{0,8},{8,16},{16,24},{24,32},{32,40},{40,48},{48,56},{56,64},{64,7... | collective-permute-start | bytes 589832 | tf_op jit(solution)/shard_map/ppermute | solution.py:44
  97.2 17.5 %collective-permute-start.3 = (bf16[256,384]{1,0:T(8,128)(2,1)S(1)}, bf16[256,384]{1,0:T(8,128)(2,1)S(1)}, u32[]{:S(2)}, u32[]{:S(2)}) collective-permute-start(bf16[256,384]{1,0:T(8,128)(2,1)S(1)} %get-tuple-element.15.here), channel_id=1, source_target_pairs={{8,0},{16,8},{24,16},{32,24},{40,32},{48,40},{56,48},{64,56},{72,6... | collective-permute-start | bytes 589832 | tf_op jit(solution)/shard_map/ppermute | solution.py:44
  98.5 6.7 %collective-permute-start.1 = (bf16[128,384]{1,0:T(8,128)(2,1)S(1)}, bf16[128,384]{1,0:T(8,128)(2,1)S(1)}, u32[]{:S(2)}, u32[]{:S(2)}) collective-permute-start(bf16[128,384]{1,0:T(8,128)(2,1)S(1)} %get-tuple-element.14), channel_id=1, source_target_pairs={{0,16},{8,24},{16,32},{24,40},{32,48},{40,56},{48,64},{56,72},{64,... | collective-permute-start | bytes 294920 | tf_op jit(solution)/shard_map/ppermute | solution.py:44
  103.6 11.1 %collective-permute-start.4 = (bf16[128,384]{1,0:T(8,128)(2,1)S(1)}, bf16[128,384]{1,0:T(8,128)(2,1)S(1)}, u32[]{:S(2)}, u32[]{:S(2)}) collective-permute-start(bf16[128,384]{1,0:T(8,128)(2,1)S(1)} %get-tuple-element.16), channel_id=1, source_target_pairs={{16,0},{24,8},{32,16},{40,24},{48,32},{56,40},{64,48},{72,56},{80,... | collective-permute-start | bytes 294920 | tf_op jit(solution)/shard_map/ppermute | solution.py:44
  121.1 4.8 %collective-permute-start.5 = (bf16[2304,128]{1,0:T(8,128)(2,1)S(1)}, bf16[2304,128]{1,0:T(8,128)(2,1)S(1)}, u32[]{:S(2)}, u32[]{:S(2)}) collective-permute-start(bf16[2304,128]{1,0:T(8,128)(2,1)S(1)} %get-tuple-element.19), channel_id=1, source_target_pairs={{0,4},{4,0},{1,5},{5,1},{2,6},{6,2},{3,7},{7,3},{8,12},{12,8},{9,1... | collective-permute-start | bytes 1769480 | tf_op jit(solution)/shard_map/ppermute | solution.py:317
Sparse Core Ops, SparseCore 0:
  37.8 51.6 all-gather.2
  126.9 23.1 reduce-scatter.1

commit v4 on v3

v4 whole, which is shorter than its diff:
```python
import functools

import jax
import jax.numpy as jnp
from jax import lax
from jax.experimental import pallas as pl
from jax.experimental.pallas import tpu as pltpu
from jax.sharding import Mesh
from jax.sharding import PartitionSpec as P

HEADS = 24
KV_HEADS = 8
HEAD_DIM = 96
GROUP = HEADS // KV_HEADS
SPAN = 3
SEQ = ("y", "z", "c")
COLUMN = ("y", "z")


def segment_of(pos, ends):
    return jnp.sum((ends[None, :] <= pos[:, None]).astype(jnp.int32), axis=1, dtype=jnp.int32)


def probe_signs(seed_row, local_row, columns):
    mixed = seed_row[:, None] * 40503 + local_row[:, None] * 69069 + columns[None, :] * 2654435
    mixed = mixed ^ jnp.right_shift(mixed, 15)
    mixed = mixed * 1597334677
    mixed = mixed ^ jnp.right_shift(mixed, 13)
    mixed = mixed * 668265263
    bit = jnp.right_shift(mixed, 11) & 1
    return (1 - 2 * bit).astype(jnp.float32)


def spread(array, axes):
    count = lax.axis_size(axes)
    copies = jnp.broadcast_to(array[None], (count,) + array.shape)
    return lax.all_to_all(copies, axes, split_axis=0, concat_axis=0, tiled=True)


def moved(array, by):
    count = lax.axis_size(COLUMN)
    pairs = [(i, i + by) for i in range(count) if 0 <= i + by < count]
    return lax.ppermute(array, COLUMN, pairs)


NT = (((1,), (1,)), ((), ()))
VMEM = pl.BlockSpec(memory_space=pltpu.VMEM)
SMEM = pl.BlockSpec(memory_space=pltpu.SMEM)
ANY = pl.BlockSpec(memory_space=pl.ANY)
LANES = 128


def params(mib):
    return pltpu.CompilerParams(vmem_limit_bytes=mib * 1024 * 1024)


def pack_kernel(depth, core_ref, in_ref, own_ref, other_ref, wide, tall):
    q_width = GROUP * HEAD_DIM
    tiles = wide.shape[1] // LANES
    k_first = 2 * q_width
    v_first = k_first + 2 * HEAD_DIM
    o_first = v_first + 2 * HEAD_DIM
    held = in_ref[...].astype(jnp.float32)
    tall[...] = jnp.zeros_like(tall)
    for core in range(2):
        k, q = core * HEAD_DIM, core * q_width
        wide[:, :HEAD_DIM] = held[:, k_first + k : k_first + k + HEAD_DIM]
        wide[:, HEAD_DIM : 2 * HEAD_DIM] = held[:, v_first + k : v_first + k + HEAD_DIM]
        wide[:, 2 * HEAD_DIM : 2 * HEAD_DIM + q_width] = held[:, q : q + q_width]
        wide[:, 2 * HEAD_DIM + q_width :] = held[:, o_first + q : o_first + q + q_width]
        for tile in range(tiles):
            tall[tile * depth : (tile + 1) * depth, :] = wide[:, tile * LANES : (tile + 1) * LANES]
        piece = tall[...].astype(jnp.bfloat16)

        @pl.when(core_ref[0] == core)
        def _(piece=piece):
            own_ref[...] = piece

        @pl.when(core_ref[0] != core)
        def _(piece=piece):
            other_ref[...] = piece


def copies_kernel(core_ref, own_ref, other_ref, out_ref):
    @pl.when(core_ref[0] == 0)
    def _():
        for to in range(out_ref.shape[0]):
            out_ref[to, 0] = own_ref[...]
            out_ref[to, 1] = other_ref[...]

    @pl.when(core_ref[0] != 0)
    def _():
        for to in range(out_ref.shape[0]):
            out_ref[to, 0] = other_ref[...]
            out_ref[to, 1] = own_ref[...]


def unpack_kernel(depth, in_ref, out_ref, tall, wide):
    for source in range(in_ref.shape[0]):
        tall[...] = in_ref[source].astype(jnp.float32)
        for tile in range(out_ref.shape[1] // LANES):
            wide[source * depth : (source + 1) * depth, tile * LANES : (tile + 1) * LANES] = tall[
                tile * depth : (tile + 1) * depth, :
            ]
    out_ref[...] = wide[...].astype(jnp.bfloat16)


def project_kernel(
    side, unit, core_ref, own_ref, other_ref, signs_ref, gain_ref, w_any,
    kv_ref, qu_ref, wide, hh, weight, sem,
):
    rows, width = wide.shape
    block = 2 * rows
    members = own_ref.shape[0] // rows
    quarter = width // members
    fetch = pltpu.make_async_copy(w_any, weight, sem)
    fetch.start()
    gain = gain_ref[...]
    for half in range(2):
        mine = core_ref[0] == half
        for x in range(members):
            a, b = x * rows, (x + 1) * rows
            held = jnp.where(mine, own_ref[a:b, :].astype(jnp.float32), other_ref[a:b, :].astype(jnp.float32))

            @pl.when(core_ref[0] == 0)
            def _(x=x, held=held):
                wide[:, x * quarter : (x + 1) * quarter] = held[:, :quarter]

            @pl.when(core_ref[0] != 0)
            def _(x=x, held=held):
                for i in range(quarter // unit):
                    y, z = divmod(x * quarter // unit + i, side)
                    to = (z * side + y) * unit
                    wide[:, to : to + unit] = held[:, i * unit : (i + 1) * unit]

        x = wide[...]
        signs = signs_ref[half * rows : (half + 1) * rows, :].astype(jnp.float32)
        inv = lax.rsqrt(jnp.sum(x * x, axis=1, keepdims=True) / width + 1e-06)
        along = jnp.sum(x * signs, axis=1, keepdims=True) / width
        hh[half * rows : (half + 1) * rows, :] = (x * inv * gain).astype(jnp.bfloat16)
        hh[(2 + half) * rows : (3 + half) * rows, :] = (
            (signs * inv - x * (inv * inv * inv * along)) * gain
        ).astype(jnp.bfloat16)
    fetch.wait()
    both = 2 * HEAD_DIM
    q_width = GROUP * HEAD_DIM
    for part in range(2):
        a, b = part * block, (part + 1) * block
        r = jnp.dot(hh[a:b, :], weight[:, : 4 * LANES], preferred_element_type=jnp.float32)
        at = part * HEAD_DIM
        kv_ref[:, at : at + HEAD_DIM] = r[:, :HEAD_DIM].astype(jnp.bfloat16)
        kv_ref[:, both + at : both + at + HEAD_DIM] = r[:, HEAD_DIM:both].astype(jnp.bfloat16)
        qu_ref[a:b, :q_width] = r[:, both : both + q_width].astype(jnp.bfloat16)
    u = jnp.dot(signs_ref[...], weight[:, 3 * LANES :], preferred_element_type=jnp.float32)
    qu_ref[2 * block :, :] = u.astype(jnp.bfloat16)


def attend_kernel(
    rows, side, core_ref, qu_ref, far_before, before, here, after, far_after, segq_ref, segk_ref, w_any,
    mine_ref, theirs_ref, share_ref, window, o_ext, weight, flat, w_sem,
):
    block = 2 * rows
    reach = (2 * SPAN + 1) * rows
    q_width = GROUP * HEAD_DIM
    o_width = weight.shape[1]
    fetch = pltpu.make_async_copy(w_any.at[:, pl.ds(w_any.shape[1] - o_width, o_width)], weight, w_sem)
    fetch.start()
    shift = o_width - q_width
    window[0:rows] = far_before[...]
    window[rows : rows + block] = before[...]
    window[rows + block : rows + 2 * block] = here[...]
    window[rows + 2 * block : rows + 3 * block] = after[...]
    window[rows + 3 * block : 2 * rows + 3 * block] = far_after[...]
    scale = 1.0 / HEAD_DIM**0.5
    to_exp2 = scale * 1.4426950408889634
    o_ext[:, :shift] = jnp.zeros((block, shift), jnp.bfloat16)
    images = share_ref.shape[1]
    share = jnp.zeros((1, images), jnp.float32)
    both = 2 * HEAD_DIM
    for tile in range(2):
        lo = tile * rows
        keys = window[lo : lo + reach, :both]
        values = window[lo : lo + reach, both:]

        def heads(first):
            parts = [
                qu_ref[first + lo : first + lo + rows, h * HEAD_DIM : (h + 1) * HEAD_DIM] for h in range(GROUP)
            ]
            return jnp.concatenate(parts, axis=0)

        q, q_t = heads(0), heads(block)
        segq = segq_ref[lo : lo + rows, :]
        mask = jnp.concatenate([segq] * GROUP, axis=0) == segk_ref[:, lo : lo + reach]
        s = lax.dot_general(q, keys[:, :HEAD_DIM], NT, preferred_element_type=jnp.float32)
        s_t = lax.dot_general(
            jnp.concatenate([q_t, q], axis=1), keys, NT, preferred_element_type=jnp.float32
        )
        s = jnp.where(mask, s, -1e30)
        e = jnp.exp2((s - jnp.max(s, axis=1, keepdims=True)) * to_exp2)
        inv = 1.0 / jnp.sum(e, axis=1, keepdims=True)
        mean = jnp.sum(e * s_t, axis=1, keepdims=True) * inv
        e_t = (e * ((s_t - mean) * scale)).astype(jnp.bfloat16)
        e = e.astype(jnp.bfloat16)
        made = jnp.dot(e, values, preferred_element_type=jnp.float32)
        out = (made[:, :HEAD_DIM] * inv).astype(jnp.bfloat16)
        out_t = jnp.dot(e_t, values[:, :HEAD_DIM], preferred_element_type=jnp.float32) + made[:, HEAD_DIM:]
        out_t = (out_t * inv).astype(jnp.bfloat16).astype(jnp.float32)
        terms = jnp.zeros((rows, 1), jnp.float32)
        for head in range(GROUP):
            a, b = shift + head * HEAD_DIM, shift + (head + 1) * HEAD_DIM
            at = head * rows
            u = qu_ref[2 * block + lo : 2 * block + lo + rows, a:b].astype(jnp.float32)
            o_ext[lo : lo + rows, a:b] = out[at : at + rows]
            terms += jnp.sum(out_t[at : at + rows] * u, axis=1, keepdims=True)
        numbers = lax.broadcasted_iota(jnp.int32, (rows, images), 1)
        share += jnp.sum(jnp.where(segq == numbers, terms, 0.0), axis=0, keepdims=True)
    share_ref[...] = share
    core = core_ref[0]
    own = o_ext[pl.ds(pl.multiple_of(core * rows, rows), rows), :]
    other = o_ext[pl.ds(pl.multiple_of((1 - core) * rows, rows), rows), :]
    both = jnp.concatenate([other, own], axis=0)
    fetch.wait()
    width = weight.shape[0]
    step, unit = width // 4, width // side**2
    for part in range(4):
        a, b = part * step, (part + 1) * step
        r = lax.dot_general(weight[a:b, :], both, NT, preferred_element_type=jnp.float32)

        @pl.when(core == 0)
        def _(a=a, b=b, r=r):
            theirs_ref[a:b, :] = r[:, :rows].astype(jnp.bfloat16)
            mine_ref[a:b, :] = r[:, rows:]

        @pl.when(core != 0)
        def _(a=a, r=r):
            for i in range(step // unit):
                z, y = divmod(a // unit + i, side)
                to = (y * side + z) * unit
                flat[to : to + unit, :] = r[i * unit : (i + 1) * unit, :rows]
                mine_ref[to : to + unit, :] = r[i * unit : (i + 1) * unit, rows:]

    @pl.when(core != 0)
    def _():
        theirs_ref[...] = flat[...].astype(jnp.bfloat16)


def body(owned_rows, arrival, image_lengths, probe_seeds, in_gain, w_q, w_kv, w_out):
    bf16, f32 = jnp.bfloat16, jnp.float32
    rows, width = owned_rows.shape
    n_x, n_z, n_seq = lax.axis_size("x"), lax.axis_size("z"), lax.axis_size(SEQ)
    core, member = lax.axis_index("c"), lax.axis_index("x")
    core_word = jnp.reshape(core, (1,)).astype(jnp.int32)
    n_block = lax.axis_size(COLUMN)
    block_index = lax.axis_index(COLUMN)
    quarter = width // n_x
    depth = w_q.shape[0]
    block = 2 * rows
    images = image_lengths.shape[0]
    q_width = GROUP * HEAD_DIM
    columns = 2 * HEAD_DIM + 2 * q_width

    tall_rows = -(-depth * (columns // LANES) // 16) * 16
    piece = jax.ShapeDtypeStruct((tall_rows, LANES), bf16)
    own_piece, other_piece = pl.pallas_call(
        functools.partial(pack_kernel, depth),
        out_shape=(piece, piece),
        in_specs=[SMEM, VMEM],
        out_specs=(VMEM, VMEM),
        scratch_shapes=[pltpu.VMEM((depth, columns), f32), pltpu.VMEM((tall_rows, LANES), f32)],
        compiler_params=params(50),
    )(core_word, jnp.concatenate([w_q, w_kv[:, 0], w_kv[:, 1], w_out.T], axis=1))
    other_piece = lax.ppermute(other_piece, "c", [(0, 1), (1, 0)])
    pieces = pl.pallas_call(
        copies_kernel,
        out_shape=jax.ShapeDtypeStruct((n_z, 2, tall_rows, LANES), bf16),
        in_specs=[SMEM] + [VMEM] * 2,
        out_specs=VMEM,
        compiler_params=params(50),
    )(core_word, own_piece, other_piece)
    side = range(n_z)
    place = lambda y, z, c: (y * n_z + z) * 2 + c
    by_z = [[place(y, z, 0) for z in side] for y in side] + [[place(y, z, 1) for y in side] for z in side]
    by_y = [[place(y, z, 0) for y in side] for z in side] + [[place(y, z, 1) for z in side] for y in side]
    strip = lax.all_to_all(pieces, SEQ, split_axis=0, concat_axis=0, tiled=True, axis_index_groups=by_z)
    strip = strip.reshape(2 * n_z, tall_rows, LANES)
    strip = pl.pallas_call(
        functools.partial(unpack_kernel, depth),
        out_shape=jax.ShapeDtypeStruct((2 * n_z * depth, columns), bf16),
        in_specs=[VMEM],
        out_specs=VMEM,
        scratch_shapes=[pltpu.VMEM((tall_rows, LANES), f32), pltpu.VMEM((2 * n_z * depth, columns), f32)],
        compiler_params=params(50),
    )(strip)
    weights = lax.all_gather(strip, SEQ, axis=0, tiled=True, axis_index_groups=by_y)

    part = lax.dynamic_slice_in_dim(owned_rows, member * quarter, quarter, 1)
    padded = -(-quarter // LANES) * LANES
    part = jnp.pad(part, ((0, 0), (0, padded - quarter))).reshape(rows, 2, padded // 2)
    part, strip = lax.optimization_barrier((part, strip))
    arrived = lax.all_to_all(part, SEQ, split_axis=0, concat_axis=0, tiled=True)
    arrived = jnp.take(arrived.reshape(rows, padded), arrival[0], axis=0, mode="clip")
    own = lax.all_gather(arrived, "x", axis=0, tiled=True)
    own, image_lengths, probe_seeds = lax.optimization_barrier((own, image_lengths, probe_seeds))
    other = lax.ppermute(own, "c", [(0, 1), (1, 0)])

    ends = jnp.cumsum(image_lengths, dtype=jnp.int32)
    starts = ends - image_lengths
    first = block_index * block
    positions = first + jnp.arange(block, dtype=jnp.int32)
    seg = segment_of(positions, ends)
    onehot = seg[:, None] == jnp.arange(images, dtype=jnp.int32)[None, :]
    start_row = jnp.sum(jnp.where(onehot, starts[None, :], 0), axis=1, dtype=jnp.int32)
    seed_row = jnp.sum(jnp.where(onehot, probe_seeds[None, :], 0), axis=1, dtype=jnp.int32)
    unit = 2 * depth
    turned = lambda row: jnp.transpose(row.reshape(n_z, n_z, unit), (1, 0, 2)).reshape(width)
    numbers = jnp.arange(width, dtype=jnp.int32)
    numbers = jnp.where(core == 0, numbers, turned(numbers))
    gain = jnp.where(core == 0, in_gain, turned(in_gain))
    signs = probe_signs(seed_row, positions - start_row, numbers).astype(bf16)
    kpos = first - SPAN * rows + jnp.arange(block + 2 * SPAN * rows, dtype=jnp.int32)
    valid = (kpos >= 0) & (kpos < block * n_block)
    segk = jnp.where(valid, segment_of(kpos, ends), -1)

    kv, qu = pl.pallas_call(
        functools.partial(project_kernel, n_z, unit),
        out_shape=(
            jax.ShapeDtypeStruct((block, 4 * HEAD_DIM), bf16),
            jax.ShapeDtypeStruct((3 * block, 3 * LANES), bf16),
        ),
        in_specs=[SMEM] + [VMEM] * 4 + [ANY],
        out_specs=(VMEM,) * 2,
        scratch_shapes=[
            pltpu.VMEM((rows, width), f32),
            pltpu.VMEM((2 * block, width), bf16),
            pltpu.VMEM((width, columns), bf16),
            pltpu.SemaphoreType.DMA,
        ],
        compiler_params=params(50),
        cost_estimate=pl.CostEstimate(flops=6 * block * width * columns, bytes_accessed=8_000_000, transcendentals=0),
    )(core_word, own, other, signs, gain[None, :], weights)
    neighbours = (moved(kv[rows:], 2), moved(kv, 1), kv, moved(kv, -1), moved(kv[:rows], -2))

    mine, theirs, share = pl.pallas_call(
        functools.partial(attend_kernel, rows, n_z),
        out_shape=(
            jax.ShapeDtypeStruct((width, rows), f32),
            jax.ShapeDtypeStruct((width, rows), bf16),
            jax.ShapeDtypeStruct((1, images), f32),
        ),
        in_specs=[SMEM] + [VMEM] * 8 + [ANY],
        out_specs=(VMEM, VMEM, VMEM),
        scratch_shapes=[
            pltpu.VMEM((8 * rows, 4 * HEAD_DIM), bf16),
            pltpu.VMEM((block, 3 * LANES), bf16),
            pltpu.VMEM((width, 3 * LANES), bf16),
            pltpu.VMEM((width, rows), f32),
            pltpu.SemaphoreType.DMA,
        ],
        compiler_params=params(50),
        cost_estimate=pl.CostEstimate(flops=2_000_000_000, bytes_accessed=5_000_000, transcendentals=700_000),
    )(core_word, qu, *neighbours, seg[:, None], segk[None, :], weights)

    theirs = lax.ppermute(theirs, "c", [(0, 1), (1, 0)])
    group = (mine + theirs.astype(f32)).astype(bf16)
    velocity = lax.psum_scatter(group, "x", scatter_dimension=0, tiled=True).T
    share, group = lax.optimization_barrier((share, group))
    share = jnp.sum(spread(share[0], ("y", "c")), axis=0)
    divergence = jnp.sum(spread(share, ("z", "x")), axis=0) / width
    return (velocity, divergence)


def solution(mesh):
    n_seq, n_x = mesh.devices.shape
    n_y = 1
    while n_y * n_y * 2 < n_seq:
        n_y *= 2
    devices = mesh.devices.reshape(n_y, n_seq // 2 // n_y, 2, n_x)
    split = Mesh(devices, ("y", "z", "c", "x"))
    in_specs = (
        P(SEQ, None),
        P(SEQ, None),
        P(),
        P(),
        P(),
        P(SEQ, "x"),
        P(SEQ, None, "x"),
        P("x", SEQ),
    )
    out_specs = (P(SEQ, "x"), P())
    return jax.shard_map(body, mesh=split, in_specs=in_specs, out_specs=out_specs, check_vma=False)
```

time: 164 us -> 158 us (0.963)
  blocking collectives: 70 us -> 55.7 us
  starting transfers between devices: 27.7 us -> 41 us
  waiting for transfers between devices: 27.9 us -> 21.7 us
  local copies, waits for them, and re-layouts: 4.8 us -> 6.71 us
    all_to_all x1, blocking collectives: 27.6 us -> 13.8 us  [body(): lax.all_to_all(pieces, SEQ, split_axis=0, concat_axis=0, tiled=True, axis...]
    ppermute x0 -> x1, starting transfers between devices: none -> 8.78 us  [body(): other_piece = lax.ppermute(other_piece, 'c', [(0, 1), (1, 0)])]
    ppermute x4, waiting for transfers between devices: 9.47 us -> 5.31 us  [moved(): return lax.ppermute(array, COLUMN, pairs)]
    ppermute x1, starting transfers between devices: 3.13 us -> 6.29 us  [body(): theirs = lax.ppermute(theirs, 'c', [(0, 1), (1, 0)])]
    all_to_all x1, starting transfers between devices: 9.43 us -> 12.3 us  [body(): arrived = lax.all_to_all(part, SEQ, split_axis=0, concat_axis=0, tiled=True)]
    ppermute x4, starting transfers between devices: 11.1 us -> 8.73 us  [moved(): return lax.ppermute(array, COLUMN, pairs)]
  transfers between devices with their start and end apart: 9 -> 10, of which waited for: 5 -> 5; matrix products, arithmetic and copies ran while one was open for 4% -> 4% of each run, Pallas kernels for 2% -> 0%
where the time goes in v4:
time: 158 us; the launch traced here: 157 us
  blocking collectives  55.7 us (35%)
  starting transfers between devices  41 us (26%)
  waiting for transfers between devices  21.7 us (14%)
  between operations  14.4 us (9%)
  Pallas kernels  13.8 us (9%)
  local copies, waits for them, and re-layouts  6.71 us (4%)
  other arithmetic  3.86 us (2%)
    all_to_all x2, blocking collectives, spread(): return lax.all_to_all(copies, axes, split_axis=0, concat_axis=0, tiled=True)  29.5 us
    all_to_all x1, waiting for transfers between devices, body(): arrived = lax.all_to_all(part, SEQ, split_axis=0, concat_axis=0, tiled=True)  13.9 us
    all_to_all x1, blocking collectives, body(): lax.all_to_all(pieces, SEQ, split_axis=0, concat_axis=0, tiled=True, axis...  13.8 us
    all_gather x1, blocking collectives, body(): own = lax.all_gather(arrived, 'x', axis=0, tiled=True)  12.4 us
    all_to_all x1, starting transfers between devices, body(): arrived = lax.all_to_all(part, SEQ, split_axis=0, concat_axis=0, tiled=True)  12.3 us
    ppermute x1, starting transfers between devices, body(): other_piece = lax.ppermute(other_piece, 'c', [(0, 1), (1, 0)])  8.78 us
    ppermute x4, starting transfers between devices, moved(): return lax.ppermute(array, COLUMN, pairs)  8.73 us
    pallas_call x1, Pallas kernels, body(): pl.pallas_call(functools.partial(attend_kernel, rows, n_z), out_shape=(ja...  6.78 us
  transfers between devices with their start and end apart: 10, of which 5 were waited for; matrix products, arithmetic and copies ran while one was open for 4% of the time, Pallas kernels for 0%

profile of v4, /device:TPU:1, one launch (start us, length us, event | category | flops | bytes accessed | tf_op | source)
XLA Modules:
  0.0 157.1 jit_solution(13607510494827119697)
XLA Ops:
  7.2 0.0 copy-start
  7.2 0.0 copy-start.3
  7.2 0.0 copy-start.6
  7.2 0.0 all-gather.3.cloned.1.call-start
  7.2 0.8 fusion.10
  8.1 0.9 concatenate.3.in_ref
  9.0 0.2 shard_map.95
  9.2 8.8 %collective-permute-start = (bf16[112,128]{1,0:T(8,128)(2,1)S(1)}, bf16[112,128]{1,0:T(8,128)(2,1)S(1)}, u32[]{:S(2)}, u32[]{:S(2)}) collective-permute-start(bf16[112,128]{1,0:T(8,128)(2,1)S(1)} %get-tuple-element.15), channel_id=1, source_target_pairs={{0,4},{4,0},{1,5},{5,1},{2,6},{6,2},{3,7},{7,3},{8,12},{12,8},{9,1... | collective-permute-start | bytes 86024 | tf_op jit(solution)/shard_map/ppermute | solution.py:272
  18.0 0.8 collective-permute-done.other_ref
  18.8 0.1 shard_map.96
  18.9 13.8 %all_to_all.22 = bf16[8,2,112,128]{3,2,1,0:T(8,128)(2,1)S(1)} all-to-all(bf16[8,2,112,128]{3,2,1,0:T(8,128)(2,1)S(1)} %shard_map.96), channel_id=1, replica_groups={{0,8,16,24,32,40,48,56},{64,72,80,88,96,104,112,120},{128,136,144,152,1..., dimensions={0} | all-to-all | bytes 917504 | tf_op jit(solution)/shard_map/all_to_all | solution.py:284
  32.7 1.0 shard_map.97
  33.7 0.0 all-gather.3.cloned.1.call-update
  33.7 0.0 copy-done
  33.7 0.1 constant_dynamic-slice_fusion
  33.8 0.0 copy-start.4
  33.8 0.0 copy-start.5
  33.8 0.1 copy.51
  34.0 0.1 reshape.167
  34.1 0.0 copy-done.3
  34.1 0.1 reshape.168
  34.2 0.1 reshape.169
  34.4 0.0 copy-done.6
  34.4 0.9 copy.42
  35.3 12.3 %all-to-all-start.1 = ((bf16[128,2,320]{2,1,0:T(2,128)(2,1)}), bf16[128,2,320]{2,1,0:T(2,128)(2,1)S(1)}, u32[]{:S(2)}, u32[]{:S(2)}) async-start(bf16[128,2,320]{2,1,0:T(2,128)(2,1)} %copy.42), calls=%async_computation.1 | async-start | bytes 393216 | tf_op jit(solution)/shard_map/all_to_all | solution.py:300
  47.6 0.0 reduce-scatter.2.cloned.1.call-start
  47.7 13.9 %all-to-all-done.1 = bf16[128,2,320]{2,1,0:T(2,128)(2,1)S(1)} async-done(((bf16[128,2,320]{2,1,0:T(2,128)(2,1)}), bf16[128,2,320]{2,1,0:T(2,128)(2,1)S(1)}, u32[]{:S(2)}, u32[]{:S(2)}) %all-to-all-start.1) | async-done | bytes 163872 | tf_op jit(solution)/shard_map/all_to_all | solution.py:300
  61.6 0.2 copy.43
  61.8 0.2 copy.44
  62.0 0.9 gather_fusion
  62.8 12.4 %all-gather.own_ref = bf16[512,640]{1,0:T(8,128)(2,1)S(1)} all-gather(bf16[128,640]{1,0:T(8,128)(2,1)S(1)} %gather_fusion), channel_id=2, replica_groups=mesh['y'=8,'z'=8,'c'=2,'x'=4] {'x'}, dimensions={0}, use_global_device_ids=true | all-gather | bytes 819200 | tf_op jit(solution)/shard_map/all_gather | solution.py:302
  75.2 0.3 reduce-window.9
  75.5 0.1 slice.21
  75.6 4.8 %collective-permute-start.1 = (bf16[512,640]{1,0:T(8,128)(2,1)S(1)}, bf16[512,640]{1,0:T(8,128)(2,1)S(1)}, u32[]{:S(2)}, u32[]{:S(2)}) collective-permute-start(bf16[512,640]{1,0:T(8,128)(2,1)S(1)} %all-gather.own_ref), channel_id=1, source_target_pairs={{0,4},{4,0},{1,5},{5,1},{2,6},{6,2},{3,7},{7,3},{8,12},{12,8},{9,1... | collective-permute-start | bytes 1966088 | tf_op jit(solution)/shard_map/ppermute | solution.py:304
  80.4 0.1 slice_reduce_fusion
  80.6 0.1 fusion.8
  80.6 0.2 convert_reduce_fusion.1
  80.8 0.0 copy-done.5
  80.8 0.2 select_reduce_fusion.1
  81.0 0.4 convert_reduce_fusion
  81.4 1.0 fusion.7.signs_ref
  82.5 0.0 collective-permute-done.1.other_ref
  82.5 0.0 all-gather.3.cloned.1.call-done.w_any
  82.5 5.8 %shard_map.98 = (bf16[256,384]{1,0:T(8,128)(2,1)S(1)}, bf16[768,384]{1,0:T(8,128)(2,1)S(1)}) custom-call(s32[1]{0:T(128)} %bitcast.core_ref, bf16[512,640]{1,0:T(8,128)(2,1)S(1)} %all-gather.own_ref, bf16[512,640]{1,0:T(8,128)(2,1)S(1)} %collective-permute-done.1.other_ref, bf16[256,2304]{1,0:T(8,128)(2,1)S(1)} %fusion.7.signs_ref, ...), custom_call_target="tpu_custom_call" | custom-call | flops 2717908992 | bytes 8000000 | tf_op jit(solution)/shard_map/pallas_call | solution.py:324
  88.3 0.8 copy-done.1
  89.2 2.2 %collective-permute-start.3 = (bf16[256,384]{1,0:T(8,128)(2,1)S(1)}, bf16[256,384]{1,0:T(8,128)(2,1)S(1)}, u32[]{:S(2)}, u32[]{:S(2)}) collective-permute-start(bf16[256,384]{1,0:T(8,128)(2,1)S(1)} %get-tuple-element.21.here), channel_id=1, source_target_pairs={{0,8},{8,16},{16,24},{24,32},{32,40},{40,48},{48,56},{56,64},{64,7... | collective-permute-start | bytes 589832 | tf_op jit(solution)/shard_map/ppermute | solution.py:43
  91.4 1.3 collective-permute-start.4
  92.7 3.7 %collective-permute-start.2 = (bf16[128,384]{1,0:T(8,128)(2,1)S(1)}, bf16[128,384]{1,0:T(8,128)(2,1)S(1)}, u32[]{:S(2)}, u32[]{:S(2)}) collective-permute-start(bf16[128,384]{1,0:T(8,128)(2,1)S(1)} %get-tuple-element.31), channel_id=1, source_target_pairs={{0,16},{8,24},{16,32},{24,40},{32,48},{40,56},{48,64},{56,72},{64,... | collective-permute-start | bytes 294920 | tf_op jit(solution)/shard_map/ppermute | solution.py:43
  96.4 1.5 collective-permute-start.5
  97.9 0.1 copy.46.segq_ref
  98.1 0.2 collective-permute-done.2.far_before
  98.2 5.1 %collective-permute-done.5.far_after = bf16[128,384]{1,0:T(8,128)(2,1)S(1)} collective-permute-done((bf16[128,384]{1,0:T(8,128)(2,1)S(1)}, bf16[128,384]{1,0:T(8,128)(2,1)S(1)}, u32[]{:S(2)}, u32[]{:S(2)}) %collective-permute-start.5) | collective-permute-done | bytes 98336 | tf_op jit(solution)/shard_map/ppermute | solution.py:43
  103.4 0.0 collective-permute-done.3.before
  103.4 0.0 collective-permute-done.4.after
  103.4 1.1 copy-done.2
  104.5 6.8 %shard_map.99 = (f32[2304,128]{1,0:T(8,128)S(1)}, bf16[2304,128]{1,0:T(8,128)(2,1)S(1)}, f32[1,256]{1,0:T(1,128)S(1)}) custom-call(s32[1]{0:T(128)} %bitcast.core_ref, bf16[768,384]{1,0:T(8,128)(2,1)S(1)} %copy-done.2, bf16[128,384]{1,0:T(8,128)(2,1)S(1)} %collective-permute-done.2.far_before, bf16[256,384]{1,0:T(8,128)(2,1)S(1)} %collective-permute-done.3.before, ...), custom_call_target="tpu_custom_call" | custom-call | flops 2000000000 | bytes 5000000 | tf_op jit(solution)/shard_map/pallas_call | solution.py:343
  111.3 6.3 %collective-permute-start.6 = (bf16[2304,128]{1,0:T(8,128)(2,1)S(1)}, bf16[2304,128]{1,0:T(8,128)(2,1)S(1)}, u32[]{:S(2)}, u32[]{:S(2)}) collective-permute-start(bf16[2304,128]{1,0:T(8,128)(2,1)S(1)} %get-tuple-element.23), channel_id=1, source_target_pairs={{0,4},{4,0},{1,5},{5,1},{2,6},{6,2},{3,7},{7,3},{8,12},{12,8},{9,1... | collective-permute-start | bytes 1769480 | tf_op jit(solution)/shard_map/ppermute | solution.py:363
  117.6 1.6 %collective-permute-done.6 = bf16[2304,128]{1,0:T(8,128)(2,1)S(1)} collective-permute-done((bf16[2304,128]{1,0:T(8,128)(2,1)S(1)}, bf16[2304,128]{1,0:T(8,128)(2,1)S(1)}, u32[]{:S(2)}, u32[]{:S(2)}) %collective-permute-start.6) | collective-permute-done | bytes 589856 | tf_op jit(solution)/shard_map/ppermute | solution.py:363
  119.2 0.9 add_convert_fusion
  120.1 0.0 reduce-scatter.2.cloned.1.call-update
  120.1 12.4 %all_to_all.23 = f32[16,1,256]{2,1,0:T(1,128)S(1)} all-to-all(f32[16,1,256]{2,1,0:T(1,128)S(1)} %broadcast_in_dim.62), channel_id=1, replica_groups=mesh['y'=8,'z'=8,'c'=2,'x'=4] {'y','c'}, dimensions={0} | all-to-all | bytes 32768 | tf_op jit(solution)/shard_map/all_to_all | solution.py:37
  132.6 17.0 %all_to_all.24 = f32[32,1,256]{2,1,0:T(1,128)S(1)} all-to-all(f32[32,1,256]{2,1,0:T(1,128)S(1)} %broadcast_in_dim.63), channel_id=1, replica_groups=mesh['y'=8,'z'=8,'c'=2,'x'=4] {'z','x'}, dimensions={0} | all-to-all | bytes 65536 | tf_op jit(solution)/shard_map/all_to_all | solution.py:37
  149.7 0.1 reduce_sum.62
  149.7 0.6 broadcast_multiply_fusion
  (21 shorter events, 0.2 us)
Async XLA Ops:
  7.2 26.5 %copy-start = (bf16[128,2304]{1,0:T(8,128)(2,1)S(1)}, bf16[128,2304]{1,0:T(8,128)(2,1)}, u32[]{:S(2)}) copy-start(bf16[128,2304]{1,0:T(8,128)(2,1)} %param.8) | copy-start | bytes 1769476
  7.2 26.9 %copy-start.3 = (f32[2304]{0:T(1024)S(1)}, f32[2304]{0:T(1024)}, u32[]{:S(2)}) copy-start(f32[2304]{0:T(1024)} %param.12) | copy-start | bytes 27652
  7.2 27.2 %copy-start.6 = (s32[1,128]{1,0:T(1,128)S(1)}, s32[1,128]{1,0:T(1,128)}, u32[]{:S(2)}) copy-start(s32[1,128]{1,0:T(1,128)} %param.9) | copy-start | bytes 1540
  7.2 75.3 %all-gather.3.cloned.1.call-start = ((), (), s32[]{:S(2)}) async-start(), calls=%async_computation.5 | async-start | bytes 3981312 | tf_op jit(solution)/shard_map/all_gather | solution.py:294
  9.2 9.6 %collective-permute-start = (bf16[112,128]{1,0:T(8,128)(2,1)S(1)}, bf16[112,128]{1,0:T(8,128)(2,1)S(1)}, u32[]{:S(2)}, u32[]{:S(2)}) collective-permute-start(bf16[112,128]{1,0:T(8,128)(2,1)S(1)} %get-tuple-element.15), channel_id=1, source_target_pairs={{0,4},{4,0},{1,5},{5,1},{2,6},{6,2},{3,7},{7,3},{8,12},{12,8},{9,1... | collective-permute-start | bytes 86024 | tf_op jit(solution)/shard_map/ppermute | solution.py:272
  33.8 41.4 %copy-start.4 = (s32[256]{0:T(256)S(1)}, s32[256]{0:T(256)}, u32[]{:S(2)}) copy-start(s32[256]{0:T(256)} %param.10) | copy-start | bytes 3076
  33.8 47.0 %copy-start.5 = (s32[256]{0:T(256)S(1)}, s32[256]{0:T(256)}, u32[]{:S(2)}) copy-start(s32[256]{0:T(256)} %param.11) | copy-start | bytes 3076
  35.3 26.3 %all-to-all-start.1 = ((bf16[128,2,320]{2,1,0:T(2,128)(2,1)}), bf16[128,2,320]{2,1,0:T(2,128)(2,1)S(1)}, u32[]{:S(2)}, u32[]{:S(2)}) async-start(bf16[128,2,320]{2,1,0:T(2,128)(2,1)} %copy.42), calls=%async_computation.1 | async-start | bytes 393216 | tf_op jit(solution)/shard_map/all_to_all | solution.py:300
  47.6 102.7 %reduce-scatter.2.cloned.1.call-start = ((), (), s32[]{:S(2)}) async-start(), calls=%async_computation.6 | async-start | bytes 737280 | tf_op jit(solution)/shard_map/reduce_scatter | solution.py:365
  75.6 6.8 %collective-permute-start.1 = (bf16[512,640]{1,0:T(8,128)(2,1)S(1)}, bf16[512,640]{1,0:T(8,128)(2,1)S(1)}, u32[]{:S(2)}, u32[]{:S(2)}) collective-permute-start(bf16[512,640]{1,0:T(8,128)(2,1)S(1)} %all-gather.own_ref), channel_id=1, source_target_pairs={{0,4},{4,0},{1,5},{5,1},{2,6},{6,2},{3,7},{7,3},{8,12},{12,8},{9,1... | collective-permute-start | bytes 1966088 | tf_op jit(solution)/shard_map/ppermute | solution.py:304
  88.3 0.8 copy-start.1
  89.2 14.2 %collective-permute-start.3 = (bf16[256,384]{1,0:T(8,128)(2,1)S(1)}, bf16[256,384]{1,0:T(8,128)(2,1)S(1)}, u32[]{:S(2)}, u32[]{:S(2)}) collective-permute-start(bf16[256,384]{1,0:T(8,128)(2,1)S(1)} %get-tuple-element.21.here), channel_id=1, source_target_pairs={{0,8},{8,16},{16,24},{24,32},{32,40},{40,48},{48,56},{56,64},{64,7... | collective-permute-start | bytes 589832 | tf_op jit(solution)/shard_map/ppermute | solution.py:43
  91.4 12.0 %collective-permute-start.4 = (bf16[256,384]{1,0:T(8,128)(2,1)S(1)}, bf16[256,384]{1,0:T(8,128)(2,1)S(1)}, u32[]{:S(2)}, u32[]{:S(2)}) collective-permute-start(bf16[256,384]{1,0:T(8,128)(2,1)S(1)} %get-tuple-element.21.here), channel_id=1, source_target_pairs={{8,0},{16,8},{24,16},{32,24},{40,32},{48,40},{56,48},{64,56},{72,6... | collective-permute-start | bytes 589832 | tf_op jit(solution)/shard_map/ppermute | solution.py:43
  92.7 5.5 %collective-permute-start.2 = (bf16[128,384]{1,0:T(8,128)(2,1)S(1)}, bf16[128,384]{1,0:T(8,128)(2,1)S(1)}, u32[]{:S(2)}, u32[]{:S(2)}) collective-permute-start(bf16[128,384]{1,0:T(8,128)(2,1)S(1)} %get-tuple-element.31), channel_id=1, source_target_pairs={{0,16},{8,24},{16,32},{24,40},{32,48},{40,56},{48,64},{56,72},{64,... | collective-permute-start | bytes 294920 | tf_op jit(solution)/shard_map/ppermute | solution.py:43
  96.4 7.0 %collective-permute-start.5 = (bf16[128,384]{1,0:T(8,128)(2,1)S(1)}, bf16[128,384]{1,0:T(8,128)(2,1)S(1)}, u32[]{:S(2)}, u32[]{:S(2)}) collective-permute-start(bf16[128,384]{1,0:T(8,128)(2,1)S(1)} %get-tuple-element.30), channel_id=1, source_target_pairs={{16,0},{24,8},{32,16},{40,24},{48,32},{56,40},{64,48},{72,56},{80,... | collective-permute-start | bytes 294920 | tf_op jit(solution)/shard_map/ppermute | solution.py:43
  103.4 1.1 copy-start.2
  111.3 7.9 %collective-permute-start.6 = (bf16[2304,128]{1,0:T(8,128)(2,1)S(1)}, bf16[2304,128]{1,0:T(8,128)(2,1)S(1)}, u32[]{:S(2)}, u32[]{:S(2)}) collective-permute-start(bf16[2304,128]{1,0:T(8,128)(2,1)S(1)} %get-tuple-element.23), channel_id=1, source_target_pairs={{0,4},{4,0},{1,5},{5,1},{2,6},{6,2},{3,7},{7,3},{8,12},{12,8},{9,1... | collective-permute-start | bytes 1769480 | tf_op jit(solution)/shard_map/ppermute | solution.py:363
Sparse Core Ops, SparseCore 0:
  33.8 43.3 all-gather.2
  120.2 23.0 reduce-scatter.1

commit v5 on v4

--- a/solution.py
+++ b/solution.py
@@ -156,92 +156,89 @@
 
 
 def attend_kernel(
-    rows, side, core_ref, qu_ref, far_before, before, here, after, far_after, segq_ref, segk_ref, w_any,
-    mine_ref, theirs_ref, share_ref, window, o_ext, weight, flat, w_sem,
+    rows, side, theirs, core_ref, qu_ref, far, before, here, after, segq_ref, segk_ref, w_any,
+    out_ref, share_ref, window, o_ext, weight, flat, w_sem,
 ):
     block = 2 * rows
     reach = (2 * SPAN + 1) * rows
-    q_width = GROUP * HEAD_DIM
+    core = core_ref[0]
+    tile = 1 - core if theirs else core
     o_width = weight.shape[1]
     fetch = pltpu.make_async_copy(w_any.at[:, pl.ds(w_any.shape[1] - o_width, o_width)], weight, w_sem)
     fetch.start()
-    shift = o_width - q_width
-    window[0:rows] = far_before[...]
-    window[rows : rows + block] = before[...]
-    window[rows + block : rows + 2 * block] = here[...]
-    window[rows + 2 * block : rows + 3 * block] = after[...]
-    window[rows + 3 * block : 2 * rows + 3 * block] = far_after[...]
+
+    @pl.when(tile == 0)
+    def _():
+        window[0:rows] = far[...]
+        window[rows : rows + block] = before[...]
+        window[rows + block : rows + 2 * block] = here[...]
+        window[rows + 2 * block :] = after[...]
+
+    @pl.when(tile != 0)
+    def _():
+        window[0:block] = before[...]
+        window[block : 2 * block] = here[...]
+        window[2 * block : 3 * block] = after[...]
+        window[3 * block :] = far[...]
+
+    lo = pl.multiple_of(tile * rows, rows)
+    shift = o_width - GROUP * HEAD_DIM
     scale = 1.0 / HEAD_DIM**0.5
     to_exp2 = scale * 1.4426950408889634
-    o_ext[:, :shift] = jnp.zeros((block, shift), jnp.bfloat16)
-    images = share_ref.shape[1]
-    share = jnp.zeros((1, images), jnp.float32)
     both = 2 * HEAD_DIM
-    for tile in range(2):
-        lo = tile * rows
-        keys = window[lo : lo + reach, :both]
-        values = window[lo : lo + reach, both:]
-
-        def heads(first):
-            parts = [
-                qu_ref[first + lo : first + lo + rows, h * HEAD_DIM : (h + 1) * HEAD_DIM] for h in range(GROUP)
-            ]
-            return jnp.concatenate(parts, axis=0)
-
-        q, q_t = heads(0), heads(block)
-        segq = segq_ref[lo : lo + rows, :]
-        mask = jnp.concatenate([segq] * GROUP, axis=0) == segk_ref[:, lo : lo + reach]
-        s = lax.dot_general(q, keys[:, :HEAD_DIM], NT, preferred_element_type=jnp.float32)
-        s_t = lax.dot_general(
-            jnp.concatenate([q_t, q], axis=1), keys, NT, preferred_element_type=jnp.float32
-        )
-        s = jnp.where(mask, s, -1e30)
-        e = jnp.exp2((s - jnp.max(s, axis=1, keepdims=True)) * to_exp2)
-        inv = 1.0 / jnp.sum(e, axis=1, keepdims=True)
-        mean = jnp.sum(e * s_t, axis=1, keepdims=True) * inv
-        e_t = (e * ((s_t - mean) * scale)).astype(jnp.bfloat16)
-        e = e.astype(jnp.bfloat16)
-        made = jnp.dot(e, values, preferred_element_type=jnp.float32)
-        out = (made[:, :HEAD_DIM] * inv).astype(jnp.bfloat16)
-        out_t = jnp.dot(e_t, values[:, :HEAD_DIM], preferred_element_type=jnp.float32) + made[:, HEAD_DIM:]
-        out_t = (out_t * inv).astype(jnp.bfloat16).astype(jnp.float32)
-        terms = jnp.zeros((rows, 1), jnp.float32)
-        for head in range(GROUP):
-            a, b = shift + head * HEAD_DIM, shift + (head + 1) * HEAD_DIM
-            at = head * rows
-            u = qu_ref[2 * block + lo : 2 * block + lo + rows, a:b].astype(jnp.float32)
-            o_ext[lo : lo + rows, a:b] = out[at : at + rows]
-            terms += jnp.sum(out_t[at : at + rows] * u, axis=1, keepdims=True)
-        numbers = lax.broadcasted_iota(jnp.int32, (rows, images), 1)
-        share += jnp.sum(jnp.where(segq == numbers, terms, 0.0), axis=0, keepdims=True)
-    share_ref[...] = share
-    core = core_ref[0]
-    own = o_ext[pl.ds(pl.multiple_of(core * rows, rows), rows), :]
-    other = o_ext[pl.ds(pl.multiple_of((1 - core) * rows, rows), rows), :]
-    both = jnp.concatenate([other, own], axis=0)
+    keys = window[:, :both]
+    values = window[:, both:]
+
+    def heads(first):
+        held = qu_ref[pl.ds(first + lo, rows), :]
+        return jnp.concatenate([held[:, h * HEAD_DIM : (h + 1) * HEAD_DIM] for h in range(GROUP)], axis=0)
+
+    q, q_t = heads(0), heads(block)
+    segq = segq_ref[pl.ds(lo, rows), :]
+    mask = jnp.concatenate([segq] * GROUP, axis=0) == segk_ref[:, pl.ds(lo, reach)]
+    s = lax.dot_general(q, keys[:, :HEAD_DIM], NT, preferred_element_type=jnp.float32)
+    s_t = lax.dot_general(jnp.concatenate([q_t, q], axis=1), keys, NT, preferred_element_type=jnp.float32)
+    s = jnp.where(mask, s, -1e30)
+    e = jnp.exp2((s - jnp.max(s, axis=1, keepdims=True)) * to_exp2)
+    inv = 1.0 / jnp.sum(e, axis=1, keepdims=True)
+    mean = jnp.sum(e * s_t, axis=1, keepdims=True) * inv
+    e_t = (e * ((s_t - mean) * scale)).astype(jnp.bfloat16)
+    e = e.astype(jnp.bfloat16)
+    made = jnp.dot(e, values, preferred_element_type=jnp.float32)
+    out = (made[:, :HEAD_DIM] * inv).astype(jnp.bfloat16)
+    out_t = jnp.dot(e_t, values[:, :HEAD_DIM], preferred_element_type=jnp.float32) + made[:, HEAD_DIM:]
+    out_t = (out_t * inv).astype(jnp.bfloat16).astype(jnp.float32)
+    u = qu_ref[pl.ds(2 * block + lo, rows), :].astype(jnp.float32)
+    terms = jnp.zeros((rows, 1), jnp.float32)
+    o_ext[:, :shift] = jnp.zeros((rows, shift), jnp.bfloat16)
+    for head in range(GROUP):
+        a, b = shift + head * HEAD_DIM, shift + (head + 1) * HEAD_DIM
+        at = head * rows
+        o_ext[:, a:b] = out[at : at + rows]
+        terms += jnp.sum(out_t[at : at + rows] * u[:, a:b], axis=1, keepdims=True)
+    numbers = lax.broadcasted_iota(jnp.int32, (rows, share_ref.shape[1]), 1)
+    share_ref[...] = jnp.sum(jnp.where(segq == numbers, terms, 0.0), axis=0, keepdims=True)
     fetch.wait()
     width = weight.shape[0]
     step, unit = width // 4, width // side**2
     for part in range(4):
         a, b = part * step, (part + 1) * step
-        r = lax.dot_general(weight[a:b, :], both, NT, preferred_element_type=jnp.float32)
+        r = lax.dot_general(weight[a:b, :], o_ext[...], NT, preferred_element_type=jnp.float32)
 
         @pl.when(core == 0)
         def _(a=a, b=b, r=r):
-            theirs_ref[a:b, :] = r[:, :rows].astype(jnp.bfloat16)
-            mine_ref[a:b, :] = r[:, rows:]
+            out_ref[a:b, :] = r.astype(out_ref.dtype)
 
         @pl.when(core != 0)
         def _(a=a, r=r):
             for i in range(step // unit):
                 z, y = divmod(a // unit + i, side)
                 to = (y * side + z) * unit
-                flat[to : to + unit, :] = r[i * unit : (i + 1) * unit, :rows]
-                mine_ref[to : to + unit, :] = r[i * unit : (i + 1) * unit, rows:]
+                flat[to : to + unit, :] = r[i * unit : (i + 1) * unit, :]
 
     @pl.when(core != 0)
     def _():
-        theirs_ref[...] = flat[...].astype(jnp.bfloat16)
+        out_ref[...] = flat[...].astype(out_ref.dtype)
 
 
 def body(owned_rows, arrival, image_lengths, probe_seeds, in_gain, w_q, w_kv, w_out):
@@ -338,34 +335,45 @@
         compiler_params=params(50),
         cost_estimate=pl.CostEstimate(flops=6 * block * width * columns, bytes_accessed=8_000_000, transcendentals=0),
     )(core_word, own, other, signs, gain[None, :], weights)
-    neighbours = (moved(kv[rows:], 2), moved(kv, 1), kv, moved(kv, -1), moved(kv[:rows], -2))
-
-    mine, theirs, share = pl.pallas_call(
-        functools.partial(attend_kernel, rows, n_z),
-        out_shape=(
-            jax.ShapeDtypeStruct((width, rows), f32),
-            jax.ShapeDtypeStruct((width, rows), bf16),
-            jax.ShapeDtypeStruct((1, images), f32),
-        ),
-        in_specs=[SMEM] + [VMEM] * 8 + [ANY],
-        out_specs=(VMEM, VMEM, VMEM),
-        scratch_shapes=[
-            pltpu.VMEM((8 * rows, 4 * HEAD_DIM), bf16),
-            pltpu.VMEM((block, 3 * LANES), bf16),
-            pltpu.VMEM((width, 3 * LANES), bf16),
-            pltpu.VMEM((width, rows), f32),
-            pltpu.SemaphoreType.DMA,
-        ],
-        compiler_params=params(50),
-        cost_estimate=pl.CostEstimate(flops=2_000_000_000, bytes_accessed=5_000_000, transcendentals=700_000),
-    )(core_word, qu, *neighbours, seg[:, None], segk[None, :], weights)
-
+    before, after = moved(kv, 1), moved(kv, -1)
+    ahead = [((b, 1), (b + 2, 1)) for b in range(n_block - 2)] + [((b + 2, 0), (b, 0)) for b in range(n_block - 2)]
+    behind = [((b + 2, 1), (b, 1)) for b in range(n_block - 2)] + [((b, 0), (b + 2, 0)) for b in range(n_block - 2)]
+    flat_pairs = lambda pairs: [(2 * b + c, 2 * to + d) for (b, c), (to, d) in pairs]
+    half = lambda which: lax.dynamic_slice_in_dim(kv, which * rows, rows, 0)
+    far_theirs = lax.ppermute(half(core), SEQ, flat_pairs(ahead))
+    far_mine = lax.ppermute(half(1 - core), SEQ, flat_pairs(behind))
+    segq, segk = seg[:, None], segk[None, :]
+
+    def attend(is_theirs, far):
+        return pl.pallas_call(
+            functools.partial(attend_kernel, rows, n_z, is_theirs),
+            out_shape=(
+                jax.ShapeDtypeStruct((width, rows), bf16 if is_theirs else f32),
+                jax.ShapeDtypeStruct((1, images), f32),
+            ),
+            in_specs=[SMEM] + [VMEM] * 7 + [ANY],
+            out_specs=(VMEM, VMEM),
+            scratch_shapes=[
+                pltpu.VMEM((7 * rows, 4 * HEAD_DIM), bf16),
+                pltpu.VMEM((rows, 3 * LANES), bf16),
+                pltpu.VMEM((width, 3 * LANES), bf16),
+                pltpu.VMEM((width, rows), f32),
+                pltpu.SemaphoreType.DMA,
+            ],
+            compiler_params=params(50),
+            cost_estimate=pl.CostEstimate(flops=1_000_000_000, bytes_accessed=4_000_000, transcendentals=350_000),
+        )(core_word, qu, far, before, kv, after, segq, segk, weights)
+
+    theirs, share_theirs = attend(True, far_theirs)
+    theirs, far_mine = lax.optimization_barrier((theirs, far_mine))
     theirs = lax.ppermute(theirs, "c", [(0, 1), (1, 0)])
+    mine, share = attend(False, far_mine)
+    share = share + share_theirs
     group = (mine + theirs.astype(f32)).astype(bf16)
     velocity = lax.psum_scatter(group, "x", scatter_dimension=0, tiled=True).T
     share, group = lax.optimization_barrier((share, group))
-    share = jnp.sum(spread(share[0], ("y", "c")), axis=0)
-    divergence = jnp.sum(spread(share, ("z", "x")), axis=0) / width
+    share = jnp.sum(spread(share[0], ("z", "c")), axis=0)
+    divergence = jnp.sum(spread(share, ("y", "x")), axis=0) / width
     return (velocity, divergence)
 
 

time: 158 us -> 151 us (0.956)
  waiting for transfers between devices: 21.7 us -> 16.9 us
  starting transfers between devices: 41 us -> 38.7 us
    ppermute x4 -> x2, starting transfers between devices: 8.73 us -> 3.72 us  [moved(): return lax.ppermute(array, COLUMN, pairs)]
    ppermute x0 -> x2, starting transfers between devices: none -> 5 us  [the longest x1 3.71 us: body(): far_theirs = lax.ppermute(half(core), SEQ, flat_pairs(ahead))]
    ppermute x4 -> x2, waiting for transfers between devices: 5.31 us -> 1.99 us  [moved(): return lax.ppermute(array, COLUMN, pairs)]
    ppermute x1, starting transfers between devices: 6.29 us -> 4.22 us  [body(): theirs = lax.ppermute(theirs, 'c', [(0, 1), (1, 0)])]
    ppermute x1, waiting for transfers between devices: 1.61 us -> 0.01 us  [body(): theirs = lax.ppermute(theirs, 'c', [(0, 1), (1, 0)])]
    pallas_call x1 -> x2, Pallas kernels: 6.78 us -> 6.73 us  [attend(): pl.pallas_call(functools.partial(attend_kernel, rows, n_z, is_theirs), ou...]
  transfers between devices with their start and end apart: 10 -> 10, of which waited for: 5 -> 4; matrix products, arithmetic and copies ran while one was open for 4% -> 4% of each run, Pallas kernels for 0% -> 4%
where the time goes in v5:
time: 151 us; the launch traced here: 150 us
  blocking collectives  56 us (37%)
  starting transfers between devices  38.7 us (26%)
  waiting for transfers between devices  16.9 us (11%)
  between operations  14.4 us (10%)
  Pallas kernels  13.7 us (9%)
  local copies, waits for them, and re-layouts  6.73 us (4%)
  other arithmetic  3.9 us (3%)
    all_to_all x2, blocking collectives, spread(): return lax.all_to_all(copies, axes, split_axis=0, concat_axis=0, tiled=True)  29.6 us
    all_to_all x1, waiting for transfers between devices, body(): arrived = lax.all_to_all(part, SEQ, split_axis=0, concat_axis=0, tiled=True)  13.9 us
    all_to_all x1, blocking collectives, body(): lax.all_to_all(pieces, SEQ, split_axis=0, concat_axis=0, tiled=True, axis...  13.8 us
    all_gather x1, blocking collectives, body(): own = lax.all_gather(arrived, 'x', axis=0, tiled=True)  12.5 us
    all_to_all x1, starting transfers between devices, body(): arrived = lax.all_to_all(part, SEQ, split_axis=0, concat_axis=0, tiled=True)  12.3 us
    ppermute x1, starting transfers between devices, body(): other_piece = lax.ppermute(other_piece, 'c', [(0, 1), (1, 0)])  8.78 us
    pallas_call x2, Pallas kernels, attend(): pl.pallas_call(functools.partial(attend_kernel, rows, n_z, is_theirs), ou...  6.73 us
    pallas_call x1, Pallas kernels, body(): pl.pallas_call(functools.partial(project_kernel, n_z, unit), out_shape=(j...  5.78 us
  transfers between devices with their start and end apart: 10, of which 4 were waited for; matrix products, arithmetic and copies ran while one was open for 4% of the time, Pallas kernels for 4%

profile of v5, /device:TPU:1, one launch (start us, length us, event | category | flops | bytes accessed | tf_op | source)
XLA Modules:
  0.0 150.4 jit_solution(8350820524338115259)
XLA Ops:
  7.2 0.0 copy-start
  7.2 0.0 copy-start.3
  7.2 0.0 copy-start.6
  7.2 0.0 all-gather.3.cloned.1.call-start
  7.2 0.8 fusion.9
  8.1 0.9 concatenate.3.in_ref
  9.0 0.2 shard_map.95
  9.2 8.8 %collective-permute-start = (bf16[112,128]{1,0:T(8,128)(2,1)S(1)}, bf16[112,128]{1,0:T(8,128)(2,1)S(1)}, u32[]{:S(2)}, u32[]{:S(2)}) collective-permute-start(bf16[112,128]{1,0:T(8,128)(2,1)S(1)} %get-tuple-element.18), channel_id=1, source_target_pairs={{0,4},{4,0},{1,5},{5,1},{2,6},{6,2},{3,7},{7,3},{8,12},{12,8},{9,1... | collective-permute-start | bytes 86024 | tf_op jit(solution)/shard_map/ppermute | solution.py:269
  18.0 0.8 collective-permute-done.other_ref
  18.8 0.1 shard_map.96
  18.9 13.8 %all_to_all.22 = bf16[8,2,112,128]{3,2,1,0:T(8,128)(2,1)S(1)} all-to-all(bf16[8,2,112,128]{3,2,1,0:T(8,128)(2,1)S(1)} %shard_map.96), channel_id=1, replica_groups={{0,8,16,24,32,40,48,56},{64,72,80,88,96,104,112,120},{128,136,144,152,1..., dimensions={0} | all-to-all | bytes 917504 | tf_op jit(solution)/shard_map/all_to_all | solution.py:281
  32.7 1.0 shard_map.97
  33.7 0.0 all-gather.3.cloned.1.call-update
  33.7 0.0 copy-done
  33.7 0.1 constant_dynamic-slice_fusion.2
  33.8 0.0 copy-start.4
  33.8 0.0 copy-start.5
  33.9 0.1 copy.56
  34.0 0.1 reshape.167
  34.1 0.0 copy-done.3
  34.1 0.1 reshape.168
  34.3 0.1 reshape.169
  34.4 0.0 copy-done.6
  34.4 0.8 copy.46
  35.3 12.3 %all-to-all-start.1 = ((bf16[128,2,320]{2,1,0:T(2,128)(2,1)}), bf16[128,2,320]{2,1,0:T(2,128)(2,1)S(1)}, u32[]{:S(2)}, u32[]{:S(2)}) async-start(bf16[128,2,320]{2,1,0:T(2,128)(2,1)} %copy.46), calls=%async_computation.1 | async-start | bytes 393216 | tf_op jit(solution)/shard_map/all_to_all | solution.py:297
  47.6 0.0 reduce-scatter.2.cloned.1.call-start
  47.7 13.9 %all-to-all-done.1 = bf16[128,2,320]{2,1,0:T(2,128)(2,1)S(1)} async-done(((bf16[128,2,320]{2,1,0:T(2,128)(2,1)}), bf16[128,2,320]{2,1,0:T(2,128)(2,1)S(1)}, u32[]{:S(2)}, u32[]{:S(2)}) %all-to-all-start.1) | async-done | bytes 163872 | tf_op jit(solution)/shard_map/all_to_all | solution.py:297
  61.6 0.2 copy.47
  61.8 0.2 copy.48
  62.0 0.9 gather_fusion
  62.8 12.5 %all-gather.own_ref = bf16[512,640]{1,0:T(8,128)(2,1)S(1)} all-gather(bf16[128,640]{1,0:T(8,128)(2,1)S(1)} %gather_fusion), channel_id=2, replica_groups=mesh['y'=8,'z'=8,'c'=2,'x'=4] {'x'}, dimensions={0}, use_global_device_ids=true | all-gather | bytes 819200 | tf_op jit(solution)/shard_map/all_gather | solution.py:299
  75.4 0.0 copy-done.4
  75.4 0.3 reduce-window.9
  75.7 0.1 slice.15
  75.8 4.6 %collective-permute-start.1 = (bf16[512,640]{1,0:T(8,128)(2,1)S(1)}, bf16[512,640]{1,0:T(8,128)(2,1)S(1)}, u32[]{:S(2)}, u32[]{:S(2)}) collective-permute-start(bf16[512,640]{1,0:T(8,128)(2,1)S(1)} %all-gather.own_ref), channel_id=1, source_target_pairs={{0,4},{4,0},{1,5},{5,1},{2,6},{6,2},{3,7},{7,3},{8,12},{12,8},{9,1... | collective-permute-start | bytes 1966088 | tf_op jit(solution)/shard_map/ppermute | solution.py:301
  80.4 0.1 slice_reduce_fusion
  80.5 0.1 fusion.8
  80.6 0.2 convert_reduce_fusion.1
  80.8 0.2 select_reduce_fusion.1
  81.0 0.4 convert_reduce_fusion
  81.4 1.0 fusion.7.signs_ref
  82.4 0.0 collective-permute-done.1.other_ref
  82.5 0.8 copy-done.1
  83.3 1.1 copy-done.2
  84.4 5.8 %shard_map.98 = (bf16[256,384]{1,0:T(8,128)(2,1)S(1)}, bf16[768,384]{1,0:T(8,128)(2,1)S(1)}) custom-call(s32[1]{0:T(128)} %bitcast.core_ref, bf16[512,640]{1,0:T(8,128)(2,1)S(1)} %all-gather.own_ref, bf16[512,640]{1,0:T(8,128)(2,1)S(1)} %copy-done.2, bf16[256,2304]{1,0:T(8,128)(2,1)S(1)} %fusion.7.signs_ref, f32[1,2304]{1,0:T(1,128)S(1)} %broadcast_in_dim.59.gain_ref, ...), custom_call_target="tpu_custom_call" | custom-call | flops 2717908992 | bytes 8000000 | tf_op jit(solution)/shard_map/pallas_call | solution.py:321
  90.2 2.4 %collective-permute-start.3 = (bf16[256,384]{1,0:T(8,128)(2,1)S(1)}, bf16[256,384]{1,0:T(8,128)(2,1)S(1)}, u32[]{:S(2)}, u32[]{:S(2)}) collective-permute-start(bf16[256,384]{1,0:T(8,128)(2,1)S(1)} %get-tuple-element.24.here), channel_id=1, source_target_pairs={{0,8},{8,16},{16,24},{24,32},{32,40},{40,48},{48,56},{56,64},{64,7... | collective-permute-start | bytes 589832 | tf_op jit(solution)/shard_map/ppermute | solution.py:43
  92.6 1.3 collective-permute-start.4
  93.9 3.7 %collective-permute-start.2 = (bf16[128,384]{1,0:T(8,128)(2,1)S(1)}, bf16[128,384]{1,0:T(8,128)(2,1)S(1)}, u32[]{:S(2)}, u32[]{:S(2)}) collective-permute-start(bf16[128,384]{1,0:T(8,128)(2,1)S(1)} %get-tuple-element.37), channel_id=1, source_target_pairs={{4,20},{12,28},{20,36},{28,44},{36,52},{44,60},{52,68},{60,76},{68... | collective-permute-start | bytes 294920 | tf_op jit(solution)/shard_map/ppermute | solution.py:343
  97.7 1.3 collective-permute-start.5
  99.0 0.1 copy.50.segq_ref
  99.1 0.2 collective-permute-done.2.far
  99.3 0.0 collective-permute-done.3.before
  99.3 2.0 %collective-permute-done.4.after = bf16[256,384]{1,0:T(8,128)(2,1)S(1)} collective-permute-done((bf16[256,384]{1,0:T(8,128)(2,1)S(1)}, bf16[256,384]{1,0:T(8,128)(2,1)S(1)}, u32[]{:S(2)}, u32[]{:S(2)}) %collective-permute-start.4) | collective-permute-done | bytes 196640 | tf_op jit(solution)/shard_map/ppermute | solution.py:43
  101.3 3.5 %shard_map.99 = (bf16[2304,128]{1,0:T(8,128)(2,1)S(1)}, f32[1,256]{1,0:T(1,128)S(1)}) custom-call(s32[1]{0:T(128)} %bitcast.core_ref, bf16[768,384]{1,0:T(8,128)(2,1)S(1)} %get-tuple-element.23.qu_ref, bf16[128,384]{1,0:T(8,128)(2,1)S(1)} %collective-permute-done.2.far, bf16[256,384]{1,0:T(8,128)(2,1)S(1)} %collective-permute-done.3.before, ...), custom_call_target="tpu_custom_call" | custom-call | flops 1000000000 | bytes 4000000 | tf_op jit(solution)/shard_map/pallas_call | solution.py:348
  104.7 0.0 collective-permute-done.5.far
  104.7 4.2 %collective-permute-start.6 = (bf16[2304,128]{1,0:T(8,128)(2,1)S(1)}, bf16[2304,128]{1,0:T(8,128)(2,1)S(1)}, u32[]{:S(2)}, u32[]{:S(2)}) collective-permute-start(bf16[2304,128]{1,0:T(8,128)(2,1)S(1)} %get-tuple-element.28), channel_id=1, source_target_pairs={{0,4},{4,0},{1,5},{5,1},{2,6},{6,2},{3,7},{7,3},{8,12},{12,8},{9,1... | collective-permute-start | bytes 1769480 | tf_op jit(solution)/shard_map/ppermute | solution.py:369
  109.0 3.3 %shard_map.100 = (f32[2304,128]{1,0:T(8,128)S(1)}, f32[1,256]{1,0:T(1,128)S(1)}) custom-call(s32[1]{0:T(128)} %bitcast.core_ref, bf16[768,384]{1,0:T(8,128)(2,1)S(1)} %get-tuple-element.23.qu_ref, bf16[128,384]{1,0:T(8,128)(2,1)S(1)} %collective-permute-done.5.far, bf16[256,384]{1,0:T(8,128)(2,1)S(1)} %collective-permute-done.3.before, ...), custom_call_target="tpu_custom_call" | custom-call | flops 1000000000 | bytes 4000000 | tf_op jit(solution)/shard_map/pallas_call | solution.py:348
  112.3 0.0 collective-permute-done.6
  112.3 1.0 add_convert_fusion
  113.2 0.0 reduce-scatter.2.cloned.1.call-update
  113.3 13.8 %all_to_all.23 = f32[16,1,256]{2,1,0:T(1,128)S(1)} all-to-all(f32[16,1,256]{2,1,0:T(1,128)S(1)} %broadcast_in_dim.62), channel_id=1, replica_groups=mesh['y'=8,'z'=8,'c'=2,'x'=4] {'z','c'}, dimensions={0} | all-to-all | bytes 32768 | tf_op jit(solution)/shard_map/all_to_all | solution.py:37
  127.1 15.9 %all_to_all.24 = f32[32,1,256]{2,1,0:T(1,128)S(1)} all-to-all(f32[32,1,256]{2,1,0:T(1,128)S(1)} %broadcast_in_dim.63), channel_id=1, replica_groups=mesh['y'=8,'z'=8,'c'=2,'x'=4] {'y','x'}, dimensions={0} | all-to-all | bytes 65536 | tf_op jit(solution)/shard_map/all_to_all | solution.py:37
  143.0 0.1 reduce_sum.62
  143.0 0.6 broadcast_multiply_fusion
  (23 shorter events, 0.2 us)
Async XLA Ops:
  7.2 26.5 %copy-start = (bf16[128,2304]{1,0:T(8,128)(2,1)S(1)}, bf16[128,2304]{1,0:T(8,128)(2,1)}, u32[]{:S(2)}) copy-start(bf16[128,2304]{1,0:T(8,128)(2,1)} %param.8) | copy-start | bytes 1769476
  7.2 26.9 %copy-start.3 = (f32[2304]{0:T(1024)S(1)}, f32[2304]{0:T(1024)}, u32[]{:S(2)}) copy-start(f32[2304]{0:T(1024)} %param.12) | copy-start | bytes 27652
  7.2 27.2 %copy-start.6 = (s32[1,128]{1,0:T(1,128)S(1)}, s32[1,128]{1,0:T(1,128)}, u32[]{:S(2)}) copy-start(s32[1,128]{1,0:T(1,128)} %param.9) | copy-start | bytes 1540
  7.2 76.1 %all-gather.3.cloned.1.call-start = ((), (), s32[]{:S(2)}) async-start(), calls=%async_computation.5 | async-start | bytes 3981312 | tf_op jit(solution)/shard_map/all_gather | solution.py:291
  9.2 9.6 %collective-permute-start = (bf16[112,128]{1,0:T(8,128)(2,1)S(1)}, bf16[112,128]{1,0:T(8,128)(2,1)S(1)}, u32[]{:S(2)}, u32[]{:S(2)}) collective-permute-start(bf16[112,128]{1,0:T(8,128)(2,1)S(1)} %get-tuple-element.18), channel_id=1, source_target_pairs={{0,4},{4,0},{1,5},{5,1},{2,6},{6,2},{3,7},{7,3},{8,12},{12,8},{9,1... | collective-permute-start | bytes 86024 | tf_op jit(solution)/shard_map/ppermute | solution.py:269
  33.8 41.6 %copy-start.4 = (s32[256]{0:T(256)S(1)}, s32[256]{0:T(256)}, u32[]{:S(2)}) copy-start(s32[256]{0:T(256)} %param.10) | copy-start | bytes 3076
  33.8 47.0 %copy-start.5 = (s32[256]{0:T(256)S(1)}, s32[256]{0:T(256)}, u32[]{:S(2)}) copy-start(s32[256]{0:T(256)} %param.11) | copy-start | bytes 3076
  35.3 26.3 %all-to-all-start.1 = ((bf16[128,2,320]{2,1,0:T(2,128)(2,1)}), bf16[128,2,320]{2,1,0:T(2,128)(2,1)S(1)}, u32[]{:S(2)}, u32[]{:S(2)}) async-start(bf16[128,2,320]{2,1,0:T(2,128)(2,1)} %copy.46), calls=%async_computation.1 | async-start | bytes 393216 | tf_op jit(solution)/shard_map/all_to_all | solution.py:297
  47.6 96.0 %reduce-scatter.2.cloned.1.call-start = ((), (), s32[]{:S(2)}) async-start(), calls=%async_computation.6 | async-start | bytes 737280 | tf_op jit(solution)/shard_map/reduce_scatter | solution.py:373
  75.8 6.6 %collective-permute-start.1 = (bf16[512,640]{1,0:T(8,128)(2,1)S(1)}, bf16[512,640]{1,0:T(8,128)(2,1)S(1)}, u32[]{:S(2)}, u32[]{:S(2)}) collective-permute-start(bf16[512,640]{1,0:T(8,128)(2,1)S(1)} %all-gather.own_ref), channel_id=1, source_target_pairs={{0,4},{4,0},{1,5},{5,1},{2,6},{6,2},{3,7},{7,3},{8,12},{12,8},{9,1... | collective-permute-start | bytes 1966088 | tf_op jit(solution)/shard_map/ppermute | solution.py:301
  82.5 0.8 copy-start.1
  83.3 1.1 copy-start.2
  90.2 9.1 %collective-permute-start.3 = (bf16[256,384]{1,0:T(8,128)(2,1)S(1)}, bf16[256,384]{1,0:T(8,128)(2,1)S(1)}, u32[]{:S(2)}, u32[]{:S(2)}) collective-permute-start(bf16[256,384]{1,0:T(8,128)(2,1)S(1)} %get-tuple-element.24.here), channel_id=1, source_target_pairs={{0,8},{8,16},{16,24},{24,32},{32,40},{40,48},{48,56},{56,64},{64,7... | collective-permute-start | bytes 589832 | tf_op jit(solution)/shard_map/ppermute | solution.py:43
  92.6 8.7 %collective-permute-start.4 = (bf16[256,384]{1,0:T(8,128)(2,1)S(1)}, bf16[256,384]{1,0:T(8,128)(2,1)S(1)}, u32[]{:S(2)}, u32[]{:S(2)}) collective-permute-start(bf16[256,384]{1,0:T(8,128)(2,1)S(1)} %get-tuple-element.24.here), channel_id=1, source_target_pairs={{8,0},{16,8},{24,16},{32,24},{40,32},{48,40},{56,48},{64,56},{72,6... | collective-permute-start | bytes 589832 | tf_op jit(solution)/shard_map/ppermute | solution.py:43
  93.9 5.3 %collective-permute-start.2 = (bf16[128,384]{1,0:T(8,128)(2,1)S(1)}, bf16[128,384]{1,0:T(8,128)(2,1)S(1)}, u32[]{:S(2)}, u32[]{:S(2)}) collective-permute-start(bf16[128,384]{1,0:T(8,128)(2,1)S(1)} %get-tuple-element.37), channel_id=1, source_target_pairs={{4,20},{12,28},{20,36},{28,44},{36,52},{44,60},{52,68},{60,76},{68... | collective-permute-start | bytes 294920 | tf_op jit(solution)/shard_map/ppermute | solution.py:343
  97.7 7.1 %collective-permute-start.5 = (bf16[128,384]{1,0:T(8,128)(2,1)S(1)}, bf16[128,384]{1,0:T(8,128)(2,1)S(1)}, u32[]{:S(2)}, u32[]{:S(2)}) collective-permute-start(bf16[128,384]{1,0:T(8,128)(2,1)S(1)} %get-tuple-element.36), channel_id=1, source_target_pairs={{20,4},{28,12},{36,20},{44,28},{52,36},{60,44},{68,52},{76,60},{84... | collective-permute-start | bytes 294920 | tf_op jit(solution)/shard_map/ppermute | solution.py:344
  104.7 7.5 %collective-permute-start.6 = (bf16[2304,128]{1,0:T(8,128)(2,1)S(1)}, bf16[2304,128]{1,0:T(8,128)(2,1)S(1)}, u32[]{:S(2)}, u32[]{:S(2)}) collective-permute-start(bf16[2304,128]{1,0:T(8,128)(2,1)S(1)} %get-tuple-element.28), channel_id=1, source_target_pairs={{0,4},{4,0},{1,5},{5,1},{2,6},{6,2},{3,7},{7,3},{8,12},{12,8},{9,1... | collective-permute-start | bytes 1769480 | tf_op jit(solution)/shard_map/ppermute | solution.py:369
Sparse Core Ops, SparseCore 0:
  33.8 43.3 all-gather.2
  113.4 23.1 reduce-scatter.1

commit v6 on v5

--- a/solution.py
+++ b/solution.py
@@ -274,6 +274,10 @@
         out_specs=VMEM,
         compiler_params=params(50),
     )(core_word, own_piece, other_piece)
+    part = lax.dynamic_slice_in_dim(owned_rows, member * quarter, quarter, 1)
+    padded = -(-quarter // LANES) * LANES
+    part = jnp.pad(part, ((0, 0), (0, padded - quarter))).reshape(rows, 2, padded // 2)
+    part, pieces = lax.optimization_barrier((part, pieces))
     side = range(n_z)
     place = lambda y, z, c: (y * n_z + z) * 2 + c
     by_z = [[place(y, z, 0) for z in side] for y in side] + [[place(y, z, 1) for y in side] for z in side]
@@ -290,14 +294,12 @@
     )(strip)
     weights = lax.all_gather(strip, SEQ, axis=0, tiled=True, axis_index_groups=by_y)
 
-    part = lax.dynamic_slice_in_dim(owned_rows, member * quarter, quarter, 1)
-    padded = -(-quarter // LANES) * LANES
-    part = jnp.pad(part, ((0, 0), (0, padded - quarter))).reshape(rows, 2, padded // 2)
-    part, strip = lax.optimization_barrier((part, strip))
     arrived = lax.all_to_all(part, SEQ, split_axis=0, concat_axis=0, tiled=True)
     arrived = jnp.take(arrived.reshape(rows, padded), arrival[0], axis=0, mode="clip")
     own = lax.all_gather(arrived, "x", axis=0, tiled=True)
-    own, image_lengths, probe_seeds = lax.optimization_barrier((own, image_lengths, probe_seeds))
+    own, image_lengths, probe_seeds, in_gain = lax.optimization_barrier(
+        (own, image_lengths, probe_seeds, in_gain)
+    )
     other = lax.ppermute(own, "c", [(0, 1), (1, 0)])
 
     ends = jnp.cumsum(image_lengths, dtype=jnp.int32)
@@ -348,7 +350,7 @@
         return pl.pallas_call(
             functools.partial(attend_kernel, rows, n_z, is_theirs),
             out_shape=(
-                jax.ShapeDtypeStruct((width, rows), bf16 if is_theirs else f32),
+                jax.ShapeDtypeStruct((width, rows), bf16),
                 jax.ShapeDtypeStruct((1, images), f32),
             ),
             in_specs=[SMEM] + [VMEM] * 7 + [ANY],
@@ -369,7 +371,7 @@
     theirs = lax.ppermute(theirs, "c", [(0, 1), (1, 0)])
     mine, share = attend(False, far_mine)
     share = share + share_theirs
-    group = (mine + theirs.astype(f32)).astype(bf16)
+    group = (mine.astype(f32) + theirs.astype(f32)).astype(bf16)
     velocity = lax.psum_scatter(group, "x", scatter_dimension=0, tiled=True).T
     share, group = lax.optimization_barrier((share, group))
     share = jnp.sum(spread(share[0], ("z", "c")), axis=0)

time: 151 us -> 151 us (level)
  transfers between devices with their start and end apart: 10 -> 10, of which waited for: 4 -> 5; matrix products, arithmetic and copies ran while one was open for 4% -> 4% of each run, Pallas kernels for 4% -> 4%
where the time goes in v6:
time: 151 us; the launch traced here: 150 us
  blocking collectives  55.5 us (37%)
  starting transfers between devices  38.8 us (26%)
  waiting for transfers between devices  16.9 us (11%)
  between operations  14.4 us (10%)
  Pallas kernels  13.7 us (9%)
  local copies, waits for them, and re-layouts  6.73 us (4%)
  other arithmetic  3.9 us (3%)
    all_to_all x2, blocking collectives, spread(): return lax.all_to_all(copies, axes, split_axis=0, concat_axis=0, tiled=True)  29.2 us
    all_to_all x1, blocking collectives, body(): lax.all_to_all(pieces, SEQ, split_axis=0, concat_axis=0, tiled=True, axis...  13.8 us
    all_to_all x1, waiting for transfers between devices, body(): arrived = lax.all_to_all(part, SEQ, split_axis=0, concat_axis=0, tiled=True)  13.8 us
    all_gather x1, blocking collectives, body(): own = lax.all_gather(arrived, 'x', axis=0, tiled=True)  12.5 us
    all_to_all x1, starting transfers between devices, body(): arrived = lax.all_to_all(part, SEQ, split_axis=0, concat_axis=0, tiled=True)  12.3 us
    ppermute x1, starting transfers between devices, body(): other_piece = lax.ppermute(other_piece, 'c', [(0, 1), (1, 0)])  8.78 us
    pallas_call x2, Pallas kernels, attend(): pl.pallas_call(functools.partial(attend_kernel, rows, n_z, is_theirs), ou...  6.7 us
    pallas_call x1, Pallas kernels, body(): pl.pallas_call(functools.partial(project_kernel, n_z, unit), out_shape=(j...  5.78 us
  transfers between devices with their start and end apart: 10, of which 5 were waited for; matrix products, arithmetic and copies ran while one was open for 4% of the time, Pallas kernels for 4%

profile of v6, /device:TPU:1, one launch (start us, length us, event | category | flops | bytes accessed | tf_op | source)
XLA Modules:
  0.0 150.0 jit_solution(7008969479650852247)
XLA Ops:
  7.2 0.0 copy-start
  7.2 0.0 copy-start.6
  7.2 0.0 all-gather.3.cloned.1.call-start
  7.2 0.8 fusion.9
  8.1 0.9 concatenate.3.in_ref
  9.0 0.2 shard_map.95
  9.2 8.8 %collective-permute-start = (bf16[112,128]{1,0:T(8,128)(2,1)S(1)}, bf16[112,128]{1,0:T(8,128)(2,1)S(1)}, u32[]{:S(2)}, u32[]{:S(2)}) collective-permute-start(bf16[112,128]{1,0:T(8,128)(2,1)S(1)} %get-tuple-element.20), channel_id=1, source_target_pairs={{0,4},{4,0},{1,5},{5,1},{2,6},{6,2},{3,7},{7,3},{8,12},{12,8},{9,1... | collective-permute-start | bytes 86024 | tf_op jit(solution)/shard_map/ppermute | solution.py:269
  18.0 0.0 copy-done
  18.0 0.1 constant_dynamic-slice_fusion.2
  18.1 0.1 copy.56
  18.3 0.5 collective-permute-done.other_ref
  18.8 0.1 shard_map.96
  18.9 13.8 %all_to_all.22 = bf16[8,2,112,128]{3,2,1,0:T(8,128)(2,1)S(1)} all-to-all(bf16[8,2,112,128]{3,2,1,0:T(8,128)(2,1)S(1)} %shard_map.96), channel_id=1, replica_groups={{0,8,16,24,32,40,48,56},{64,72,80,88,96,104,112,120},{128,136,144,152,1..., dimensions={0} | all-to-all | bytes 917504 | tf_op jit(solution)/shard_map/all_to_all | solution.py:285
  32.7 1.0 shard_map.97
  33.6 0.0 copy-start.4
  33.7 0.0 all-gather.3.cloned.1.call-update
  33.7 0.1 reshape.166
  33.8 0.0 copy-done.6
  33.8 0.8 copy.46
  34.7 12.3 %all-to-all-start = ((bf16[128,2,320]{2,1,0:T(2,128)(2,1)}), bf16[128,2,320]{2,1,0:T(2,128)(2,1)S(1)}, u32[]{:S(2)}, u32[]{:S(2)}) async-start(bf16[128,2,320]{2,1,0:T(2,128)(2,1)} %copy.46), calls=%async_computation | async-start | bytes 393216 | tf_op jit(solution)/shard_map/all_to_all | solution.py:297
  47.0 0.0 reduce-scatter.2.cloned.1.call-start
  47.1 13.8 %all-to-all-done = bf16[128,2,320]{2,1,0:T(2,128)(2,1)S(1)} async-done(((bf16[128,2,320]{2,1,0:T(2,128)(2,1)}), bf16[128,2,320]{2,1,0:T(2,128)(2,1)S(1)}, u32[]{:S(2)}, u32[]{:S(2)}) %all-to-all-start) | async-done | bytes 163872 | tf_op jit(solution)/shard_map/all_to_all | solution.py:297
  60.9 0.2 copy.47
  61.1 0.2 copy.48
  61.3 0.9 gather_fusion
  62.2 12.5 %all-gather.own_ref = bf16[512,640]{1,0:T(8,128)(2,1)S(1)} all-gather(bf16[128,640]{1,0:T(8,128)(2,1)S(1)} %gather_fusion), channel_id=2, replica_groups=mesh['y'=8,'z'=8,'c'=2,'x'=4] {'x'}, dimensions={0}, use_global_device_ids=true | all-gather | bytes 819200 | tf_op jit(solution)/shard_map/all_gather | solution.py:299
  74.7 0.0 copy-done.4
  74.7 0.3 reduce-window.9
  75.0 0.1 slice.15
  75.1 0.0 copy-done.3
  75.1 0.1 reshape.167
  75.2 0.1 reshape.168
  75.3 4.4 %collective-permute-start.1 = (bf16[512,640]{1,0:T(8,128)(2,1)S(1)}, bf16[512,640]{1,0:T(8,128)(2,1)S(1)}, u32[]{:S(2)}, u32[]{:S(2)}) collective-permute-start(bf16[512,640]{1,0:T(8,128)(2,1)S(1)} %all-gather.own_ref), channel_id=1, source_target_pairs={{0,4},{4,0},{1,5},{5,1},{2,6},{6,2},{3,7},{7,3},{8,12},{12,8},{9,1... | collective-permute-start | bytes 1966088 | tf_op jit(solution)/shard_map/ppermute | solution.py:303
  79.7 0.1 slice_reduce_fusion
  79.8 0.1 fusion.8
  79.9 0.2 convert_reduce_fusion.1
  80.1 0.0 copy-done.5
  80.1 0.2 select_reduce_fusion.1
  80.3 0.4 convert_reduce_fusion
  80.7 1.0 fusion.7.signs_ref
  81.7 0.0 collective-permute-done.1.other_ref
  81.7 0.0 copy-start.1
  81.7 0.8 copy-done.1
  82.6 1.1 copy-done.2
  83.7 5.8 %shard_map.98 = (bf16[256,384]{1,0:T(8,128)(2,1)S(1)}, bf16[768,384]{1,0:T(8,128)(2,1)S(1)}) custom-call(s32[1]{0:T(128)} %bitcast.core_ref, bf16[512,640]{1,0:T(8,128)(2,1)S(1)} %all-gather.own_ref, bf16[512,640]{1,0:T(8,128)(2,1)S(1)} %copy-done.2, bf16[256,2304]{1,0:T(8,128)(2,1)S(1)} %fusion.7.signs_ref, f32[1,2304]{1,0:T(1,128)S(1)} %broadcast_in_dim.59.gain_ref, ...), custom_call_target="tpu_custom_call" | custom-call | flops 2717908992 | bytes 8000000 | tf_op jit(solution)/shard_map/pallas_call | solution.py:323
  89.5 2.2 %collective-permute-start.3 = (bf16[256,384]{1,0:T(8,128)(2,1)S(1)}, bf16[256,384]{1,0:T(8,128)(2,1)S(1)}, u32[]{:S(2)}, u32[]{:S(2)}) collective-permute-start(bf16[256,384]{1,0:T(8,128)(2,1)S(1)} %get-tuple-element.28.here), channel_id=1, source_target_pairs={{0,8},{8,16},{16,24},{24,32},{32,40},{40,48},{48,56},{56,64},{64,7... | collective-permute-start | bytes 589832 | tf_op jit(solution)/shard_map/ppermute | solution.py:43
  91.7 1.3 collective-permute-start.4
  93.0 3.8 %collective-permute-start.2 = (bf16[128,384]{1,0:T(8,128)(2,1)S(1)}, bf16[128,384]{1,0:T(8,128)(2,1)S(1)}, u32[]{:S(2)}, u32[]{:S(2)}) collective-permute-start(bf16[128,384]{1,0:T(8,128)(2,1)S(1)} %get-tuple-element.41), channel_id=1, source_target_pairs={{4,20},{12,28},{20,36},{28,44},{36,52},{44,60},{52,68},{60,76},{68... | collective-permute-start | bytes 294920 | tf_op jit(solution)/shard_map/ppermute | solution.py:345
  96.8 1.3 collective-permute-start.5
  98.2 0.1 copy.50.segq_ref
  98.3 0.2 collective-permute-done.2.far
  98.5 0.0 collective-permute-done.3.before
  98.5 1.2 collective-permute-done.4.after
  99.7 3.5 %shard_map.99 = (bf16[2304,128]{1,0:T(8,128)(2,1)S(1)}, f32[1,256]{1,0:T(1,128)S(1)}) custom-call(s32[1]{0:T(128)} %bitcast.core_ref, bf16[768,384]{1,0:T(8,128)(2,1)S(1)} %get-tuple-element.27.qu_ref, bf16[128,384]{1,0:T(8,128)(2,1)S(1)} %collective-permute-done.2.far, bf16[256,384]{1,0:T(8,128)(2,1)S(1)} %collective-permute-done.3.before, ...), custom_call_target="tpu_custom_call" | custom-call | flops 1000000000 | bytes 4000000 | tf_op jit(solution)/shard_map/pallas_call | solution.py:350
  103.1 1.1 collective-permute-done.5.far
  104.2 4.7 %collective-permute-start.6 = (bf16[2304,128]{1,0:T(8,128)(2,1)S(1)}, bf16[2304,128]{1,0:T(8,128)(2,1)S(1)}, u32[]{:S(2)}, u32[]{:S(2)}) collective-permute-start(bf16[2304,128]{1,0:T(8,128)(2,1)S(1)} %get-tuple-element.32), channel_id=1, source_target_pairs={{0,4},{4,0},{1,5},{5,1},{2,6},{6,2},{3,7},{7,3},{8,12},{12,8},{9,1... | collective-permute-start | bytes 1769480 | tf_op jit(solution)/shard_map/ppermute | solution.py:371
  109.0 3.2 %shard_map.100 = (bf16[2304,128]{1,0:T(8,128)(2,1)S(1)}, f32[1,256]{1,0:T(1,128)S(1)}) custom-call(s32[1]{0:T(128)} %bitcast.core_ref, bf16[768,384]{1,0:T(8,128)(2,1)S(1)} %get-tuple-element.27.qu_ref, bf16[128,384]{1,0:T(8,128)(2,1)S(1)} %collective-permute-done.5.far, bf16[256,384]{1,0:T(8,128)(2,1)S(1)} %collective-permute-done.3.before, ...), custom_call_target="tpu_custom_call" | custom-call | flops 1000000000 | bytes 4000000 | tf_op jit(solution)/shard_map/pallas_call | solution.py:350
  112.2 0.0 collective-permute-done.6
  112.2 1.0 add_convert_fusion
  113.2 0.0 reduce-scatter.2.cloned.1.call-update
  113.3 13.2 %all_to_all.23 = f32[16,1,256]{2,1,0:T(1,128)S(1)} all-to-all(f32[16,1,256]{2,1,0:T(1,128)S(1)} %broadcast_in_dim.62), channel_id=1, replica_groups=mesh['y'=8,'z'=8,'c'=2,'x'=4] {'z','c'}, dimensions={0} | all-to-all | bytes 32768 | tf_op jit(solution)/shard_map/all_to_all | solution.py:37
  126.6 15.9 %all_to_all.24 = f32[32,1,256]{2,1,0:T(1,128)S(1)} all-to-all(f32[32,1,256]{2,1,0:T(1,128)S(1)} %broadcast_in_dim.63), channel_id=1, replica_groups=mesh['y'=8,'z'=8,'c'=2,'x'=4] {'y','x'}, dimensions={0} | all-to-all | bytes 65536 | tf_op jit(solution)/shard_map/all_to_all | solution.py:37
  142.5 0.1 reduce_sum.62
  142.6 0.6 broadcast_multiply_fusion
  (23 shorter events, 0.2 us)
Async XLA Ops:
  7.2 10.8 %copy-start = (bf16[128,2304]{1,0:T(8,128)(2,1)S(1)}, bf16[128,2304]{1,0:T(8,128)(2,1)}, u32[]{:S(2)}) copy-start(bf16[128,2304]{1,0:T(8,128)(2,1)} %param.8) | copy-start | bytes 1769476
  7.2 26.6 %copy-start.6 = (s32[1,128]{1,0:T(1,128)S(1)}, s32[1,128]{1,0:T(1,128)}, u32[]{:S(2)}) copy-start(s32[1,128]{1,0:T(1,128)} %param.9) | copy-start | bytes 1540
  7.2 75.4 %all-gather.3.cloned.1.call-start = ((), (), s32[]{:S(2)}) async-start(), calls=%async_computation.5 | async-start | bytes 3981312 | tf_op jit(solution)/shard_map/all_gather | solution.py:295
  9.2 9.6 %collective-permute-start = (bf16[112,128]{1,0:T(8,128)(2,1)S(1)}, bf16[112,128]{1,0:T(8,128)(2,1)S(1)}, u32[]{:S(2)}, u32[]{:S(2)}) collective-permute-start(bf16[112,128]{1,0:T(8,128)(2,1)S(1)} %get-tuple-element.20), channel_id=1, source_target_pairs={{0,4},{4,0},{1,5},{5,1},{2,6},{6,2},{3,7},{7,3},{8,12},{12,8},{9,1... | collective-permute-start | bytes 86024 | tf_op jit(solution)/shard_map/ppermute | solution.py:269
  33.6 41.0 %copy-start.4 = (s32[256]{0:T(256)S(1)}, s32[256]{0:T(256)}, u32[]{:S(2)}) copy-start(s32[256]{0:T(256)} %param.10) | copy-start | bytes 3076
  33.6 41.4 %copy-start.3 = (f32[2304]{0:T(1024)S(1)}, f32[2304]{0:T(1024)}, u32[]{:S(2)}) copy-start(f32[2304]{0:T(1024)} %param.12) | copy-start | bytes 27652
  33.7 46.4 %copy-start.5 = (s32[256]{0:T(256)S(1)}, s32[256]{0:T(256)}, u32[]{:S(2)}) copy-start(s32[256]{0:T(256)} %param.11) | copy-start | bytes 3076
  34.7 26.2 %all-to-all-start = ((bf16[128,2,320]{2,1,0:T(2,128)(2,1)}), bf16[128,2,320]{2,1,0:T(2,128)(2,1)S(1)}, u32[]{:S(2)}, u32[]{:S(2)}) async-start(bf16[128,2,320]{2,1,0:T(2,128)(2,1)} %copy.46), calls=%async_computation | async-start | bytes 393216 | tf_op jit(solution)/shard_map/all_to_all | solution.py:297
  47.0 96.1 %reduce-scatter.2.cloned.1.call-start = ((), (), s32[]{:S(2)}) async-start(), calls=%async_computation.6 | async-start | bytes 737280 | tf_op jit(solution)/shard_map/reduce_scatter | solution.py:375
  75.3 6.4 %collective-permute-start.1 = (bf16[512,640]{1,0:T(8,128)(2,1)S(1)}, bf16[512,640]{1,0:T(8,128)(2,1)S(1)}, u32[]{:S(2)}, u32[]{:S(2)}) collective-permute-start(bf16[512,640]{1,0:T(8,128)(2,1)S(1)} %all-gather.own_ref), channel_id=1, source_target_pairs={{0,4},{4,0},{1,5},{5,1},{2,6},{6,2},{3,7},{7,3},{8,12},{12,8},{9,1... | collective-permute-start | bytes 1966088 | tf_op jit(solution)/shard_map/ppermute | solution.py:303
  81.7 0.8 copy-start.1
  82.6 1.1 copy-start.2
  89.5 9.0 %collective-permute-start.3 = (bf16[256,384]{1,0:T(8,128)(2,1)S(1)}, bf16[256,384]{1,0:T(8,128)(2,1)S(1)}, u32[]{:S(2)}, u32[]{:S(2)}) collective-permute-start(bf16[256,384]{1,0:T(8,128)(2,1)S(1)} %get-tuple-element.28.here), channel_id=1, source_target_pairs={{0,8},{8,16},{16,24},{24,32},{32,40},{40,48},{48,56},{56,64},{64,7... | collective-permute-start | bytes 589832 | tf_op jit(solution)/shard_map/ppermute | solution.py:43
  91.7 8.0 %collective-permute-start.4 = (bf16[256,384]{1,0:T(8,128)(2,1)S(1)}, bf16[256,384]{1,0:T(8,128)(2,1)S(1)}, u32[]{:S(2)}, u32[]{:S(2)}) collective-permute-start(bf16[256,384]{1,0:T(8,128)(2,1)S(1)} %get-tuple-element.28.here), channel_id=1, source_target_pairs={{8,0},{16,8},{24,16},{32,24},{40,32},{48,40},{56,48},{64,56},{72,6... | collective-permute-start | bytes 589832 | tf_op jit(solution)/shard_map/ppermute | solution.py:43
  93.0 5.5 %collective-permute-start.2 = (bf16[128,384]{1,0:T(8,128)(2,1)S(1)}, bf16[128,384]{1,0:T(8,128)(2,1)S(1)}, u32[]{:S(2)}, u32[]{:S(2)}) collective-permute-start(bf16[128,384]{1,0:T(8,128)(2,1)S(1)} %get-tuple-element.41), channel_id=1, source_target_pairs={{4,20},{12,28},{20,36},{28,44},{36,52},{44,60},{52,68},{60,76},{68... | collective-permute-start | bytes 294920 | tf_op jit(solution)/shard_map/ppermute | solution.py:345
  96.8 7.4 %collective-permute-start.5 = (bf16[128,384]{1,0:T(8,128)(2,1)S(1)}, bf16[128,384]{1,0:T(8,128)(2,1)S(1)}, u32[]{:S(2)}, u32[]{:S(2)}) collective-permute-start(bf16[128,384]{1,0:T(8,128)(2,1)S(1)} %get-tuple-element.40), channel_id=1, source_target_pairs={{20,4},{28,12},{36,20},{44,28},{52,36},{60,44},{68,52},{76,60},{84... | collective-permute-start | bytes 294920 | tf_op jit(solution)/shard_map/ppermute | solution.py:346
  104.2 8.0 %collective-permute-start.6 = (bf16[2304,128]{1,0:T(8,128)(2,1)S(1)}, bf16[2304,128]{1,0:T(8,128)(2,1)S(1)}, u32[]{:S(2)}, u32[]{:S(2)}) collective-permute-start(bf16[2304,128]{1,0:T(8,128)(2,1)S(1)} %get-tuple-element.32), channel_id=1, source_target_pairs={{0,4},{4,0},{1,5},{5,1},{2,6},{6,2},{3,7},{7,3},{8,12},{12,8},{9,1... | collective-permute-start | bytes 1769480 | tf_op jit(solution)/shard_map/ppermute | solution.py:371
Sparse Core Ops, SparseCore 0:
  33.8 43.1 all-gather.2
  113.3 22.3 reduce-scatter.1
